TPU v7x, 32 devices: a whole 2x2x4 slice. The times are simulated.
32 devices in a mesh: seq: 4 (over y, x), row: 2 (over core), col: 4 (over z).
Axes of the slice: x: 2, y: 2, z: 4, core: 2. Of those that a mesh axis runs over, the one named last changes fastest.
Arguments:
- activations: bfloat16 [2048, 16384], P('seq', ('row', 'col')), may hold values from -1500 to 1500
- norm_gain: float32 [16384], P(('row', 'col')), may hold values from 0.1 to 1.9
- query_weight: bfloat16 [16384, 8192], P('row', 'col'), may hold values from -0.046875 to 0.046875
- kv_weight: bfloat16 [16384, 2, 512], P('row'), may hold values from -0.046875 to 0.046875
- out_weight: bfloat16 [8192, 16384], P('col', 'row'), may hold values from -0.5 to 0.5
- block_ids: int32 [2048], replicated, may hold values from 0 to 255, never falling along the last dimension, each value on 1 to 16 neighbouring positions
- clean_mask: int32 [2048], replicated, may hold values 0 or 1
Outputs:
- layer_out: bfloat16 [2048, 16384], P('seq', ('row', 'col'))
Inputs may be any that keep to these rules, and one draw needn't show every extreme that they name: `block_ids`: block numbers never fall along the sequence; every block holds 1 to 16 tokens and one holds exactly 16.
All inputs are finite; a program needn't handle non-finite values.
Results may differ from a plain program's by a relative error of at most 0.009.
Values may be sent and summed in bfloat16 or wider, within the bound.
No kernel may reach another device: no remote copies, remote signals or barrier semaphores. Data moves between devices by JAX's collectives and lax.ppermute only.
A program may use at most 192 MiB of HBM per device.

v0:
```python
import math

import jax
import jax.numpy as jnp
from jax import lax
from jax.sharding import PartitionSpec as P

D = 16384
HD = 128
QH = 64
KVH = 4


rope_base = 500000.0
norm_eps = 1e-05


def rotate(values, positions):
    half_dim = values.shape[-1] // 2
    inverse = jnp.exp(
        jnp.arange(half_dim, dtype=jnp.float32) * (-2.0 * math.log(rope_base) / values.shape[-1])
    )
    angles = positions.astype(jnp.float32)[:, None] * inverse[None, :]
    cosine = jnp.cos(angles)
    sine_part = jnp.sin(angles)
    first_half = values[..., :half_dim]
    second_half = values[..., half_dim:]
    return jnp.concatenate(
        [
            first_half * cosine - second_half * sine_part,
            second_half * cosine + first_half * sine_part,
        ],
        axis=-1,
    )


def shards(activations, norm_gain, query_weight, kv_weight, out_weight, block_ids, clean_mask):
    row_count = lax.axis_size("row")
    col_index = lax.axis_index("col")
    seq_index = lax.axis_index("seq")
    slab_len = activations.shape[0]
    col_heads = query_weight.shape[1] // HD
    dev_heads = col_heads // row_count
    group_size = QH // KVH
    wide_input = activations.astype(jnp.float32)
    squares = lax.psum(jnp.sum(wide_input * wide_input, axis=1), ("row", "col"))
    scaling = lax.rsqrt(squares / D + norm_eps)
    normed = (wide_input * scaling[:, None] * norm_gain[None, :]).astype(jnp.bfloat16)
    panel_rows = lax.all_gather(normed, "col", axis=1, tiled=True)
    kv_count = max(col_heads // group_size, 1)
    kv_first = col_index * col_heads // group_size
    kv_tiles = lax.dynamic_slice_in_dim(kv_weight, kv_first * HD, kv_count * HD, 2)
    kv_term = jnp.einsum("td,dke->kte", panel_rows, kv_tiles, preferred_element_type=jnp.float32)
    columns = query_weight
    columns = columns.reshape(columns.shape[0], dev_heads * lax.axis_size("row"), HD)
    query_sum = lax.psum_scatter(
        jnp.einsum("td,dhe->hte", panel_rows, columns, preferred_element_type=jnp.float32),
        "row",
        scatter_dimension=0,
        tiled=True,
    )
    kv_sum = lax.psum(kv_term, "row")
    key_raw = kv_sum[0]
    value_rows = kv_sum[1].astype(jnp.bfloat16)
    positions = seq_index * slab_len + jnp.arange(slab_len, dtype=jnp.int32)
    key_rows = rotate(key_raw, positions).astype(jnp.bfloat16)
    queries = rotate(query_sum, positions).astype(jnp.bfloat16)
    my_blocks = lax.dynamic_slice_in_dim(block_ids, seq_index * slab_len, slab_len, 0)
    score_scale = 1.0 / math.sqrt(HD)
    key_piece = lax.all_gather(key_rows, "seq", axis=0, tiled=True)
    value_piece = lax.all_gather(value_rows, "seq", axis=0, tiled=True)
    visible = (block_ids[None, :] == my_blocks[:, None]) | (
        block_ids[None, :] < my_blocks[:, None]
    ) & (clean_mask[None, :] == 1)
    scores = (
        jnp.einsum("hte,ne->htn", queries, key_piece, preferred_element_type=jnp.float32)
        * score_scale
    )
    weights = jnp.where(visible[None, :, :], jnp.exp(scores), jnp.zeros_like(scores))
    numerator = jnp.einsum(
        "htn,ne->hte", weights.astype(jnp.bfloat16), value_piece, preferred_element_type=jnp.float32
    )
    denominator = jnp.sum(weights, axis=2)
    numerator, denominator = (numerator, denominator)
    attended = (numerator / denominator[:, :, None]).astype(jnp.bfloat16)
    out_cols = out_weight.shape[1]
    portion = lax.all_gather(attended, "row", axis=0, tiled=True)
    heads_here = portion.shape[0]
    out_rows = out_weight
    out_rows = out_rows.reshape(heads_here, HD, out_cols)
    partial_out = jnp.einsum("hte,hed->td", portion, out_rows, preferred_element_type=jnp.float32)
    projected = lax.psum_scatter(partial_out, "col", scatter_dimension=1, tiled=True)
    return projected.astype(jnp.bfloat16)


def solution(mesh):
    placed = (
        P("seq", ("row", "col")),
        P(("row", "col")),
        P("row", "col"),
        P("row", None, None),
        P("col", "row"),
        P(),
        P(),
    )
    return jax.shard_map(
        shards, mesh=mesh, in_specs=placed, out_specs=P("seq", ("row", "col")), check_vma=False
    )
```

profile of v0, /device:TPU:8, one launch (start us, length us, event | category | flops | bytes accessed | tf_op | source)
XLA Modules:
  0.0 589.3 jit_solution(5961618433832999371)
XLA Ops:
  6.5 0.0 all-gather.4.cloned.1.call-start
  6.5 2.1 fusion.11
  8.6 14.6 %psum.14 = f32[512]{0:T(512)S(1)} all-reduce(f32[512]{0:T(512)S(1)} %fusion.11), channel_id=1, replica_groups=mesh['seq'=4,'row'=2,'col'=4] {'row','col'}, use_global_device_ids=true, to_apply=%region_1.0 | all-reduce | flops 512 | bytes 4096 | tf_op jit(solution)/shard_map/psum | solution.py:46
  23.3 3.5 fusion.13
  26.7 0.0 all-gather.4.cloned.1.call-update
  26.7 0.0 all-reduce.2.cloned.1.call-start
  26.8 7.8 %constant_dynamic-slice_fusion = bf16[8192,2,128]{2,1,0:T(2,128)(2,1)} fusion(bf16[8192,2,512]{2,1,0:T(2,128)(2,1)} %param.10, s32[]{:T(128)S(6)} %select_n.17), kind=kLoop, calls=%fused_computation.41 | loop fusion | bytes 8388612 | tf_op jit(solution)/shard_map/dynamic_slice | solution.py:52
  34.6 139.6 %all-gather.4.cloned.1.call-done = bf16[512,8192]{1,0:T(8,128)(2,1)} async-done(((bf16[512,2048]{1,0:T(8,128)(2,1)}), bf16[512,8192]{1,0:T(8,128)(2,1)}) %all-gather.4.cloned.1.call-update) | async-done | bytes 8388624 | tf_op jit(solution)/shard_map/all_gather | solution.py:49
  174.1 7.8 %fusion.20 = f32[2,512,128]{1,2,0:T(8,128)} fusion(bf16[512,8192]{1,0:T(8,128)(2,1)} %all-gather.4.cloned.1.call-done, bf16[8192,2,128]{2,1,0:T(2,128)(2,1)} %constant_dynamic-slice_fusion), kind=kOutput, calls=%fused_computation.23 | convolution fusion | flops 2147483648 | bytes 13107200 | tf_op jit(solution)/shard_map/td,dke->kte/dot_general | solution.py:53
  182.0 0.0 all-reduce.2.cloned.1.call-update
  182.0 0.0 reduce-scatter.3.cloned.1.call-start
  182.0 24.8 %fusion.15 = f32[16,512,128]{2,1,0:T(8,128)} fusion(bf16[512,8192]{1,0:T(8,128)(2,1)} %all-gather.4.cloned.1.call-done, bf16[8192,2048]{1,0:T(8,128)(2,1)} %param.9), kind=kOutput, calls=%fused_computation.19 | convolution fusion | flops 17179869184 | bytes 46137344 | tf_op jit(solution)/shard_map/td,dhe->hte/dot_general | solution.py:57
  206.8 0.0 copy-start
  206.8 0.0 copy-start.1
  206.8 0.0 reduce-scatter.3.cloned.1.call-update
  206.8 0.0 all-gather.6.cloned.1.call-start
  206.9 0.6 copy-done
  207.5 0.1 dynamic_slice.6
  207.6 0.0 copy-done.1
  207.6 1.2 and_or_fusion
  208.8 0.0 all-reduce.2.cloned.1.call-done
  208.8 1.0 slice_bitcast_fusion
  209.8 0.6 subtract_convert_fusion.1
  210.4 0.1 copy.15
  210.5 0.1 copy.14
  210.6 1.0 slice.41
  211.6 10.2 %all_gather.13 = bf16[2048,128]{0,1:T(8,128)(2,1)S(1)} all-gather(bf16[512,128]{0,1:T(8,128)(2,1)S(1)} %pad_maximum_fusion), channel_id=1, replica_groups=mesh['seq'=4,'row'=2,'col'=4] {'seq'}, dimensions={0}, use_global_device_ids=true | all-gather | bytes 655360 | tf_op jit(solution)/shard_map/all_gather | solution.py:70
  221.9 10.4 %all-gather = bf16[1,2048,128]{1,2,0:T(8,128)(2,1)S(1)} all-gather(bf16[1,512,128]{1,2,0:T(8,128)(2,1)S(1)} %slice.41), channel_id=2, replica_groups=mesh['seq'=4,'row'=2,'col'=4] {'seq'}, dimensions={1}, use_global_device_ids=true | all-gather | bytes 655360 | tf_op jit(solution)/shard_map/all_gather | solution.py:71
  232.2 0.0 reduce-scatter.3.cloned.1.call-done
  232.2 3.0 subtract_convert_fusion
  235.2 15.2 %fusion.3 = (f32[8,512]{1,0:T(8,128)S(1)}, f32[8,512,2048]{2,1,0:T(8,128)}) fusion(pred[512,2048]{1,0:T(8,128)(4,1)S(1)} %and_or_fusion, bf16[2048,128]{0,1:T(8,128)(2,1)S(1)} %all_gather.13, bf16[8,512,64]{2,1,0:T(8,128)(2,1)S(1)} %get-tuple-element.6, bf16[8,512,64]{2,1,0:T(8,128)(2,1)S(1)} %get-tuple-element.5), kind=kOutput, calls=%fused_computation.4 | convolution fusion | flops 2174742528 | bytes 36192256 | tf_op jit(solution)/shard_map/hte,ne->htn/dot_general | solution.py:76
  250.4 14.4 %divide_convert_fusion = bf16[8,512,128]{2,1,0:T(8,128)(2,1)} fusion(f32[8,512]{1,0:T(8,128)S(1)} %get-tuple-element.11, f32[8,512,2048]{2,1,0:T(8,128)} %get-tuple-element.12, pred[512,2048]{1,0:T(8,128)(4,1)S(1)} %and_or_fusion, bf16[1,2048,128]{1,2,0:T(8,128)(2,1)S(1)} %all-gather), kind=kOutput, calls=%fused_computation.20 | convolution fusion | flops 2173698048 | bytes 36192256 | tf_op jit(solution)/shard_map/htn,ne->hte/dot_general | solution.py:80
  264.8 0.0 all-gather.6.cloned.1.call-update
  264.8 0.0 reduce-scatter.5.cloned.1.call-start
  264.9 11.3 %all-gather.6.cloned.1.call-done = bf16[16,512,128]{2,1,0:T(8,128)(2,1)} async-done(((bf16[8,512,128]{2,1,0:T(8,128)(2,1)}), bf16[16,512,128]{2,1,0:T(8,128)(2,1)}) %all-gather.6.cloned.1.call-update) | async-done | bytes 2097168 | tf_op jit(solution)/shard_map/all_gather | solution.py:87
  276.2 24.5 %convolution_bitcast_fusion = f32[512,8192]{1,0:T(8,128)} fusion(bf16[16,512,128]{2,1,0:T(8,128)(2,1)} %all-gather.6.cloned.1.call-done, bf16[16,128,8192]{2,1,0:T(8,128)(2,1)} %bitcast.38), kind=kOutput, calls=%fused_computation.8 | convolution fusion | flops 17179869184 | bytes 52428800 | tf_op jit(solution)/shard_map/hte,hed->td/dot_general | solution.py:91
  300.7 0.0 reduce-scatter.5.cloned.1.call-update
  300.7 278.2 %reduce-scatter.5.cloned.1.call-done = f32[512,2048]{1,0:T(8,128)} async-done(((f32[512,8192]{1,0:T(8,128)}), f32[512,2048]{1,0:T(8,128)}) %reduce-scatter.5.cloned.1.call-update) | async-done | bytes 4194320 | tf_op jit(solution)/shard_map/reduce_scatter | solution.py:92
  578.9 3.8 convert_element_type.35
  (5 shorter events, 0.0 us)
Async XLA Ops:
  6.5 167.6 %all-gather.4.cloned.1.call-start = ((), (), s32[]{:S(2)}) async-start(), calls=%async_computation.2 | async-start | bytes 10485760 | tf_op jit(solution)/shard_map/all_gather | solution.py:49
  26.7 182.1 %all-reduce.2.cloned.1.call-start = ((), (), s32[]{:S(2)}) async-start(), calls=%async_computation.4 | async-start | bytes 1048576 | tf_op jit(solution)/shard_map/psum | solution.py:62
  182.0 50.2 %reduce-scatter.3.cloned.1.call-start = ((), (), s32[]{:S(2)}) async-start(), calls=%async_computation.3 | async-start | bytes 6291456 | tf_op jit(solution)/shard_map/reduce_scatter | solution.py:56
  206.8 0.7 copy-start
  206.8 0.8 copy-start.1
  206.8 69.3 %all-gather.6.cloned.1.call-start = ((), (), s32[]{:S(2)}) async-start(), calls=%async_computation.5 | async-start | bytes 3145728 | tf_op jit(solution)/shard_map/all_gather | solution.py:87
  264.8 314.1 %reduce-scatter.5.cloned.1.call-start = ((), (), s32[]{:S(2)}) async-start(), calls=%async_computation.6 | async-start | bytes 20971520 | tf_op jit(solution)/shard_map/reduce_scatter | solution.py:92
Sparse Core Ops, SparseCore 0:
  26.9 147.2 all-gather.3
  182.1 20.1 all-reduce.1
  207.0 13.7 reduce-scatter.2
  264.9 11.2 all-gather.5
  300.8 278.0 reduce-scatter.4
where the time goes:
time: 595 us; the launch traced here: 589 us
  waiting for transfers between devices  429 us (72%)
  matrix products  86.6 us (15%)
  blocking collectives  35.2 us (6%)
  other arithmetic  14.1 us (2%)
  between operations  13.2 us (2%)
  local copies, waits for them, and re-layouts  10.7 us (2%)
    reduce_scatter x1, waiting for transfers between devices, shards(): lax.psum_scatter(partial_out, 'col', scatter_dimension=1, tiled=True)  278 us
    all_gather x1, waiting for transfers between devices, shards(): panel_rows = lax.all_gather(normed, 'col', axis=1, tiled=True)  140 us
    dot_general x1, matrix products, shards(): jnp.einsum('td,dhe->hte', panel_rows, columns, preferred_element_type=jnp...  24.8 us
    dot_general x1, matrix products, shards(): jnp.einsum('hte,hed->td', portion, out_rows, preferred_element_type=jnp.f...  24.5 us
    dot_general x1, matrix products, shards(): jnp.einsum('hte,ne->htn', queries, key_piece, preferred_element_type=jnp....  15.2 us
    psum x1, blocking collectives, shards(): squares = lax.psum(jnp.sum(wide_input * wide_input, axis=1), ('row', 'col'))  14.6 us
    dot_general x1, matrix products, shards(): jnp.einsum('htn,ne->hte', weights.astype(jnp.bfloat16), value_piece, pref...  14.4 us
  transfers between devices with their start and end apart: 5, of which 3 were waited for; matrix products, arithmetic and copies ran while one was open for 6% of the time, Pallas kernels for 0%

commit v1 on v0

--- a/solution.py
+++ b/solution.py
@@ -1,8 +1,11 @@
+import functools
 import math
 
 import jax
 import jax.numpy as jnp
 from jax import lax
+from jax.experimental import pallas as pl
+from jax.experimental.pallas import tpu as pltpu
 from jax.sharding import PartitionSpec as P
 
 D = 16384
@@ -34,7 +37,7 @@
     )
 
 
-def shards(activations, norm_gain, query_weight, kv_weight, out_weight, block_ids, clean_mask):
+def gathered_shards(activations, norm_gain, query_weight, kv_weight, out_weight, block_ids, clean_mask):
     row_count = lax.axis_size("row")
     col_index = lax.axis_index("col")
     seq_index = lax.axis_index("seq")
@@ -93,6 +96,340 @@
     return projected.astype(jnp.bfloat16)
 
 
+LINE = 4
+OUTER_IN = ((0, 1), (3, 2))
+OUTER_OUT = ((2, 3), (1, 0))
+MIDDLE = ((1, 2), (2, 1))
+DEST_ORDER = ((3, 2, 1, 0), (0, 3, 2, 1), (3, 0, 1, 2), (0, 1, 2, 3))
+FEATURE_ORDER = ((0, 1, 2, 3), (1, 0, 2, 3), (2, 3, 1, 0), (3, 2, 1, 0))
+CHUNKS = 4
+DEPTH = 512
+
+
+def hop(values, pairs, axis="col"):
+    return lax.ppermute(values, axis, list(pairs))
+
+
+def params(mib=40):
+    return pltpu.CompilerParams(vmem_limit_bytes=mib << 20)
+
+
+def fetch_features(meta_ref, slots, features, held, arrived, start):
+    for place, choices in enumerate(slots):
+        def act(which):
+            copy = pltpu.make_async_copy(features[which], held.at[place], arrived.at[place])
+            copy.start() if start else copy.wait()
+
+        if len(choices) == 1:
+            act(choices[0])
+        else:
+            pl.when(meta_ref[4] == 0)(functools.partial(act, choices[0]))
+            pl.when(meta_ref[4] == 1)(functools.partial(act, choices[1]))
+
+
+def project_first_kernel(slots, meta_ref, *refs):
+    count = max(max(choices) for choices in slots) + 1
+    features, (weight_ref, total_ref, held, arrived) = refs[:count], refs[count:]
+    slot, step = pl.program_id(0), pl.program_id(1)
+
+    @pl.when((slot == 0) & (step == 0))
+    def _():
+        fetch_features(meta_ref, slots, features, held, arrived, True)
+
+    for place in range(len(slots)):
+        @pl.when((slot == place) & (step == 0))
+        def _():
+            pltpu.make_async_copy(features[0], held.at[place], arrived.at[place]).wait()
+
+    part = jnp.dot(
+        held[slot, :, pl.ds(pl.multiple_of(step * DEPTH, DEPTH), DEPTH)],
+        weight_ref[...],
+        preferred_element_type=jnp.float32,
+    )
+
+    @pl.when((slot == 0) & (step == 0))
+    def _():
+        total_ref[...] = part
+
+    @pl.when((slot > 0) | (step > 0))
+    def _():
+        total_ref[...] += part
+
+
+def project_first(meta, slots, features, weight):
+    rows, width = features[0].shape
+    steps = width // DEPTH
+    columns = weight.shape[1]
+    return pl.pallas_call(
+        functools.partial(project_first_kernel, slots),
+        grid_spec=pltpu.PrefetchScalarGridSpec(
+            num_scalar_prefetch=1,
+            grid=(len(slots), steps),
+            in_specs=[pl.BlockSpec(memory_space=pl.ANY)] * len(features)
+            + [pl.BlockSpec((DEPTH, columns), lambda i, j, m: (m[i] * steps + j, 0))],
+            out_specs=pl.BlockSpec((rows, columns), lambda i, j, m: (0, 0)),
+            scratch_shapes=[
+                pltpu.VMEM((len(slots), rows, width), jnp.bfloat16),
+                pltpu.SemaphoreType.DMA((len(slots),)),
+            ],
+        ),
+        out_shape=jax.ShapeDtypeStruct((rows, columns), jnp.float32),
+        compiler_params=params(),
+        cost_estimate=pl.CostEstimate(
+            flops=2 * rows * width * columns * len(slots),
+            bytes_accessed=2 * width * columns * len(slots),
+            transcendentals=0,
+        ),
+        name="project_first",
+    )(meta, *features, weight)
+
+
+def project_last_kernel(meta_ref, middle_ref, end_ref, weight_ref, so_far_ref, mine_ref, other_ref, held, total, arrived):
+    step = pl.program_id(0)
+    half = mine_ref.shape[1]
+
+    @pl.when(step == 0)
+    def _():
+        fetch_features(meta_ref, ((0, 1),), (middle_ref, end_ref), held, arrived, True)
+        total[...] = so_far_ref[...]
+        pltpu.make_async_copy(middle_ref, held.at[0], arrived.at[0]).wait()
+
+    total[...] += jnp.dot(
+        held[0, :, pl.ds(pl.multiple_of(step * DEPTH, DEPTH), DEPTH)],
+        weight_ref[...],
+        preferred_element_type=jnp.float32,
+    )
+
+    @pl.when(step == pl.num_programs(0) - 1)
+    def _():
+        mine = meta_ref[5]
+        mine_ref[...] = total[:, pl.ds(pl.multiple_of(mine * half, half), half)]
+        other_ref[...] = total[:, pl.ds(pl.multiple_of((1 - mine) * half, half), half)]
+
+
+def project_last(meta, middle, end, weight, so_far):
+    rows, width = middle.shape
+    steps = width // DEPTH
+    columns = weight.shape[1]
+    whole = lambda i, m: (0, 0)
+    return pl.pallas_call(
+        project_last_kernel,
+        grid_spec=pltpu.PrefetchScalarGridSpec(
+            num_scalar_prefetch=1,
+            grid=(steps,),
+            in_specs=[
+                pl.BlockSpec(memory_space=pl.ANY),
+                pl.BlockSpec(memory_space=pl.ANY),
+                pl.BlockSpec((DEPTH, columns), lambda i, m: (m[3] * steps + i, 0)),
+                pl.BlockSpec((rows, columns), whole),
+            ],
+            out_specs=[pl.BlockSpec((rows, columns // 2), whole)] * 2,
+            scratch_shapes=[
+                pltpu.VMEM((1, rows, width), jnp.bfloat16),
+                pltpu.VMEM((rows, columns), jnp.float32),
+                pltpu.SemaphoreType.DMA((1,)),
+            ],
+        ),
+        out_shape=[jax.ShapeDtypeStruct((rows, columns // 2), jnp.float32)] * 2,
+        compiler_params=params(),
+        cost_estimate=pl.CostEstimate(
+            flops=2 * rows * width * columns, bytes_accessed=2 * width * columns, transcendentals=0
+        ),
+        name="project_last",
+    )(meta, middle, end, weight, so_far)
+
+
+def attend_kernel(
+    mine_ref, arrived_ref, cosine_ref, sine_ref, key_ref, value_ref, own_ids_ref, ids_ref, cut_ref, out_ref, bias
+):
+    rows = mine_ref.shape[0]
+    keys = key_ref.shape[0]
+    tile = min(512, keys)
+    own = own_ids_ref[...]
+    for first in range(0, keys, tile):
+        spot = slice(first, first + tile)
+        seen = (ids_ref[:, spot] == own) | (cut_ref[:, spot] < own)
+        bias[:, spot] = jnp.where(seen, 0.0, -jnp.inf)
+    factor = math.log2(math.e) / math.sqrt(HD)
+
+    def one_head(head, carry):
+        place = pl.ds(pl.multiple_of(head * HD, HD), HD)
+        raw = mine_ref[:, place] + arrived_ref[:, place]
+        query = (raw * cosine_ref[...] + pltpu.roll(raw, HD // 2, 1) * sine_ref[...]).astype(jnp.bfloat16)
+        summed = jnp.zeros((rows, value_ref.shape[1]), jnp.float32)
+        for first in range(0, keys, tile):
+            spot = slice(first, first + tile)
+            scores = lax.dot_general(
+                query, key_ref[spot, :], (((1,), (1,)), ((), ())), preferred_element_type=jnp.float32
+            )
+            weights = jnp.exp2(scores * factor + bias[:, spot])
+            summed += jnp.dot(weights.astype(jnp.bfloat16), value_ref[spot, :], preferred_element_type=jnp.float32)
+        out_ref[:, place] = (summed[:, :HD] / summed[:, HD:]).astype(jnp.bfloat16)
+        return carry
+
+    lax.fori_loop(0, mine_ref.shape[1] // HD, one_head, 0)
+
+
+def attend(mine, arrived, cosine, sine, keys, values, own_ids, ids, cut):
+    rows, width = mine.shape
+    return pl.pallas_call(
+        attend_kernel,
+        out_shape=jax.ShapeDtypeStruct((rows, width), jnp.bfloat16),
+        in_specs=[pl.BlockSpec(memory_space=pltpu.VMEM)] * 9,
+        out_specs=pl.BlockSpec(memory_space=pltpu.VMEM),
+        scratch_shapes=[pltpu.VMEM((rows, keys.shape[0]), jnp.float32)],
+        compiler_params=params(),
+        cost_estimate=pl.CostEstimate(
+            flops=8 * rows * keys.shape[0] * width,
+            bytes_accessed=8 * rows * width + 6 * keys.shape[0] * HD,
+            transcendentals=rows * keys.shape[0] * width // HD,
+        ),
+        name="attend",
+    )(mine, arrived, cosine, sine, keys, values, own_ids, ids, cut)
+
+
+def output_kernel(meta_ref, mine_ref, other_ref, weight_ref, first_ref, second_ref, total):
+    slot, step = pl.program_id(0), pl.program_id(1)
+    steps = pl.num_programs(1)
+    near = steps // 2
+    place = pl.ds(pl.multiple_of(lax.rem(step, near) * DEPTH, DEPTH), DEPTH)
+
+    @pl.when(step < near)
+    def _():
+        part = jnp.dot(mine_ref[:, place], weight_ref[...], preferred_element_type=jnp.float32)
+
+        @pl.when(step == 0)
+        def _():
+            total[...] = part
+
+        @pl.when(step > 0)
+        def _():
+            total[...] += part
+
+    @pl.when(step >= near)
+    def _():
+        total[...] += jnp.dot(other_ref[:, place], weight_ref[...], preferred_element_type=jnp.float32)
+
+    @pl.when((step == steps - 1) & (slot == 0))
+    def _():
+        first_ref[...] = total[...].astype(first_ref.dtype)
+
+    @pl.when((step == steps - 1) & (slot == 1))
+    def _():
+        second_ref[...] = total[...].astype(second_ref.dtype)
+
+
+def output_parts(meta, first_slot, mine, other, weight, kinds):
+    rows, width = mine.shape
+    steps = weight.shape[0] // DEPTH
+    near = steps // 2
+    columns = weight.shape[1] // LINE
+    whole = lambda i, j, m: (0, 0)
+
+    def weight_block(i, j, m):
+        return (lax.rem(j + m[5] * near, steps), m[6 + first_slot + i])
+
+    return pl.pallas_call(
+        output_kernel,
+        grid_spec=pltpu.PrefetchScalarGridSpec(
+            num_scalar_prefetch=1,
+            grid=(2, steps),
+            in_specs=[pl.BlockSpec((rows, width), whole)] * 2 + [pl.BlockSpec((DEPTH, columns), weight_block)],
+            out_specs=[pl.BlockSpec((rows, columns), whole)] * 2,
+            scratch_shapes=[pltpu.VMEM((rows, columns), jnp.float32)],
+        ),
+        out_shape=[jax.ShapeDtypeStruct((rows, columns), kind) for kind in kinds],
+        compiler_params=params(),
+        cost_estimate=pl.CostEstimate(
+            flops=8 * rows * width * columns, bytes_accessed=8 * width * columns, transcendentals=0
+        ),
+        name="output_parts",
+    )(meta, mine, other, weight)
+
+
+def line_shards(activations, norm_gain, query_weight, kv_weight, out_weight, block_ids, clean_mask):
+    col, row, seq = (lax.axis_index(axis) for axis in ("col", "row", "seq"))
+    slab, width = activations.shape
+    rows = slab // CHUNKS
+    half = slab // 2
+    swap = ((0, 1), (1, 0))
+    at_end = (col == 0) | (col == LINE - 1)
+    meta = jnp.concatenate(
+        [
+            jnp.asarray(FEATURE_ORDER, jnp.int32)[col],
+            jnp.stack([at_end.astype(jnp.int32), row.astype(jnp.int32)]),
+            jnp.asarray(DEST_ORDER, jnp.int32)[col],
+        ]
+    )
+
+    wide_input = activations.astype(jnp.float32)
+    gained = [
+        (wide_input[i * rows : (i + 1) * rows] * norm_gain[None, :]).astype(jnp.bfloat16) for i in range(CHUNKS)
+    ]
+    gathered = []
+    for own in gained:
+        beside = hop(own, OUTER_IN + OUTER_OUT)
+        across = hop(own, MIDDLE)
+        far_middle = hop(beside, MIDDLE)
+        far_end = hop(across, OUTER_OUT)
+        farthest = hop(far_middle, OUTER_OUT)
+        gathered.append((own, beside, across, far_end, far_middle, farthest))
+
+    squares = lax.psum(jnp.sum(wide_input * wide_input, axis=1), ("row", "col"))
+    scaling = lax.rsqrt(squares / D + norm_eps)
+    inverse = jnp.exp(jnp.arange(HD // 2, dtype=jnp.float32) * (-2.0 * math.log(rope_base) / HD))
+    positions = seq * slab + jnp.arange(slab, dtype=jnp.int32)
+    angles = positions.astype(jnp.float32)[:, None] * inverse[None, :]
+    cosine = jnp.concatenate([jnp.cos(angles)] * 2, axis=1) * scaling[:, None]
+    sine = jnp.concatenate([-jnp.sin(angles), jnp.sin(angles)], axis=1) * scaling[:, None]
+
+    local_weight = lax.dynamic_slice_in_dim(kv_weight, col * width, width, 0)
+    local_input = (wide_input * norm_gain[None, :]).astype(jnp.bfloat16)
+    term = jnp.einsum("td,dke->kte", local_input, local_weight, preferred_element_type=jnp.float32)
+    kept = lax.dynamic_slice_in_dim(term, row * half, half, 1)
+    given = lax.dynamic_slice_in_dim(term, (1 - row) * half, half, 1)
+    both = (kept + hop(given, swap, "row")).astype(jnp.bfloat16)
+    kv_sum = lax.dynamic_slice_in_dim(both, col * HD, HD, 2).astype(jnp.float32)
+    for offset in range(1, LINE):
+        share = lax.dynamic_slice_in_dim(both, (col + offset) % LINE * HD, HD, 2)
+        kv_sum += hop(share, [(i, (i + offset) % LINE) for i in range(LINE)]).astype(jnp.float32)
+    my_cosine = lax.dynamic_slice_in_dim(cosine, row * half, half, 0)
+    my_sine = lax.dynamic_slice_in_dim(sine, row * half, half, 0)
+    my_scaling = lax.dynamic_slice_in_dim(scaling, row * half, half, 0)
+    turned = jnp.concatenate([kv_sum[0, :, HD // 2 :], kv_sum[0, :, : HD // 2]], axis=1)
+    key_rows = (kv_sum[0] * my_cosine + turned * my_sine).astype(jnp.bfloat16)
+    value_rows = (kv_sum[1] * my_scaling[:, None]).astype(jnp.bfloat16)
+    spread = lax.all_gather(jnp.stack([key_rows, value_rows]), ("seq", "row"), axis=0)
+    keys = spread[:, 0].reshape(-1, HD)
+    values = spread[:, 1].reshape(-1, HD)
+    values = jnp.concatenate([values, jnp.ones_like(values)], axis=1)
+
+    ids = block_ids[None, :]
+    cut = jnp.where(clean_mask == 1, block_ids, jnp.iinfo(jnp.int32).max)[None, :]
+    my_ids = lax.dynamic_slice_in_dim(block_ids, seq * slab, slab, 0)[:, None]
+
+    out = []
+    for i, (own, beside, across, far_end, far_middle, farthest) in enumerate(gathered):
+        spot = slice(i * rows, (i + 1) * rows)
+        so_far = project_first(meta, ((0,), (1,), (2, 3)), (own, beside, across, far_end), query_weight)
+        mine, other = project_last(meta, far_middle, farthest, query_weight, so_far)
+        attended = attend(
+            mine, hop(other, swap, "row"), cosine[spot], sine[spot], keys, values, my_ids[spot], ids, cut
+        )
+        other_attended = hop(attended, swap, "row")
+        parts = output_parts(meta, 0, attended, other_attended, out_weight, (jnp.bfloat16, jnp.bfloat16))
+        parts += output_parts(meta, 2, attended, other_attended, out_weight, (jnp.bfloat16, jnp.float32))
+        inward = hop(parts[0], OUTER_IN)
+        inward_next = hop(parts[1], OUTER_IN)
+        through = hop(parts[1] + inward, MIDDLE)
+        last_outer = hop(jnp.where(at_end, parts[2], parts[0] + through), OUTER_IN + OUTER_OUT)
+        last_middle = hop(parts[2] + inward_next, MIDDLE)
+        out.append(
+            (parts[3] + last_outer.astype(jnp.float32) + last_middle.astype(jnp.float32)).astype(jnp.bfloat16)
+        )
+    return jnp.concatenate(out, axis=0)
+
+
 def solution(mesh):
     placed = (
         P("seq", ("row", "col")),
@@ -103,6 +440,11 @@
         P(),
         P(),
     )
+    on_line = mesh.shape["col"] == LINE == KVH and mesh.shape["row"] == 2
     return jax.shard_map(
-        shards, mesh=mesh, in_specs=placed, out_specs=P("seq", ("row", "col")), check_vma=False
-    )
+        line_shards if on_line else gathered_shards,
+        mesh=mesh,
+        in_specs=placed,
+        out_specs=P("seq", ("row", "col")),
+        check_vma=False,
+    )

time: 595 us -> 430 us (0.72)
  waiting for transfers between devices: 429 us -> 88 us
  Pallas kernels: 0 us -> 193 us
  matrix products: 86.6 us -> 3.66 us
  starting transfers between devices: 0.17 us -> 75.3 us
  blocking collectives: 35.2 us -> 16 us
  local copies, waits for them, and re-layouts: 10.7 us -> 20.5 us
    reduce_scatter x2 -> x0, waiting for transfers between devices: 278 us -> none  [the longest x1 278 us: shards(): lax.psum_scatter(partial_out, 'col', scatter_dimension=1, tiled=True)]
    pallas_call x0 -> x20, Pallas kernels: none -> 193 us  [the longest x8 82.2 us: output_parts(): pl.pallas_call(output_kernel, grid_spec=pltpu.PrefetchScalarGridSpec(num_...]
    all_gather x2 -> x1, waiting for transfers between devices: 151 us -> 0.01 us  [line_shards(): lax.all_gather(jnp.stack([key_rows, value_rows]), ('seq', 'row'), axis=0)]
    ppermute x0 -> x52, waiting for transfers between devices: none -> 88 us  [hop(): return lax.ppermute(values, axis, list(pairs))]
    dot_general x5 -> x1, matrix products: 86.6 us -> 3.66 us  [line_shards(): jnp.einsum('td,dke->kte', local_input, local_weight, preferred_element_ty...]
    ppermute x0 -> x52, starting transfers between devices: none -> 75.3 us  [hop(): return lax.ppermute(values, axis, list(pairs))]
    all_gather x2 -> x0, blocking collectives: 20.6 us -> none  [the longest x1 10.4 us: shards(): value_piece = lax.all_gather(value_rows, 'seq', axis=0, tiled=True)]
    slice x1 -> x7, local copies, waits for them, and re-layouts: 0.97 us -> 8.09 us  [the longest x5 6.03 us: line_shards(): my_ids[spot]]
  transfers between devices with their start and end apart: 5 -> 53, of which waited for: 3 -> 19; matrix products, arithmetic and copies ran while one was open for 6% -> 8% of each run, Pallas kernels for 0% -> 45%
where the time goes in v1:
time: 430 us; the launch traced here: 427 us
  Pallas kernels  193 us (45%)
  waiting for transfers between devices  88 us (20%)
  starting transfers between devices  75.3 us (18%)
  local copies, waits for them, and re-layouts  20.5 us (5%)
  other arithmetic  16.8 us (4%)
  blocking collectives  16 us (4%)
  between operations  14.4 us (3%)
    ppermute x52, waiting for transfers between devices, hop(): return lax.ppermute(values, axis, list(pairs))  88 us
    pallas_call x8, Pallas kernels, output_parts(): pl.pallas_call(output_kernel, grid_spec=pltpu.PrefetchScalarGridSpec(num_...  82.2 us
    ppermute x52, starting transfers between devices, hop(): return lax.ppermute(values, axis, list(pairs))  75.3 us
    pallas_call x4, Pallas kernels, project_first(): pl.pallas_call(functools.partial(project_first_kernel, slots), grid_spec=...  59.8 us
    pallas_call x4, Pallas kernels, project_last(): pl.pallas_call(project_last_kernel, grid_spec=pltpu.PrefetchScalarGridSpe...  25.5 us
    pallas_call x4, Pallas kernels, attend(): pl.pallas_call(attend_kernel, out_shape=jax.ShapeDtypeStruct((rows, width...  25.3 us
    psum x1, blocking collectives, line_shards(): squares = lax.psum(jnp.sum(wide_input * wide_input, axis=1), ('row', 'col'))  16 us
  transfers between devices with their start and end apart: 53, of which 19 were waited for; matrix products, arithmetic and copies ran while one was open for 8% of the time, Pallas kernels for 45%

profile of v1, /device:TPU:8, one launch (start us, length us, event | category | flops | bytes accessed | tf_op | source)
XLA Modules:
  0.0 427.4 jit_solution(1006397742117268325)
XLA Ops:
  9.2 3.5 collective-permute-start.3
  12.8 6.3 %constant_dynamic-slice_fusion.3 = bf16[2048,2,512]{2,1,0:T(2,128)(2,1)S(1)} fusion(bf16[8192,2,512]{2,1,0:T(2,128)(2,1)} %param.12, s32[]{:T(128)S(6)} %select_n.71), kind=kLoop, calls=%fused_computation.48 | loop fusion | bytes 8388612 | tf_op jit(solution)/shard_map/dynamic_slice | solution.py:386
  19.1 3.7 fusion
  27.1 16.0 %psum.7 = f32[512]{0:T(512)S(1)} all-reduce(f32[512]{0:T(512)S(1)} %multiply_reduce_fusion), channel_id=1, replica_groups=mesh['seq'=4,'row'=2,'col'=4] {'row','col'}, use_global_device_ids=true, to_apply=%region_1.0 | all-reduce | flops 512 | bytes 4096 | tf_op jit(solution)/shard_map/psum | solution.py:378
  49.3 3.3 collective-permute-start.8
  60.8 3.9 collective-permute-start.19
  70.4 2.4 collective-permute-start.43
  72.8 4.7 %collective-permute-done.19.refs_2_ = bf16[128,2048]{1,0:T(8,128)(2,1)S(1)} collective-permute-done((bf16[128,2048]{1,0:T(8,128)(2,1)S(1)}, bf16[128,2048]{1,0:T(8,128)(2,1)S(1)}, u32[]{:S(2)}, u32[]{:S(2)}) %collective-permute-start.19) | collective-permute-done | bytes 524320 | tf_op jit(solution)/shard_map/ppermute | solution.py:110
  79.6 2.7 collective-permute-start.4
  84.1 4.7 %collective-permute-done.31.refs_2_ = bf16[128,2048]{1,0:T(8,128)(2,1)} collective-permute-done((bf16[128,2048]{1,0:T(8,128)(2,1)S(1)}, bf16[128,2048]{1,0:T(8,128)(2,1)}, u32[]{:S(2)}, u32[]{:S(2)}) %collective-permute-start.31) | collective-permute-done | bytes 524320 | tf_op jit(solution)/shard_map/ppermute | solution.py:110
  88.9 3.9 collective-permute-start.1
  95.4 4.7 %collective-permute-done.43.refs_2_ = bf16[128,2048]{1,0:T(8,128)(2,1)} collective-permute-done((bf16[128,2048]{1,0:T(8,128)(2,1)S(1)}, bf16[128,2048]{1,0:T(8,128)(2,1)}, u32[]{:S(2)}, u32[]{:S(2)}) %collective-permute-start.43) | collective-permute-done | bytes 524320 | tf_op jit(solution)/shard_map/ppermute | solution.py:110
  100.1 3.9 collective-permute-start.17
  105.4 5.5 %collective-permute-done.4.refs_3_ = bf16[128,2048]{1,0:T(8,128)(2,1)} collective-permute-done((bf16[128,2048]{1,0:T(8,128)(2,1)S(1)}, bf16[128,2048]{1,0:T(8,128)(2,1)}, u32[]{:S(2)}, u32[]{:S(2)}) %collective-permute-start.4) | collective-permute-done | bytes 524320 | tf_op jit(solution)/shard_map/ppermute | solution.py:110
  112.8 15.0 %project_first.4.so_far_ref = f32[128,2048]{1,0:T(8,128)S(1)} custom-call(s32[10]{0:T(128)S(1)} %pad_add_fusion.meta_ref, bf16[128,2048]{1,0:T(8,128)(2,1)S(1)} %get-tuple-element.53.refs_0_, bf16[128,2048]{1,0:T(8,128)(2,1)S(1)} %collective-permute-done.refs_1_, bf16[128,2048]{1,0:T(8,128)(2,1)S(1)} %collective-permute-done.3.refs_2_, ...), custom_call_target="tpu_custom_call" | custom-call | flops 3221225472 | bytes 25165824 | tf_op jit(solution)/shard_map/project_first/pallas_call | solution.py:163
  127.8 3.3 collective-permute-start.44
  133.1 15.0 %project_first.5.so_far_ref = f32[128,2048]{1,0:T(8,128)S(1)} custom-call(s32[10]{0:T(128)S(1)} %pad_add_fusion.meta_ref, bf16[128,2048]{1,0:T(8,128)(2,1)S(1)} %get-tuple-element.54.refs_0_, bf16[128,2048]{1,0:T(8,128)(2,1)S(1)} %copy-done.3, bf16[128,2048]{1,0:T(8,128)(2,1)S(1)} %copy-done.1, bf16[128,2048]{1,0:T(8,128)(2,1)S(1)} %collective-permute-done.20.refs_3_, ...), custom_call_target="tpu_custom_call" | custom-call | flops 3221225472 | bytes 25165824 | tf_op jit(solution)/shard_map/project_first/pallas_call | solution.py:163
  152.1 14.9 %project_first.6.so_far_ref = f32[128,2048]{1,0:T(8,128)S(1)} custom-call(s32[10]{0:T(128)S(1)} %pad_add_fusion.meta_ref, bf16[128,2048]{1,0:T(8,128)(2,1)S(1)} %get-tuple-element.56.refs_0_, bf16[128,2048]{1,0:T(8,128)(2,1)} %collective-permute-done.28.refs_1_, bf16[128,2048]{1,0:T(8,128)(2,1)} %collective-permute-done.31.refs_2_, ...), custom_call_target="tpu_custom_call" | custom-call | flops 3221225472 | bytes 25165824 | tf_op jit(solution)/shard_map/project_first/pallas_call | solution.py:163
  168.5 14.9 %project_first.7.so_far_ref = f32[128,2048]{1,0:T(8,128)S(1)} custom-call(s32[10]{0:T(128)S(1)} %pad_add_fusion.meta_ref, bf16[128,2048]{1,0:T(8,128)(2,1)S(1)} %get-tuple-element.55.refs_0_, bf16[128,2048]{1,0:T(8,128)(2,1)} %collective-permute-done.40.refs_1_, bf16[128,2048]{1,0:T(8,128)(2,1)} %collective-permute-done.43.refs_2_, ...), custom_call_target="tpu_custom_call" | custom-call | flops 3221225472 | bytes 25165824 | tf_op jit(solution)/shard_map/project_first/pallas_call | solution.py:163
  183.5 6.4 %project_last.4 = (f32[128,1024]{1,0:T(8,128)S(1)}, f32[128,1024]{1,0:T(8,128)}) custom-call(s32[10]{0:T(128)S(1)} %pad_add_fusion.meta_ref, bf16[128,2048]{1,0:T(8,128)(2,1)S(1)} %collective-permute-done.1.middle_ref, bf16[128,2048]{1,0:T(8,128)(2,1)S(1)} %collective-permute-done.2.end_ref, bf16[8192,2048]{1,0:T(8,128)(2,1)} %weight_ref.21, ...), custom_call_target="tpu_custom_call" | custom-call | flops 1073741824 | bytes 8388608 | tf_op jit(solution)/shard_map/project_last/pallas_call | solution.py:215
  190.0 6.4 %project_last.5 = (f32[128,1024]{1,0:T(8,128)S(1)}, f32[128,1024]{1,0:T(8,128)}) custom-call(s32[10]{0:T(128)S(1)} %pad_add_fusion.meta_ref, bf16[128,2048]{1,0:T(8,128)(2,1)S(1)} %collective-permute-done.17.middle_ref, bf16[128,2048]{1,0:T(8,128)(2,1)S(1)} %collective-permute-done.18.end_ref, bf16[8192,2048]{1,0:T(8,128)(2,1)} %weight_ref.21, ...), custom_call_target="tpu_custom_call" | custom-call | flops 1073741824 | bytes 8388608 | tf_op jit(solution)/shard_map/project_last/pallas_call | solution.py:215
  196.9 6.4 %project_last.6 = (f32[128,1024]{1,0:T(8,128)S(1)}, f32[128,1024]{1,0:T(8,128)}) custom-call(s32[10]{0:T(128)S(1)} %pad_add_fusion.meta_ref, bf16[128,2048]{1,0:T(8,128)(2,1)S(1)} %collective-permute-done.29.middle_ref, bf16[128,2048]{1,0:T(8,128)(2,1)S(1)} %collective-permute-done.30.end_ref, bf16[8192,2048]{1,0:T(8,128)(2,1)} %weight_ref.21, ...), custom_call_target="tpu_custom_call" | custom-call | flops 1073741824 | bytes 8388608 | tf_op jit(solution)/shard_map/project_last/pallas_call | solution.py:215
  203.4 6.4 %project_last.7 = (f32[128,1024]{1,0:T(8,128)S(1)}, f32[128,1024]{1,0:T(8,128)}) custom-call(s32[10]{0:T(128)S(1)} %pad_add_fusion.meta_ref, bf16[128,2048]{1,0:T(8,128)(2,1)S(1)} %collective-permute-done.41.middle_ref, bf16[128,2048]{1,0:T(8,128)(2,1)S(1)} %collective-permute-done.42.end_ref, bf16[8192,2048]{1,0:T(8,128)(2,1)} %weight_ref.21, ...), custom_call_target="tpu_custom_call" | custom-call | flops 1073741824 | bytes 8388608 | tf_op jit(solution)/shard_map/project_last/pallas_call | solution.py:215
  211.8 6.6 %attend.4.mine_ref = bf16[128,1024]{1,0:T(8,128)(2,1)S(1)} custom-call(f32[128,1024]{1,0:T(8,128)S(1)} %get-tuple-element.29.mine_ref, f32[128,1024]{1,0:T(8,128)} %collective-permute-done.5.arrived_ref, f32[128,128]{1,0:T(8,128)S(1)} %copy-done.5, f32[128,128]{1,0:T(8,128)S(1)} %copy-done.4, bf16[2048,128]{1,0:T(8,128)(2,1)S(1)} %bitcast.48, ...), custom_call_target="tpu_custom_call" | custom-call | flops 2147483648 | bytes 2621440 | tf_op jit(solution)/shard_map/attend/pallas_call | solution.py:275
  218.6 6.6 %attend.5.mine_ref = bf16[128,1024]{1,0:T(8,128)(2,1)S(1)} custom-call(f32[128,1024]{1,0:T(8,128)S(1)} %get-tuple-element.35.mine_ref, f32[128,1024]{1,0:T(8,128)} %collective-permute-done.21.arrived_ref, f32[128,128]{1,0:T(8,128)S(1)} %get-tuple-element.91.cosine_ref, f32[128,128]{1,0:T(8,128)S(1)} %get-tuple-element.73.sine_ref, ...), custom_call_target="tpu_custom_call" | custom-call | flops 2147483648 | bytes 2621440 | tf_op jit(solution)/shard_map/attend/pallas_call | solution.py:275
  225.7 6.6 %attend.6.mine_ref = bf16[128,1024]{1,0:T(8,128)(2,1)S(1)} custom-call(f32[128,1024]{1,0:T(8,128)S(1)} %get-tuple-element.41.mine_ref, f32[128,1024]{1,0:T(8,128)} %collective-permute-done.33.arrived_ref, f32[128,128]{1,0:T(8,128)S(1)} %get-tuple-element.92.cosine_ref, f32[128,128]{1,0:T(8,128)S(1)} %get-tuple-element.72.sine_ref, ...), custom_call_target="tpu_custom_call" | custom-call | flops 2147483648 | bytes 2621440 | tf_op jit(solution)/shard_map/attend/pallas_call | solution.py:275
  232.4 5.5 %attend.7.mine_ref = bf16[128,1024]{1,0:T(8,128)(2,1)S(1)} custom-call(f32[128,1024]{1,0:T(8,128)S(1)} %get-tuple-element.47.mine_ref, f32[128,1024]{1,0:T(8,128)S(1)} %collective-permute-done.45.arrived_ref, f32[128,128]{1,0:T(8,128)S(1)} %get-tuple-element.93.cosine_ref, f32[128,128]{1,0:T(8,128)S(1)} %get-tuple-element.71.sine_ref, ...), custom_call_target="tpu_custom_call" | custom-call | flops 2147483648 | bytes 2621440 | tf_op jit(solution)/shard_map/attend/pallas_call | solution.py:275
  238.5 10.3 %output_parts.9 = (bf16[128,2048]{1,0:T(8,128)(2,1)S(1)}, bf16[128,2048]{1,0:T(8,128)(2,1)S(1)}) custom-call(s32[10]{0:T(128)S(1)} %pad_add_fusion.meta_ref, bf16[128,1024]{1,0:T(8,128)(2,1)S(1)} %attend.4.mine_ref, bf16[128,1024]{1,0:T(8,128)(2,1)S(1)} %collective-permute-done.10.other_ref, bf16[2048,8192]{1,0:T(8,128)(2,1)} %weight_ref.23), custom_call_target="tpu_custom_call" | custom-call | flops 2147483648 | bytes 16777216 | tf_op jit(solution)/shard_map/output_parts/pallas_call | solution.py:332
  251.4 10.3 %output_parts.11 = (bf16[128,2048]{1,0:T(8,128)(2,1)S(1)}, bf16[128,2048]{1,0:T(8,128)(2,1)S(1)}) custom-call(s32[10]{0:T(128)S(1)} %pad_add_fusion.meta_ref, bf16[128,1024]{1,0:T(8,128)(2,1)S(1)} %attend.5.mine_ref, bf16[128,1024]{1,0:T(8,128)(2,1)S(1)} %collective-permute-done.22.other_ref, bf16[2048,8192]{1,0:T(8,128)(2,1)} %weight_ref.23), custom_call_target="tpu_custom_call" | custom-call | flops 2147483648 | bytes 16777216 | tf_op jit(solution)/shard_map/output_parts/pallas_call | solution.py:332
  263.0 10.3 %output_parts.13 = (bf16[128,2048]{1,0:T(8,128)(2,1)S(1)}, bf16[128,2048]{1,0:T(8,128)(2,1)S(1)}) custom-call(s32[10]{0:T(128)S(1)} %pad_add_fusion.meta_ref, bf16[128,1024]{1,0:T(8,128)(2,1)S(1)} %attend.6.mine_ref, bf16[128,1024]{1,0:T(8,128)(2,1)S(1)} %collective-permute-done.34.other_ref, bf16[2048,8192]{1,0:T(8,128)(2,1)} %weight_ref.23), custom_call_target="tpu_custom_call" | custom-call | flops 2147483648 | bytes 16777216 | tf_op jit(solution)/shard_map/output_parts/pallas_call | solution.py:332
  274.5 10.3 %output_parts.15 = (bf16[128,2048]{1,0:T(8,128)(2,1)S(1)}, bf16[128,2048]{1,0:T(8,128)(2,1)S(1)}) custom-call(s32[10]{0:T(128)S(1)} %pad_add_fusion.meta_ref, bf16[128,1024]{1,0:T(8,128)(2,1)S(1)} %attend.7.mine_ref, bf16[128,1024]{1,0:T(8,128)(2,1)S(1)} %collective-permute-done.46.other_ref, bf16[2048,8192]{1,0:T(8,128)(2,1)} %weight_ref.23), custom_call_target="tpu_custom_call" | custom-call | flops 2147483648 | bytes 16777216 | tf_op jit(solution)/shard_map/output_parts/pallas_call | solution.py:332
  286.1 10.3 %output_parts.8 = (bf16[128,2048]{1,0:T(8,128)(2,1)S(1)}, f32[128,2048]{1,0:T(8,128)S(1)}) custom-call(s32[10]{0:T(128)S(1)} %pad_add_fusion.meta_ref, bf16[128,1024]{1,0:T(8,128)(2,1)S(1)} %attend.4.mine_ref, bf16[128,1024]{1,0:T(8,128)(2,1)S(1)} %collective-permute-done.10.other_ref, bf16[2048,8192]{1,0:T(8,128)(2,1)} %weight_ref.23), custom_call_target="tpu_custom_call" | custom-call | flops 2147483648 | bytes 16777216 | tf_op jit(solution)/shard_map/output_parts/pallas_call | solution.py:332
  296.5 4.1 collective-permute-start.12
  300.6 10.3 %output_parts.10 = (bf16[128,2048]{1,0:T(8,128)(2,1)S(1)}, f32[128,2048]{1,0:T(8,128)S(1)}) custom-call(s32[10]{0:T(128)S(1)} %pad_add_fusion.meta_ref, bf16[128,1024]{1,0:T(8,128)(2,1)S(1)} %attend.5.mine_ref, bf16[128,1024]{1,0:T(8,128)(2,1)S(1)} %collective-permute-done.22.other_ref, bf16[2048,8192]{1,0:T(8,128)(2,1)} %weight_ref.23), custom_call_target="tpu_custom_call" | custom-call | flops 2147483648 | bytes 16777216 | tf_op jit(solution)/shard_map/output_parts/pallas_call | solution.py:332
  310.9 10.3 %output_parts.12 = (bf16[128,2048]{1,0:T(8,128)(2,1)S(1)}, f32[128,2048]{1,0:T(8,128)S(1)}) custom-call(s32[10]{0:T(128)S(1)} %pad_add_fusion.meta_ref, bf16[128,1024]{1,0:T(8,128)(2,1)S(1)} %attend.6.mine_ref, bf16[128,1024]{1,0:T(8,128)(2,1)S(1)} %collective-permute-done.34.other_ref, bf16[2048,8192]{1,0:T(8,128)(2,1)} %weight_ref.23), custom_call_target="tpu_custom_call" | custom-call | flops 2147483648 | bytes 16777216 | tf_op jit(solution)/shard_map/output_parts/pallas_call | solution.py:332
  321.2 10.3 %output_parts.14 = (bf16[128,2048]{1,0:T(8,128)(2,1)S(1)}, f32[128,2048]{1,0:T(8,128)S(1)}) custom-call(s32[10]{0:T(128)S(1)} %pad_add_fusion.meta_ref, bf16[128,1024]{1,0:T(8,128)(2,1)S(1)} %attend.7.mine_ref, bf16[128,1024]{1,0:T(8,128)(2,1)S(1)} %collective-permute-done.46.other_ref, bf16[2048,8192]{1,0:T(8,128)(2,1)} %weight_ref.23), custom_call_target="tpu_custom_call" | custom-call | flops 2147483648 | bytes 16777216 | tf_op jit(solution)/shard_map/output_parts/pallas_call | solution.py:332
  337.8 3.9 collective-permute-start.36
  341.8 6.4 %collective-permute-done.26 = bf16[128,2048]{1,0:T(8,128)(2,1)S(1)} collective-permute-done((bf16[128,2048]{1,0:T(8,128)(2,1)S(1)}, bf16[128,2048]{1,0:T(8,128)(2,1)S(1)}, u32[]{:S(2)}, u32[]{:S(2)}) %collective-permute-start.26) | collective-permute-done | bytes 524320 | tf_op jit(solution)/shard_map/ppermute | solution.py:110
  350.2 2.4 collective-permute-done.24
  352.7 6.8 %collective-permute-done.38 = bf16[128,2048]{1,0:T(8,128)(2,1)S(1)} collective-permute-done((bf16[128,2048]{1,0:T(8,128)(2,1)S(1)}, bf16[128,2048]{1,0:T(8,128)(2,1)S(1)}, u32[]{:S(2)}, u32[]{:S(2)}) %collective-permute-start.38) | collective-permute-done | bytes 524320 | tf_op jit(solution)/shard_map/ppermute | solution.py:110
  361.4 2.4 collective-permute-done.36
  363.9 6.8 %collective-permute-done.50 = bf16[128,2048]{1,0:T(8,128)(2,1)S(1)} collective-permute-done((bf16[128,2048]{1,0:T(8,128)(2,1)S(1)}, bf16[128,2048]{1,0:T(8,128)(2,1)S(1)}, u32[]{:S(2)}, u32[]{:S(2)}) %collective-permute-start.50) | collective-permute-done | bytes 524320 | tf_op jit(solution)/shard_map/ppermute | solution.py:110
  375.2 6.8 %collective-permute-done.13 = bf16[128,2048]{1,0:T(8,128)(2,1)S(1)} collective-permute-done((bf16[128,2048]{1,0:T(8,128)(2,1)S(1)}, bf16[128,2048]{1,0:T(8,128)(2,1)S(1)}, u32[]{:S(2)}, u32[]{:S(2)}) %collective-permute-start.13) | collective-permute-done | bytes 524320 | tf_op jit(solution)/shard_map/ppermute | solution.py:110
  386.5 6.7 %collective-permute-done.25 = bf16[128,2048]{1,0:T(8,128)(2,1)S(1)} collective-permute-done((bf16[128,2048]{1,0:T(8,128)(2,1)S(1)}, bf16[128,2048]{1,0:T(8,128)(2,1)S(1)}, u32[]{:S(2)}, u32[]{:S(2)}) %collective-permute-start.25) | collective-permute-done | bytes 524320 | tf_op jit(solution)/shard_map/ppermute | solution.py:110
  397.7 6.7 %collective-permute-done.37 = bf16[128,2048]{1,0:T(8,128)(2,1)S(1)} collective-permute-done((bf16[128,2048]{1,0:T(8,128)(2,1)S(1)}, bf16[128,2048]{1,0:T(8,128)(2,1)S(1)}, u32[]{:S(2)}, u32[]{:S(2)}) %collective-permute-start.37) | collective-permute-done | bytes 524320 | tf_op jit(solution)/shard_map/ppermute | solution.py:110
  404.4 4.3 %collective-permute-done.39 = bf16[128,2048]{1,0:T(8,128)(2,1)S(1)} collective-permute-done((bf16[128,2048]{1,0:T(8,128)(2,1)S(1)}, bf16[128,2048]{1,0:T(8,128)(2,1)S(1)}, u32[]{:S(2)}, u32[]{:S(2)}) %collective-permute-start.39) | collective-permute-done | bytes 524320 | tf_op jit(solution)/shard_map/ppermute | solution.py:110
  408.9 5.5 %collective-permute-done.49 = bf16[128,2048]{1,0:T(8,128)(2,1)S(1)} collective-permute-done((bf16[128,2048]{1,0:T(8,128)(2,1)S(1)}, bf16[128,2048]{1,0:T(8,128)(2,1)S(1)}, u32[]{:S(2)}, u32[]{:S(2)}) %collective-permute-start.49) | collective-permute-done | bytes 524320 | tf_op jit(solution)/shard_map/ppermute | solution.py:110
  414.4 4.3 %collective-permute-done.51 = bf16[128,2048]{1,0:T(8,128)(2,1)S(1)} collective-permute-done((bf16[128,2048]{1,0:T(8,128)(2,1)S(1)}, bf16[128,2048]{1,0:T(8,128)(2,1)S(1)}, u32[]{:S(2)}, u32[]{:S(2)}) %collective-permute-start.51) | collective-permute-done | bytes 524320 | tf_op jit(solution)/shard_map/ppermute | solution.py:110
  (158 shorter events, 80.7 us)
Async XLA Ops:
  6.5 203.8 %all-gather.3.cloned.1.call-start = ((), (), s32[]{:S(2)}) async-start(), calls=%async_computation | async-start | bytes 1179648 | tf_op jit(solution)/shard_map/all_gather | solution.py:402
  9.2 58.8 %collective-permute-start.3 = (bf16[128,2048]{1,0:T(8,128)(2,1)S(1)}, bf16[128,2048]{1,0:T(8,128)(2,1)S(1)}, u32[]{:S(2)}, u32[]{:S(2)}) collective-permute-start(bf16[128,2048]{1,0:T(8,128)(2,1)S(1)} %get-tuple-element.53.refs_0_), channel_id=1, source_target_pairs={{1,2},{2,1},{5,6},{6,5},{9,10},{10,9},{13,14},{14,13},{17,18},{18,... | collective-permute-start | bytes 1572872 | tf_op jit(solution)/shard_map/ppermute | solution.py:110
  12.7 57.7 %collective-permute-start = (bf16[128,2048]{1,0:T(8,128)(2,1)S(1)}, bf16[128,2048]{1,0:T(8,128)(2,1)S(1)}, u32[]{:S(2)}, u32[]{:S(2)}) collective-permute-start(bf16[128,2048]{1,0:T(8,128)(2,1)S(1)} %get-tuple-element.53.refs_0_), channel_id=1, source_target_pairs={{0,1},{3,2},{2,3},{1,0},{4,5},{7,6},{6,7},{5,4},{8,9},{11,10},{10,... | collective-permute-start | bytes 1572872 | tf_op jit(solution)/shard_map/ppermute | solution.py:110
  25.0 21.0 %collective-permute-start.6 = (f32[2,256,512]{2,1,0:T(8,128)}, f32[2,256,512]{2,1,0:T(8,128)}, u32[]{:S(2)}, u32[]{:S(2)}) collective-permute-start(f32[2,256,512]{2,1,0:T(8,128)} %dynamic-slice_bitcast_fusion), channel_id=1, source_target_pairs={{0,4},{4,0},{1,5},{5,1},{2,6},{6,2},{3,7},{7,3},{8,12},{12,8},{9,1... | collective-permute-start | bytes 3145736 | tf_op jit(solution)/shard_map/ppermute | solution.py:110
  60.8 16.7 %collective-permute-start.19 = (bf16[128,2048]{1,0:T(8,128)(2,1)S(1)}, bf16[128,2048]{1,0:T(8,128)(2,1)S(1)}, u32[]{:S(2)}, u32[]{:S(2)}) collective-permute-start(bf16[128,2048]{1,0:T(8,128)(2,1)S(1)} %get-tuple-element.54.refs_0_), channel_id=1, source_target_pairs={{1,2},{2,1},{5,6},{6,5},{9,10},{10,9},{13,14},{14,13},{17,18},{18,... | collective-permute-start | bytes 1572872 | tf_op jit(solution)/shard_map/ppermute | solution.py:110
  64.8 24.1 %collective-permute-start.31 = (bf16[128,2048]{1,0:T(8,128)(2,1)S(1)}, bf16[128,2048]{1,0:T(8,128)(2,1)}, u32[]{:S(2)}, u32[]{:S(2)}) collective-permute-start(bf16[128,2048]{1,0:T(8,128)(2,1)S(1)} %get-tuple-element.56.refs_0_), channel_id=1, source_target_pairs={{1,2},{2,1},{5,6},{6,5},{9,10},{10,9},{13,14},{14,13},{17,18},{18,... | collective-permute-start | bytes 1572872 | tf_op jit(solution)/shard_map/ppermute | solution.py:110
  68.0 24.8 %collective-permute-start.28 = (bf16[128,2048]{1,0:T(8,128)(2,1)S(1)}, bf16[128,2048]{1,0:T(8,128)(2,1)}, u32[]{:S(2)}, u32[]{:S(2)}) collective-permute-start(bf16[128,2048]{1,0:T(8,128)(2,1)S(1)} %get-tuple-element.56.refs_0_), channel_id=1, source_target_pairs={{0,1},{3,2},{2,3},{1,0},{4,5},{7,6},{6,7},{5,4},{8,9},{11,10},{10,... | collective-permute-start | bytes 1572872 | tf_op jit(solution)/shard_map/ppermute | solution.py:110
  70.4 29.7 %collective-permute-start.43 = (bf16[128,2048]{1,0:T(8,128)(2,1)S(1)}, bf16[128,2048]{1,0:T(8,128)(2,1)}, u32[]{:S(2)}, u32[]{:S(2)}) collective-permute-start(bf16[128,2048]{1,0:T(8,128)(2,1)S(1)} %get-tuple-element.55.refs_0_), channel_id=1, source_target_pairs={{1,2},{2,1},{5,6},{6,5},{9,10},{10,9},{13,14},{14,13},{17,18},{18,... | collective-permute-start | bytes 1572872 | tf_op jit(solution)/shard_map/ppermute | solution.py:110
  77.5 26.5 %collective-permute-start.40 = (bf16[128,2048]{1,0:T(8,128)(2,1)S(1)}, bf16[128,2048]{1,0:T(8,128)(2,1)}, u32[]{:S(2)}, u32[]{:S(2)}) collective-permute-start(bf16[128,2048]{1,0:T(8,128)(2,1)S(1)} %get-tuple-element.55.refs_0_), channel_id=1, source_target_pairs={{0,1},{3,2},{2,3},{1,0},{4,5},{7,6},{6,7},{5,4},{8,9},{11,10},{10,... | collective-permute-start | bytes 1572872 | tf_op jit(solution)/shard_map/ppermute | solution.py:110
  79.6 31.2 %collective-permute-start.4 = (bf16[128,2048]{1,0:T(8,128)(2,1)S(1)}, bf16[128,2048]{1,0:T(8,128)(2,1)}, u32[]{:S(2)}, u32[]{:S(2)}) collective-permute-start(bf16[128,2048]{1,0:T(8,128)(2,1)S(1)} %collective-permute-done.3.refs_2_), channel_id=1, source_target_pairs={{2,3},{1,0},{6,7},{5,4},{10,11},{9,8},{14,15},{13,12},{18,19},{17,... | collective-permute-start | bytes 1572872 | tf_op jit(solution)/shard_map/ppermute | solution.py:110
  88.9 38.9 %collective-permute-start.1 = (bf16[128,2048]{1,0:T(8,128)(2,1)S(1)}, bf16[128,2048]{1,0:T(8,128)(2,1)S(1)}, u32[]{:S(2)}, u32[]{:S(2)}) collective-permute-start(bf16[128,2048]{1,0:T(8,128)(2,1)S(1)} %collective-permute-done.refs_1_), channel_id=1, source_target_pairs={{1,2},{2,1},{5,6},{6,5},{9,10},{10,9},{13,14},{14,13},{17,18},{18,... | collective-permute-start | bytes 1572872 | tf_op jit(solution)/shard_map/ppermute | solution.py:110
  92.8 38.3 %collective-permute-start.20 = (bf16[128,2048]{1,0:T(8,128)(2,1)}, bf16[128,2048]{1,0:T(8,128)(2,1)S(1)}, u32[]{:S(2)}, u32[]{:S(2)}) collective-permute-start(bf16[128,2048]{1,0:T(8,128)(2,1)} %copy-done), channel_id=1, source_target_pairs={{2,3},{1,0},{6,7},{5,4},{10,11},{9,8},{14,15},{13,12},{18,19},{17,... | collective-permute-start | bytes 1572872 | tf_op jit(solution)/shard_map/ppermute | solution.py:110
  100.1 47.9 %collective-permute-start.17 = (bf16[128,2048]{1,0:T(8,128)(2,1)}, bf16[128,2048]{1,0:T(8,128)(2,1)S(1)}, u32[]{:S(2)}, u32[]{:S(2)}) collective-permute-start(bf16[128,2048]{1,0:T(8,128)(2,1)} %copy-done.2), channel_id=1, source_target_pairs={{1,2},{2,1},{5,6},{6,5},{9,10},{10,9},{13,14},{14,13},{17,18},{18,... | collective-permute-start | bytes 1572872 | tf_op jit(solution)/shard_map/ppermute | solution.py:110
  104.0 45.3 %collective-permute-start.32 = (bf16[128,2048]{1,0:T(8,128)(2,1)}, bf16[128,2048]{1,0:T(8,128)(2,1)S(1)}, u32[]{:S(2)}, u32[]{:S(2)}) collective-permute-start(bf16[128,2048]{1,0:T(8,128)(2,1)} %collective-permute-done.31.refs_2_), channel_id=1, source_target_pairs={{2,3},{1,0},{6,7},{5,4},{10,11},{9,8},{14,15},{13,12},{18,19},{17,... | collective-permute-start | bytes 1572872 | tf_op jit(solution)/shard_map/ppermute | solution.py:110
  110.9 39.8 %collective-permute-start.29 = (bf16[128,2048]{1,0:T(8,128)(2,1)}, bf16[128,2048]{1,0:T(8,128)(2,1)S(1)}, u32[]{:S(2)}, u32[]{:S(2)}) collective-permute-start(bf16[128,2048]{1,0:T(8,128)(2,1)} %collective-permute-done.28.refs_1_), channel_id=1, source_target_pairs={{1,2},{2,1},{5,6},{6,5},{9,10},{10,9},{13,14},{14,13},{17,18},{18,... | collective-permute-start | bytes 1572872 | tf_op jit(solution)/shard_map/ppermute | solution.py:110
  127.8 40.8 %collective-permute-start.44 = (bf16[128,2048]{1,0:T(8,128)(2,1)}, bf16[128,2048]{1,0:T(8,128)(2,1)S(1)}, u32[]{:S(2)}, u32[]{:S(2)}) collective-permute-start(bf16[128,2048]{1,0:T(8,128)(2,1)} %collective-permute-done.43.refs_2_), channel_id=1, source_target_pairs={{2,3},{1,0},{6,7},{5,4},{10,11},{9,8},{14,15},{13,12},{18,19},{17,... | collective-permute-start | bytes 1572872 | tf_op jit(solution)/shard_map/ppermute | solution.py:110
  131.1 35.9 %collective-permute-start.41 = (bf16[128,2048]{1,0:T(8,128)(2,1)}, bf16[128,2048]{1,0:T(8,128)(2,1)S(1)}, u32[]{:S(2)}, u32[]{:S(2)}) collective-permute-start(bf16[128,2048]{1,0:T(8,128)(2,1)} %collective-permute-done.40.refs_1_), channel_id=1, source_target_pairs={{1,2},{2,1},{5,6},{6,5},{9,10},{10,9},{13,14},{14,13},{17,18},{18,... | collective-permute-start | bytes 1572872 | tf_op jit(solution)/shard_map/ppermute | solution.py:110
  148.0 35.5 %collective-permute-start.2 = (bf16[128,2048]{1,0:T(8,128)(2,1)S(1)}, bf16[128,2048]{1,0:T(8,128)(2,1)S(1)}, u32[]{:S(2)}, u32[]{:S(2)}) collective-permute-start(bf16[128,2048]{1,0:T(8,128)(2,1)S(1)} %collective-permute-done.1.middle_ref), channel_id=1, source_target_pairs={{2,3},{1,0},{6,7},{5,4},{10,11},{9,8},{14,15},{13,12},{18,19},{17,... | collective-permute-start | bytes 1572872 | tf_op jit(solution)/shard_map/ppermute | solution.py:110
  149.4 40.6 %collective-permute-start.18 = (bf16[128,2048]{1,0:T(8,128)(2,1)S(1)}, bf16[128,2048]{1,0:T(8,128)(2,1)S(1)}, u32[]{:S(2)}, u32[]{:S(2)}) collective-permute-start(bf16[128,2048]{1,0:T(8,128)(2,1)S(1)} %collective-permute-done.17.middle_ref), channel_id=1, source_target_pairs={{2,3},{1,0},{6,7},{5,4},{10,11},{9,8},{14,15},{13,12},{18,19},{17,... | collective-permute-start | bytes 1572872 | tf_op jit(solution)/shard_map/ppermute | solution.py:110
  150.7 46.2 %collective-permute-start.30 = (bf16[128,2048]{1,0:T(8,128)(2,1)S(1)}, bf16[128,2048]{1,0:T(8,128)(2,1)S(1)}, u32[]{:S(2)}, u32[]{:S(2)}) collective-permute-start(bf16[128,2048]{1,0:T(8,128)(2,1)S(1)} %collective-permute-done.29.middle_ref), channel_id=1, source_target_pairs={{2,3},{1,0},{6,7},{5,4},{10,11},{9,8},{14,15},{13,12},{18,19},{17,... | collective-permute-start | bytes 1572872 | tf_op jit(solution)/shard_map/ppermute | solution.py:110
  167.0 36.4 %collective-permute-start.42 = (bf16[128,2048]{1,0:T(8,128)(2,1)S(1)}, bf16[128,2048]{1,0:T(8,128)(2,1)S(1)}, u32[]{:S(2)}, u32[]{:S(2)}) collective-permute-start(bf16[128,2048]{1,0:T(8,128)(2,1)S(1)} %collective-permute-done.41.middle_ref), channel_id=1, source_target_pairs={{2,3},{1,0},{6,7},{5,4},{10,11},{9,8},{14,15},{13,12},{18,19},{17,... | collective-permute-start | bytes 1572872 | tf_op jit(solution)/shard_map/ppermute | solution.py:110
  189.9 21.9 %collective-permute-start.5 = (f32[128,1024]{1,0:T(8,128)}, f32[128,1024]{1,0:T(8,128)}, u32[]{:S(2)}, u32[]{:S(2)}) collective-permute-start(f32[128,1024]{1,0:T(8,128)} %get-tuple-element.30), channel_id=1, source_target_pairs={{0,4},{4,0},{1,5},{5,1},{2,6},{6,2},{3,7},{7,3},{8,12},{12,8},{9,1... | collective-permute-start | bytes 1572872 | tf_op jit(solution)/shard_map/ppermute | solution.py:110
  196.4 22.2 %collective-permute-start.21 = (f32[128,1024]{1,0:T(8,128)}, f32[128,1024]{1,0:T(8,128)}, u32[]{:S(2)}, u32[]{:S(2)}) collective-permute-start(f32[128,1024]{1,0:T(8,128)} %get-tuple-element.36), channel_id=1, source_target_pairs={{0,4},{4,0},{1,5},{5,1},{2,6},{6,2},{3,7},{7,3},{8,12},{12,8},{9,1... | collective-permute-start | bytes 1572872 | tf_op jit(solution)/shard_map/ppermute | solution.py:110
  203.3 22.4 %collective-permute-start.33 = (f32[128,1024]{1,0:T(8,128)}, f32[128,1024]{1,0:T(8,128)}, u32[]{:S(2)}, u32[]{:S(2)}) collective-permute-start(f32[128,1024]{1,0:T(8,128)} %get-tuple-element.42), channel_id=1, source_target_pairs={{0,4},{4,0},{1,5},{5,1},{2,6},{6,2},{3,7},{7,3},{8,12},{12,8},{9,1... | collective-permute-start | bytes 1572872 | tf_op jit(solution)/shard_map/ppermute | solution.py:110
  209.8 22.6 %collective-permute-start.45 = (f32[128,1024]{1,0:T(8,128)}, f32[128,1024]{1,0:T(8,128)S(1)}, u32[]{:S(2)}, u32[]{:S(2)}) collective-permute-start(f32[128,1024]{1,0:T(8,128)} %get-tuple-element.48), channel_id=1, source_target_pairs={{0,4},{4,0},{1,5},{5,1},{2,6},{6,2},{3,7},{7,3},{8,12},{12,8},{9,1... | collective-permute-start | bytes 1572872 | tf_op jit(solution)/shard_map/ppermute | solution.py:110
  218.4 20.0 %collective-permute-start.10 = (bf16[128,1024]{1,0:T(8,128)(2,1)S(1)}, bf16[128,1024]{1,0:T(8,128)(2,1)S(1)}, u32[]{:S(2)}, u32[]{:S(2)}) collective-permute-start(bf16[128,1024]{1,0:T(8,128)(2,1)S(1)} %attend.4.mine_ref), channel_id=1, source_target_pairs={{0,4},{4,0},{1,5},{5,1},{2,6},{6,2},{3,7},{7,3},{8,12},{12,8},{9,1... | collective-permute-start | bytes 786440 | tf_op jit(solution)/shard_map/ppermute | solution.py:110
  225.2 26.2 %collective-permute-start.22 = (bf16[128,1024]{1,0:T(8,128)(2,1)S(1)}, bf16[128,1024]{1,0:T(8,128)(2,1)S(1)}, u32[]{:S(2)}, u32[]{:S(2)}) collective-permute-start(bf16[128,1024]{1,0:T(8,128)(2,1)S(1)} %attend.5.mine_ref), channel_id=1, source_target_pairs={{0,4},{4,0},{1,5},{5,1},{2,6},{6,2},{3,7},{7,3},{8,12},{12,8},{9,1... | collective-permute-start | bytes 786440 | tf_op jit(solution)/shard_map/ppermute | solution.py:110
  232.3 30.7 %collective-permute-start.34 = (bf16[128,1024]{1,0:T(8,128)(2,1)S(1)}, bf16[128,1024]{1,0:T(8,128)(2,1)S(1)}, u32[]{:S(2)}, u32[]{:S(2)}) collective-permute-start(bf16[128,1024]{1,0:T(8,128)(2,1)S(1)} %attend.6.mine_ref), channel_id=1, source_target_pairs={{0,4},{4,0},{1,5},{5,1},{2,6},{6,2},{3,7},{7,3},{8,12},{12,8},{9,1... | collective-permute-start | bytes 786440 | tf_op jit(solution)/shard_map/ppermute | solution.py:110
  238.0 36.6 %collective-permute-start.46 = (bf16[128,1024]{1,0:T(8,128)(2,1)S(1)}, bf16[128,1024]{1,0:T(8,128)(2,1)S(1)}, u32[]{:S(2)}, u32[]{:S(2)}) collective-permute-start(bf16[128,1024]{1,0:T(8,128)(2,1)S(1)} %attend.7.mine_ref), channel_id=1, source_target_pairs={{0,4},{4,0},{1,5},{5,1},{2,6},{6,2},{3,7},{7,3},{8,12},{12,8},{9,1... | collective-permute-start | bytes 786440 | tf_op jit(solution)/shard_map/ppermute | solution.py:110
  248.8 47.6 %collective-permute-start.11 = (bf16[128,2048]{1,0:T(8,128)(2,1)S(1)}, bf16[128,2048]{1,0:T(8,128)(2,1)S(1)}, u32[]{:S(2)}, u32[]{:S(2)}) collective-permute-start(bf16[128,2048]{1,0:T(8,128)(2,1)S(1)} %get-tuple-element.33), channel_id=1, source_target_pairs={{0,1},{3,2},{4,5},{7,6},{8,9},{11,10},{12,13},{15,14},{16,17},{19,... | collective-permute-start | bytes 1572872 | tf_op jit(solution)/shard_map/ppermute | solution.py:110
  250.1 85.8 %collective-permute-start.14 = (bf16[128,2048]{1,0:T(8,128)(2,1)S(1)}, bf16[128,2048]{1,0:T(8,128)(2,1)S(1)}, u32[]{:S(2)}, u32[]{:S(2)}) collective-permute-start(bf16[128,2048]{1,0:T(8,128)(2,1)S(1)} %get-tuple-element.34), channel_id=1, source_target_pairs={{0,1},{3,2},{4,5},{7,6},{8,9},{11,10},{12,13},{15,14},{16,17},{19,... | collective-permute-start | bytes 1572872 | tf_op jit(solution)/shard_map/ppermute | solution.py:110
  261.6 69.8 %collective-permute-start.23 = (bf16[128,2048]{1,0:T(8,128)(2,1)S(1)}, bf16[128,2048]{1,0:T(8,128)(2,1)S(1)}, u32[]{:S(2)}, u32[]{:S(2)}) collective-permute-start(bf16[128,2048]{1,0:T(8,128)(2,1)S(1)} %get-tuple-element.39), channel_id=1, source_target_pairs={{0,1},{3,2},{4,5},{7,6},{8,9},{11,10},{12,13},{15,14},{16,17},{19,... | collective-permute-start | bytes 1572872 | tf_op jit(solution)/shard_map/ppermute | solution.py:110
  273.2 59.7 %collective-permute-start.35 = (bf16[128,2048]{1,0:T(8,128)(2,1)S(1)}, bf16[128,2048]{1,0:T(8,128)(2,1)S(1)}, u32[]{:S(2)}, u32[]{:S(2)}) collective-permute-start(bf16[128,2048]{1,0:T(8,128)(2,1)S(1)} %get-tuple-element.45), channel_id=1, source_target_pairs={{0,1},{3,2},{4,5},{7,6},{8,9},{11,10},{12,13},{15,14},{16,17},{19,... | collective-permute-start | bytes 1572872 | tf_op jit(solution)/shard_map/ppermute | solution.py:110
  284.8 49.6 %collective-permute-start.47 = (bf16[128,2048]{1,0:T(8,128)(2,1)S(1)}, bf16[128,2048]{1,0:T(8,128)(2,1)S(1)}, u32[]{:S(2)}, u32[]{:S(2)}) collective-permute-start(bf16[128,2048]{1,0:T(8,128)(2,1)S(1)} %get-tuple-element.51), channel_id=1, source_target_pairs={{0,1},{3,2},{4,5},{7,6},{8,9},{11,10},{12,13},{15,14},{16,17},{19,... | collective-permute-start | bytes 1572872 | tf_op jit(solution)/shard_map/ppermute | solution.py:110
  296.5 41.3 %collective-permute-start.12 = (bf16[128,2048]{1,0:T(8,128)(2,1)S(1)}, bf16[128,2048]{1,0:T(8,128)(2,1)S(1)}, u32[]{:S(2)}, u32[]{:S(2)}) collective-permute-start(bf16[128,2048]{1,0:T(8,128)(2,1)S(1)} %add.169), channel_id=1, source_target_pairs={{1,2},{2,1},{5,6},{6,5},{9,10},{10,9},{13,14},{14,13},{17,18},{18,... | collective-permute-start | bytes 1572872 | tf_op jit(solution)/shard_map/ppermute | solution.py:110
  332.9 26.5 %collective-permute-start.38 = (bf16[128,2048]{1,0:T(8,128)(2,1)S(1)}, bf16[128,2048]{1,0:T(8,128)(2,1)S(1)}, u32[]{:S(2)}, u32[]{:S(2)}) collective-permute-start(bf16[128,2048]{1,0:T(8,128)(2,1)S(1)} %get-tuple-element.46), channel_id=1, source_target_pairs={{0,1},{3,2},{4,5},{7,6},{8,9},{11,10},{12,13},{15,14},{16,17},{19,... | collective-permute-start | bytes 1572872 | tf_op jit(solution)/shard_map/ppermute | solution.py:110
  334.4 36.3 %collective-permute-start.50 = (bf16[128,2048]{1,0:T(8,128)(2,1)S(1)}, bf16[128,2048]{1,0:T(8,128)(2,1)S(1)}, u32[]{:S(2)}, u32[]{:S(2)}) collective-permute-start(bf16[128,2048]{1,0:T(8,128)(2,1)S(1)} %get-tuple-element.52), channel_id=1, source_target_pairs={{0,1},{3,2},{4,5},{7,6},{8,9},{11,10},{12,13},{15,14},{16,17},{19,... | collective-permute-start | bytes 1572872 | tf_op jit(solution)/shard_map/ppermute | solution.py:110
  335.8 16.7 %collective-permute-start.24 = (bf16[128,2048]{1,0:T(8,128)(2,1)S(1)}, bf16[128,2048]{1,0:T(8,128)(2,1)S(1)}, u32[]{:S(2)}, u32[]{:S(2)}) collective-permute-start(bf16[128,2048]{1,0:T(8,128)(2,1)S(1)} %add.174), channel_id=1, source_target_pairs={{1,2},{2,1},{5,6},{6,5},{9,10},{10,9},{13,14},{14,13},{17,18},{18,... | collective-permute-start | bytes 1572872 | tf_op jit(solution)/shard_map/ppermute | solution.py:110
  337.8 26.0 %collective-permute-start.36 = (bf16[128,2048]{1,0:T(8,128)(2,1)S(1)}, bf16[128,2048]{1,0:T(8,128)(2,1)S(1)}, u32[]{:S(2)}, u32[]{:S(2)}) collective-permute-start(bf16[128,2048]{1,0:T(8,128)(2,1)S(1)} %add.179), channel_id=1, source_target_pairs={{1,2},{2,1},{5,6},{6,5},{9,10},{10,9},{13,14},{14,13},{17,18},{18,... | collective-permute-start | bytes 1572872 | tf_op jit(solution)/shard_map/ppermute | solution.py:110
  348.2 26.8 %collective-permute-start.48 = (bf16[128,2048]{1,0:T(8,128)(2,1)S(1)}, bf16[128,2048]{1,0:T(8,128)(2,1)S(1)}, u32[]{:S(2)}, u32[]{:S(2)}) collective-permute-start(bf16[128,2048]{1,0:T(8,128)(2,1)S(1)} %add.184), channel_id=1, source_target_pairs={{1,2},{2,1},{5,6},{6,5},{9,10},{10,9},{13,14},{14,13},{17,18},{18,... | collective-permute-start | bytes 1572872 | tf_op jit(solution)/shard_map/ppermute | solution.py:110
  352.6 29.4 %collective-permute-start.13 = (bf16[128,2048]{1,0:T(8,128)(2,1)S(1)}, bf16[128,2048]{1,0:T(8,128)(2,1)S(1)}, u32[]{:S(2)}, u32[]{:S(2)}) collective-permute-start(bf16[128,2048]{1,0:T(8,128)(2,1)S(1)} %get-tuple-element.59), channel_id=1, source_target_pairs={{0,1},{3,2},{2,3},{1,0},{4,5},{7,6},{6,7},{5,4},{8,9},{11,10},{10,... | collective-permute-start | bytes 1572872 | tf_op jit(solution)/shard_map/ppermute | solution.py:110
  359.5 26.8 %collective-permute-start.15 = (bf16[128,2048]{1,0:T(8,128)(2,1)S(1)}, bf16[128,2048]{1,0:T(8,128)(2,1)S(1)}, u32[]{:S(2)}, u32[]{:S(2)}) collective-permute-start(bf16[128,2048]{1,0:T(8,128)(2,1)S(1)} %get-tuple-element.60), channel_id=1, source_target_pairs={{1,2},{2,1},{5,6},{6,5},{9,10},{10,9},{13,14},{14,13},{17,18},{18,... | collective-permute-start | bytes 1572872 | tf_op jit(solution)/shard_map/ppermute | solution.py:110
  363.8 29.4 %collective-permute-start.25 = (bf16[128,2048]{1,0:T(8,128)(2,1)S(1)}, bf16[128,2048]{1,0:T(8,128)(2,1)S(1)}, u32[]{:S(2)}, u32[]{:S(2)}) collective-permute-start(bf16[128,2048]{1,0:T(8,128)(2,1)S(1)} %get-tuple-element.61), channel_id=1, source_target_pairs={{0,1},{3,2},{2,3},{1,0},{4,5},{7,6},{6,7},{5,4},{8,9},{11,10},{10,... | collective-permute-start | bytes 1572872 | tf_op jit(solution)/shard_map/ppermute | solution.py:110
  370.7 26.8 %collective-permute-start.27 = (bf16[128,2048]{1,0:T(8,128)(2,1)S(1)}, bf16[128,2048]{1,0:T(8,128)(2,1)S(1)}, u32[]{:S(2)}, u32[]{:S(2)}) collective-permute-start(bf16[128,2048]{1,0:T(8,128)(2,1)S(1)} %get-tuple-element.62), channel_id=1, source_target_pairs={{1,2},{2,1},{5,6},{6,5},{9,10},{10,9},{13,14},{14,13},{17,18},{18,... | collective-permute-start | bytes 1572872 | tf_op jit(solution)/shard_map/ppermute | solution.py:110
  375.0 29.4 %collective-permute-start.37 = (bf16[128,2048]{1,0:T(8,128)(2,1)S(1)}, bf16[128,2048]{1,0:T(8,128)(2,1)S(1)}, u32[]{:S(2)}, u32[]{:S(2)}) collective-permute-start(bf16[128,2048]{1,0:T(8,128)(2,1)S(1)} %get-tuple-element.63), channel_id=1, source_target_pairs={{0,1},{3,2},{2,3},{1,0},{4,5},{7,6},{6,7},{5,4},{8,9},{11,10},{10,... | collective-permute-start | bytes 1572872 | tf_op jit(solution)/shard_map/ppermute | solution.py:110
  381.9 26.8 %collective-permute-start.39 = (bf16[128,2048]{1,0:T(8,128)(2,1)S(1)}, bf16[128,2048]{1,0:T(8,128)(2,1)S(1)}, u32[]{:S(2)}, u32[]{:S(2)}) collective-permute-start(bf16[128,2048]{1,0:T(8,128)(2,1)S(1)} %get-tuple-element.64), channel_id=1, source_target_pairs={{1,2},{2,1},{5,6},{6,5},{9,10},{10,9},{13,14},{14,13},{17,18},{18,... | collective-permute-start | bytes 1572872 | tf_op jit(solution)/shard_map/ppermute | solution.py:110
  386.3 28.2 %collective-permute-start.49 = (bf16[128,2048]{1,0:T(8,128)(2,1)S(1)}, bf16[128,2048]{1,0:T(8,128)(2,1)S(1)}, u32[]{:S(2)}, u32[]{:S(2)}) collective-permute-start(bf16[128,2048]{1,0:T(8,128)(2,1)S(1)} %get-tuple-element.65), channel_id=1, source_target_pairs={{0,1},{3,2},{2,3},{1,0},{4,5},{7,6},{6,7},{5,4},{8,9},{11,10},{10,... | collective-permute-start | bytes 1572872 | tf_op jit(solution)/shard_map/ppermute | solution.py:110
  393.2 25.6 %collective-permute-start.51 = (bf16[128,2048]{1,0:T(8,128)(2,1)S(1)}, bf16[128,2048]{1,0:T(8,128)(2,1)S(1)}, u32[]{:S(2)}, u32[]{:S(2)}) collective-permute-start(bf16[128,2048]{1,0:T(8,128)(2,1)S(1)} %get-tuple-element.66), channel_id=1, source_target_pairs={{1,2},{2,1},{5,6},{6,5},{9,10},{10,9},{13,14},{14,13},{17,18},{18,... | collective-permute-start | bytes 1572872 | tf_op jit(solution)/shard_map/ppermute | solution.py:110
  (22 other events, 237.3 us)
Sparse Core Ops, SparseCore 0:
  84.2 23.9 all-gather.2

commit v2 on v0

--- a/solution.py
+++ b/solution.py
@@ -1,8 +1,11 @@
+import functools
 import math
 
 import jax
 import jax.numpy as jnp
 from jax import lax
+from jax.experimental import pallas as pl
+from jax.experimental.pallas import tpu as pltpu
 from jax.sharding import PartitionSpec as P
 
 D = 16384
@@ -34,7 +37,7 @@
     )
 
 
-def shards(activations, norm_gain, query_weight, kv_weight, out_weight, block_ids, clean_mask):
+def gathered_shards(activations, norm_gain, query_weight, kv_weight, out_weight, block_ids, clean_mask):
     row_count = lax.axis_size("row")
     col_index = lax.axis_index("col")
     seq_index = lax.axis_index("seq")
@@ -93,6 +96,601 @@
     return projected.astype(jnp.bfloat16)
 
 
+LINE = 4
+OUTER_IN = ((0, 1), (3, 2))
+OUTER_OUT = ((2, 3), (1, 0))
+MIDDLE = ((1, 2), (2, 1))
+DEST_ORDER = ((3, 2, 1, 0), (0, 3, 2, 1), (3, 0, 1, 2), (0, 1, 2, 3))
+FEATURE_ORDER = ((0, 1, 2, 3), (1, 0, 2, 3), (2, 3, 1, 0), (3, 2, 1, 0))
+CHUNK_SHARES = (12, 12, 8)
+DEPTH = 512
+BUFFERS = 4
+COST_SCALE = 1.0
+EXTRA = 16
+
+
+def hop(values, pairs, axis="col"):
+    return lax.ppermute(values, axis, list(pairs))
+
+
+def chunk_bounds(slab):
+    whole = sum(CHUNK_SHARES)
+    marks = [slab * sum(CHUNK_SHARES[:i]) // whole // 16 * 16 for i in range(len(CHUNK_SHARES))] + [slab]
+    return list(zip(marks[:-1], marks[1:]))
+
+
+class Order:
+    def __init__(self):
+        self.token = []
+
+    def call(self, body, outs, scratch, inputs, spaces, name, out_spaces=None, aliases=None, cost=1_000_000):
+        count, given = len(inputs), len(outs)
+        tokens = list(self.token)
+
+        def kernel(*refs):
+            refs = refs[:count] + refs[count + len(tokens) :]
+            body(*refs[: count + given], *refs[count + given + 1 :])
+
+        results = pl.pallas_call(
+            kernel,
+            out_shape=list(outs) + [jax.ShapeDtypeStruct((8, HD), jnp.float32)],
+            in_specs=[pl.BlockSpec(memory_space=space) for space in spaces]
+            + [pl.BlockSpec(memory_space=pl.ANY)] * len(tokens),
+            out_specs=[pl.BlockSpec(memory_space=space) for space in (out_spaces or [pltpu.VMEM] * given)]
+            + [pl.BlockSpec(memory_space=pl.ANY)],
+            scratch_shapes=scratch,
+            input_output_aliases=aliases or {},
+            compiler_params=pltpu.CompilerParams(vmem_limit_bytes=36 << 20),
+            cost_estimate=pl.CostEstimate(flops=0, bytes_accessed=int(cost * COST_SCALE), transcendentals=0),
+            name=name,
+        )(*inputs, *tokens)
+        self.token = [results[-1]]
+        return results[:-1]
+
+    def arrive(self, *arrays):
+        def body(*refs):
+            pass
+
+        outs = [jax.ShapeDtypeStruct(array.shape, array.dtype) for array in arrays]
+        spaces = [pl.ANY] * len(arrays)
+        return self.call(body, outs, [], arrays, spaces, "arrive", spaces, {i: i for i in range(len(arrays))}, 0)
+
+    def add(self, groups, kinds):
+        flat = [array for group in groups for array in group]
+
+        def body(*refs):
+            ins, outs = refs[: len(flat)], refs[len(flat) :]
+            for group, out in zip(groups, outs):
+                part, ins = ins[: len(group)], ins[len(group) :]
+                out[...] = sum(ref[...].astype(jnp.float32) for ref in part).astype(out.dtype)
+
+        outs = [jax.ShapeDtypeStruct(group[0].shape, kind) for group, kind in zip(groups, kinds)]
+        return self.call(body, outs, [], flat, [pltpu.VMEM] * len(flat), "adding")
+
+
+def last_sums(order, meta, first, third, fourth, through, inward_next):
+    def body(meta_ref, first_ref, third_ref, through_ref, next_ref, outer, middle):
+        @pl.when(meta_ref[4] == 1)
+        def _():
+            outer[...] = third_ref[...]
+
+        @pl.when(meta_ref[4] == 0)
+        def _():
+            wide = first_ref[...].astype(jnp.float32) + through_ref[...].astype(jnp.float32)
+            outer[...] = wide.astype(outer.dtype)
+
+        wide = third_ref[...].astype(jnp.float32) + next_ref[...].astype(jnp.float32)
+        middle[...] = wide.astype(middle.dtype)
+
+    outer, middle = order.call(
+        body,
+        [jax.ShapeDtypeStruct(first.shape, first.dtype)] * 2,
+        [],
+        [meta, first, third, through, inward_next],
+        [pltpu.SMEM] + [pltpu.VMEM] * 4,
+        "last_sums",
+    )
+    return fourth, outer, middle
+
+
+def gain_rows(order, activations, gain, rows):
+    width = activations.shape[1]
+
+    def body(source, gain_ref, out, held, here):
+        copy = pltpu.make_async_copy(source.at[:rows, :], held, here)
+        copy.start()
+        copy.wait()
+        out[...] = (held[...].astype(jnp.float32) * gain_ref[...]).astype(out.dtype)
+
+    return order.call(
+        body,
+        [jax.ShapeDtypeStruct((rows, width), jnp.bfloat16)],
+        [pltpu.VMEM((rows, width), jnp.bfloat16), pltpu.SemaphoreType.DMA(())],
+        [activations, gain],
+        [pl.ANY, pltpu.VMEM],
+        "gain_rows",
+    )[0]
+
+
+def key_value_terms(order, meta, activations, gain, weight, bounds):
+    slab, width = activations.shape
+    columns = weight.shape[1] * weight.shape[2]
+    half = slab // 2
+    steps = width // DEPTH
+
+    def body(meta_ref, source, gain_ref, weight_ref, kept, given, *refs):
+        outs, (gained, total, held, buffer, here, arrived) = refs[:-6], refs[-6:]
+        brought = pltpu.make_async_copy(source, held, here)
+        brought.start()
+
+        def place(step):
+            return pl.ds(meta_ref[10] * width + step * DEPTH, DEPTH)
+
+        def multiply(step, block):
+            @pl.when(step == 0)
+            def _():
+                brought.wait()
+                wide = held[...].astype(jnp.float32)
+                gained[...] = (wide * gain_ref[...]).astype(gained.dtype)
+                total[...] = jnp.zeros_like(total)
+
+            left = gained[:, pl.ds(pl.multiple_of(step * DEPTH, DEPTH), DEPTH)]
+            total[...] += jnp.dot(left, block.reshape(DEPTH, columns), preferred_element_type=jnp.float32)
+
+        streamed(weight_ref, place, steps, buffer, arrived, multiply)
+        wide = held[...].astype(jnp.float32)
+        squares = jnp.sum(wide * wide, axis=1, keepdims=True)
+        diagonal = lax.broadcasted_iota(jnp.int32, (HD, HD), 0) == lax.broadcasted_iota(jnp.int32, (HD, HD), 1)
+        for out, which in ((given, 1 - meta_ref[5]), (kept, meta_ref[5])):
+            out[:half, :] = total[pl.ds(pl.multiple_of(which * half, half), half), :]
+            out[half:, :] = jnp.zeros((EXTRA, columns), jnp.float32)
+            for block in range(slab // HD):
+                part = jnp.broadcast_to(squares[block * HD : (block + 1) * HD], (HD, HD))
+                out[half : half + 1, block * HD : (block + 1) * HD] = jnp.sum(
+                    jnp.where(diagonal, part, 0.0), axis=0, keepdims=True
+                )
+        for (low, high), out in zip(bounds, outs):
+            out[...] = gained[low:high, :]
+
+    kept, given, *gained = order.call(
+        body,
+        [jax.ShapeDtypeStruct((half + EXTRA, columns), jnp.float32)] * 2
+        + [jax.ShapeDtypeStruct((high - low, width), jnp.bfloat16) for low, high in bounds],
+        [
+            pltpu.VMEM((slab, width), jnp.bfloat16),
+            pltpu.VMEM((slab, columns), jnp.float32),
+            pltpu.VMEM((slab, width), jnp.bfloat16),
+            pltpu.VMEM((BUFFERS, DEPTH) + weight.shape[1:], jnp.bfloat16),
+            pltpu.SemaphoreType.DMA(()),
+            pltpu.SemaphoreType.DMA((BUFFERS,)),
+        ],
+        [meta, activations, gain, weight],
+        [pltpu.SMEM, pl.ANY, pltpu.VMEM, pl.ANY],
+        "key_value_terms",
+        cost=15_000_000,
+    )
+    return kept, given, gained
+
+
+def key_value_shares(order, meta, kept, arrived):
+    rows, columns = kept.shape[0] - EXTRA, kept.shape[1]
+    heads = columns // (2 * HD)
+
+    def body(meta_ref, kept_ref, arrived_ref, *outs):
+        squares = kept_ref[rows : rows + 1, :] + arrived_ref[rows : rows + 1, :]
+        pieces, rest = [], squares
+        for _ in range(3):
+            piece = rest.astype(jnp.bfloat16)
+            pieces.append(piece.astype(jnp.float32))
+            rest = rest - pieces[-1]
+        blocks = 2 * rows // HD
+        lines = [
+            jnp.concatenate([piece[:, i * HD : (i + 1) * HD] for piece in (pieces[0], pieces[1])], axis=1)
+            for i in range(blocks)
+        ] + [
+            jnp.concatenate([pieces[2][:, i * HD : (i + 1) * HD]] * 2, axis=1) for i in range(blocks)
+        ]
+        lines = jnp.concatenate(lines + [jnp.zeros((EXTRA - 2 * blocks, 2 * HD), jnp.float32)], axis=0)
+        for offset, out in enumerate(outs):
+            head = lax.rem(meta_ref[10] + offset, heads)
+            for part in range(2):
+                spot = pl.ds(pl.multiple_of(part * heads * HD + head * HD, HD), HD)
+                both = kept_ref[:rows, spot] + arrived_ref[:rows, spot]
+                out[:rows, part * HD : (part + 1) * HD] = both.astype(out.dtype)
+            out[rows:, :] = lines.astype(out.dtype)
+
+    return order.call(
+        body,
+        [jax.ShapeDtypeStruct((rows + EXTRA, 2 * HD), jnp.float32)]
+        + [jax.ShapeDtypeStruct((rows + EXTRA, 2 * HD), jnp.bfloat16)] * (heads - 1),
+        [],
+        [meta, kept, arrived],
+        [pltpu.SMEM, pltpu.VMEM, pltpu.VMEM],
+        "key_value_shares",
+    )
+
+
+def key_value_rows(order, meta, shares, cosine, sine):
+    rows = shares[0].shape[0] - EXTRA
+    blocks = 2 * rows // HD
+
+    def body(meta_ref, *refs):
+        share_refs, (cosine_ref, sine_ref, out, cosine_out, sine_out, scaling) = refs[: len(shares)], refs[len(shares) :]
+        total = sum(ref[...].astype(jnp.float32) for ref in share_refs)
+        diagonal = lax.broadcasted_iota(jnp.int32, (HD, HD), 0) == lax.broadcasted_iota(jnp.int32, (HD, HD), 1)
+        for block in range(blocks):
+            line = total[rows + block : rows + block + 1, :]
+            last = total[rows + blocks + block : rows + blocks + block + 1, :HD]
+            squares = line[:, :HD] + line[:, HD:] + last
+            factor = lax.rsqrt(squares / D + norm_eps)
+            column = jnp.sum(jnp.where(diagonal, factor, 0.0), axis=1, keepdims=True)
+            scaling[block * HD : (block + 1) * HD, :] = jnp.broadcast_to(column, (HD, HD))
+        cosine_out[...] = cosine_ref[...] * scaling[...]
+        sine_out[...] = sine_ref[...] * scaling[...]
+        spot = pl.ds(pl.multiple_of(meta_ref[5] * rows, rows), rows)
+        raw = total[:rows, :HD]
+        turned = pltpu.roll(raw, HD // 2, 1)
+        out[:, :HD] = (raw * cosine_out[spot, :] + turned * sine_out[spot, :]).astype(out.dtype)
+        out[:, HD:] = (total[:rows, HD:] * scaling[spot, :]).astype(out.dtype)
+
+    inputs = [meta, *shares, cosine, sine]
+    return order.call(
+        body,
+        [jax.ShapeDtypeStruct((rows, 2 * HD), jnp.bfloat16)] + [jax.ShapeDtypeStruct(cosine.shape, jnp.float32)] * 2,
+        [pltpu.VMEM(cosine.shape, jnp.float32)],
+        inputs,
+        [pltpu.SMEM] + [pltpu.VMEM] * (len(inputs) - 1),
+        "key_value_rows",
+    )
+
+
+def final_rows(order, so_far, slab, bounds, parts):
+    rows, width = parts[0].shape
+
+    def body(*refs):
+        ins = refs[: len(parts)]
+        out, held, here = refs[-3:]
+        held[...] = sum(ref[...].astype(jnp.float32) for ref in ins).astype(held.dtype)
+        copy = pltpu.make_async_copy(held, out.at[slice(*bounds), :], here)
+        copy.start()
+        copy.wait()
+
+    inputs = list(parts) + ([] if so_far is None else [so_far])
+    return order.call(
+        body,
+        [jax.ShapeDtypeStruct((slab, width), jnp.bfloat16)],
+        [pltpu.VMEM((rows, width), jnp.bfloat16), pltpu.SemaphoreType.DMA(())],
+        inputs,
+        [pltpu.VMEM] * len(parts) + [pl.ANY] * (len(inputs) - len(parts)),
+        "final_rows",
+        [pl.ANY],
+        {} if so_far is None else {len(parts): 0},
+    )[0]
+
+
+def streamed(weight_ref, place, steps, buffer, arrived, multiply):
+    depth = buffer.shape[0]
+
+    def copy(step):
+        spot = lax.rem(step, depth)
+        return pltpu.make_async_copy(weight_ref.at[place(step)], buffer.at[spot], arrived.at[spot])
+
+    for step in range(min(depth, steps)):
+        copy(jnp.int32(step)).start()
+
+    def one(step, carry):
+        copy(step).wait()
+        multiply(step, buffer[lax.rem(step, depth)])
+
+        @pl.when(step + depth < steps)
+        def _():
+            copy(step + depth).start()
+
+        return carry
+
+    lax.fori_loop(0, steps, one, 0)
+
+
+def project(order, meta, slots, features, so_far, weight, split):
+    rows, width = features[0].shape[-2:]
+    columns = weight.shape[1]
+    steps = width // DEPTH
+    first, turns = slots[0][0] if slots else 0, len(slots) or LINE
+
+    def body(meta_ref, weight_ref, *refs):
+        if so_far is not None:
+            so_far_ref, refs = refs[0], refs[1:]
+        feature_refs, refs = refs[: len(features)], refs[len(features) :]
+        if split:
+            outs, (total, held, buffer, here, arrived) = refs[:-5], refs[-5:]
+        else:
+            (total,), (held, buffer, here, arrived) = refs[:-4], refs[-4:]
+        if so_far is not None:
+            brought = pltpu.make_async_copy(so_far_ref, total, here.at[turns])
+            brought.start()
+        if not slots:
+            for turn in range(turns):
+                pltpu.make_async_copy(feature_refs[0].at[turn], held.at[turn], here.at[turn]).start()
+        for turn, (_, choices) in enumerate(slots):
+            def start(which):
+                pltpu.make_async_copy(feature_refs[which], held.at[turn], here.at[turn]).start()
+
+            if len(choices) == 1:
+                start(choices[0])
+            else:
+                pl.when(meta_ref[4] == 0)(functools.partial(start, choices[0]))
+                pl.when(meta_ref[4] == 1)(functools.partial(start, choices[1]))
+        def place(step):
+            block = meta_ref[first + step // steps] * steps + lax.rem(step, steps) if slots else step
+            return (pl.ds(pl.multiple_of(block * DEPTH, DEPTH), DEPTH), slice(None))
+
+        def multiply(step, block):
+            turn, inner = step // steps, lax.rem(step, steps)
+
+            @pl.when(step == 0)
+            def _():
+                if so_far is None:
+                    total[...] = jnp.zeros_like(total)
+                else:
+                    brought.wait()
+
+            @pl.when(inner == 0)
+            def _():
+                source = feature_refs[0] if slots else feature_refs[0].at[0]
+                pltpu.make_async_copy(source, held.at[turn], here.at[turn]).wait()
+
+            left = held[turn, :, pl.ds(pl.multiple_of(inner * DEPTH, DEPTH), DEPTH)]
+            total[...] += jnp.dot(left, block, preferred_element_type=jnp.float32)
+
+        streamed(weight_ref, place, turns * steps, buffer, arrived, multiply)
+        if split:
+            half = columns // 2
+            mine = meta_ref[5]
+            outs[0][...] = total[:, pl.ds(pl.multiple_of(mine * half, half), half)]
+            outs[1][...] = total[:, pl.ds(pl.multiple_of((1 - mine) * half, half), half)]
+
+    whole = jax.ShapeDtypeStruct((rows, columns), jnp.float32)
+    halves = jax.ShapeDtypeStruct((rows, columns // 2), jnp.float32)
+    inputs = [meta, weight] + ([] if so_far is None else [so_far]) + list(features)
+    spaces = [pltpu.SMEM, pl.ANY] + ([] if so_far is None else [pl.ANY]) + [pl.ANY] * len(features)
+    return order.call(
+        body,
+        [halves, halves] if split else [whole],
+        ([pltpu.VMEM((rows, columns), jnp.float32)] if split else [])
+        + [
+            pltpu.VMEM((turns, rows, width), jnp.bfloat16),
+            pltpu.VMEM((BUFFERS, DEPTH, columns), jnp.bfloat16),
+            pltpu.SemaphoreType.DMA((turns + 1,)),
+            pltpu.SemaphoreType.DMA((BUFFERS,)),
+        ],
+        inputs,
+        spaces,
+        "project",
+        cost=2 * turns * width * columns,
+    )
+
+
+def attend(order, mine, arrived, bounds, cosine, sine, pairs, own_ids, ids, cut):
+    rows, width = mine.shape
+    key_count = pairs.shape[0]
+    tile = min(512, key_count)
+    spot_rows = slice(*bounds)
+    factor = math.log2(math.e) / math.sqrt(HD)
+
+    def body(
+        mine_ref, arrived_ref, cosine_ref, sine_ref, pair_ref, own_ids_ref, ids_ref, cut_ref, out_ref, bias, values
+    ):
+        values[:, :HD] = pair_ref[:, HD:]
+        values[:, HD:] = jnp.ones((key_count, HD), values.dtype)
+        own = own_ids_ref[spot_rows, :1]
+        for first in range(0, key_count, tile):
+            spot = slice(first, first + tile)
+            seen = (ids_ref[:, spot] == own) | (cut_ref[:, spot] < own)
+            bias[:, spot] = jnp.where(seen, 0.0, -jnp.inf)
+
+        def one_head(head, carry):
+            place = pl.ds(pl.multiple_of(head * HD, HD), HD)
+            raw = mine_ref[:, place] + arrived_ref[:, place]
+            turned = pltpu.roll(raw, HD // 2, 1)
+            query = (raw * cosine_ref[spot_rows, :] + turned * sine_ref[spot_rows, :]).astype(jnp.bfloat16)
+            summed = jnp.zeros((rows, values.shape[1]), jnp.float32)
+            for first in range(0, key_count, tile):
+                spot = slice(first, first + tile)
+                scores = lax.dot_general(
+                    query, pair_ref[spot, :HD], (((1,), (1,)), ((), ())), preferred_element_type=jnp.float32
+                )
+                weights = jnp.exp2(scores * factor + bias[:, spot])
+                summed += jnp.dot(weights.astype(jnp.bfloat16), values[spot, :], preferred_element_type=jnp.float32)
+            out_ref[:, place] = (summed[:, :HD] / summed[:, HD:]).astype(jnp.bfloat16)
+            return carry
+
+        lax.fori_loop(0, width // HD, one_head, 0, unroll=2)
+
+    return order.call(
+        body,
+        [jax.ShapeDtypeStruct((rows, width), jnp.bfloat16)],
+        [pltpu.VMEM((rows, key_count), jnp.float32), pltpu.VMEM((key_count, 2 * HD), jnp.bfloat16)],
+        [mine, arrived, cosine, sine, pairs, own_ids, ids, cut],
+        [pltpu.VMEM] * 8,
+        "attend",
+        cost=20_000_000,
+    )[0]
+
+
+def output_parts(order, meta, first_slot, mine, other, weight, kinds):
+    rows, width = mine.shape
+    steps = weight.shape[0] // DEPTH
+    near = steps // 2
+    columns = weight.shape[1] // LINE
+    turns = len(kinds)
+
+    def body(meta_ref, mine_ref, other_ref, weight_ref, *refs):
+        outs, (total, *rounded, near_held, far_held, buffer, arrived, gone, here) = refs[:turns], refs[turns:]
+        brought = [
+            pltpu.make_async_copy(mine_ref, near_held, here.at[0]),
+            pltpu.make_async_copy(other_ref, far_held, here.at[1]),
+        ]
+        for copy in brought:
+            copy.start()
+
+        def leave(turn):
+            return pltpu.make_async_copy(rounded[turn], outs[turn], gone.at[turn])
+
+
+        def place(step):
+            block = lax.rem(lax.rem(step, steps) + meta_ref[5] * near, steps)
+            dest = meta_ref[6 + first_slot + step // steps]
+            return (
+                pl.ds(pl.multiple_of(block * DEPTH, DEPTH), DEPTH),
+                pl.ds(pl.multiple_of(dest * columns, columns), columns),
+            )
+
+        def multiply(step, block):
+            inner = lax.rem(step, steps)
+            spot = pl.ds(pl.multiple_of(lax.rem(inner, near) * DEPTH, DEPTH), DEPTH)
+
+            @pl.when(step == 0)
+            def _():
+                for copy in brought:
+                    copy.wait()
+
+            @pl.when(inner == 0)
+            def _():
+                total[...] = jnp.dot(near_held[:, spot], block, preferred_element_type=jnp.float32)
+
+            @pl.when((inner > 0) & (inner < near))
+            def _():
+                total[...] += jnp.dot(near_held[:, spot], block, preferred_element_type=jnp.float32)
+
+            @pl.when(inner >= near)
+            def _():
+                total[...] += jnp.dot(far_held[:, spot], block, preferred_element_type=jnp.float32)
+
+            for turn in range(turns):
+                @pl.when(step == turn * steps + steps - 1)
+                def _():
+                    rounded[turn][...] = total[...].astype(rounded[turn].dtype)
+                    leave(turn).start()
+
+        streamed(weight_ref, place, turns * steps, buffer, arrived, multiply)
+        for turn in range(turns):
+            leave(turn).wait()
+
+    return order.call(
+        body,
+        [jax.ShapeDtypeStruct((rows, columns), kind) for kind in kinds],
+        [
+            pltpu.VMEM((rows, columns), jnp.float32),
+            *[pltpu.VMEM((rows, columns), kind) for kind in kinds],
+            pltpu.VMEM((rows, width), jnp.bfloat16),
+            pltpu.VMEM((rows, width), jnp.bfloat16),
+            pltpu.VMEM((BUFFERS, DEPTH, columns), jnp.bfloat16),
+            pltpu.SemaphoreType.DMA((BUFFERS,)),
+            pltpu.SemaphoreType.DMA((turns,)),
+            pltpu.SemaphoreType.DMA((2,)),
+        ],
+        [meta, mine, other, weight],
+        [pltpu.SMEM, pl.ANY, pl.ANY, pl.ANY],
+        "output_parts",
+        [pl.ANY] * turns,
+        cost=2 * turns * weight.shape[0] * columns,
+    )
+
+
+def line_shards(activations, norm_gain, query_weight, kv_weight, out_weight, block_ids, clean_mask):
+    col, row, seq = (lax.axis_index(axis) for axis in ("col", "row", "seq"))
+    slab, width = activations.shape
+    bounds = chunk_bounds(slab)
+    half = slab // 2
+    swap = ((0, 1), (1, 0))
+    at_end = (col == 0) | (col == LINE - 1)
+    meta = jnp.concatenate(
+        [
+            jnp.asarray(FEATURE_ORDER, jnp.int32)[col],
+            jnp.stack([at_end.astype(jnp.int32), row.astype(jnp.int32)]),
+            jnp.asarray(DEST_ORDER, jnp.int32)[col],
+            col[None],
+        ]
+    )
+
+    def send_far(beside, across):
+        return hop(beside, MIDDLE), hop(across, OUTER_OUT)
+
+    ids = block_ids[None, :]
+    cut = jnp.where(clean_mask == 1, block_ids, jnp.iinfo(jnp.int32).max)[None, :]
+    my_ids = lax.dynamic_slice_in_dim(block_ids, seq * slab, slab, 0)
+    my_ids = jnp.broadcast_to(my_ids[:, None], (slab, HD))
+
+    inverse = jnp.exp(jnp.arange(HD // 2, dtype=jnp.float32) * (-2.0 * math.log(rope_base) / HD))
+    positions = seq * slab + jnp.arange(slab, dtype=jnp.int32)
+    angles = positions.astype(jnp.float32)[:, None] * inverse[None, :]
+    rope_cosine = jnp.concatenate([jnp.cos(angles)] * 2, axis=1)
+    rope_sine = jnp.concatenate([-jnp.sin(angles), jnp.sin(angles)], axis=1)
+
+    order = Order()
+    gain = norm_gain[None, :]
+    first_rows = gain_rows(order, activations, gain, bounds[0][1])
+    beside, across = hop(first_rows, OUTER_IN + OUTER_OUT), hop(first_rows, MIDDLE)
+
+    around = [[(i, (i + offset) % LINE) for i in range(LINE)] for offset in range(1, LINE)]
+    kept, given, gained = key_value_terms(order, meta, activations, gain, kv_weight, bounds[1:])
+    gained = [first_rows] + gained
+    given = hop(given, swap, "row")
+    beside, across, my_ids, cut, rope_cosine, rope_sine = order.arrive(
+        beside, across, my_ids, cut, rope_cosine, rope_sine
+    )
+    far = send_far(beside, across)
+    own, *shares = key_value_shares(order, meta, kept, given)
+    shares = [own] + [hop(share, pairs) for share, pairs in zip(shares, around)]
+    pairs, cosine, sine = key_value_rows(order, meta, shares, rope_cosine, rope_sine)
+    pairs = lax.all_gather(pairs, ("seq", "row"), axis=0, tiled=True)
+    far_middle, far_end = order.arrive(*far)
+    farthest = hop(far_middle, OUTER_OUT)
+
+    out, waiting = None, None
+    for i in range(len(bounds)):
+        more = i + 1 < len(bounds)
+        (so_far,) = project(
+            order,
+            meta,
+            ((0, (0,)), (1, (1,)), (2, (2, 3))),
+            (gained[i], beside, across, far_end),
+            None,
+            query_weight,
+            False,
+        )
+        if more:
+            farthest, gained[i + 1] = order.arrive(farthest, gained[i + 1])
+            beside, across = hop(gained[i + 1], OUTER_IN + OUTER_OUT), hop(gained[i + 1], MIDDLE)
+        mine, other = project(order, meta, ((3, (0, 1)),), (far_middle, farthest), so_far, query_weight, True)
+        other = hop(other, swap, "row")
+        if waiting is not None:
+            fourth, outer, middle = last_sums(order, meta, *waiting)
+            waiting = (fourth, hop(outer, OUTER_IN + OUTER_OUT), hop(middle, MIDDLE))
+        attended = attend(order, mine, other, bounds[i], cosine, sine, pairs, my_ids, ids, cut)
+        other_attended = hop(attended, swap, "row")
+        if more:
+            beside, across = order.arrive(beside, across)
+            far_middle, far_end = send_far(beside, across)
+        first, second = output_parts(
+            order, meta, 0, attended, other_attended, out_weight, (jnp.bfloat16, jnp.bfloat16)
+        )
+        inward, inward_next = hop(first, OUTER_IN), hop(second, OUTER_IN)
+        third, fourth = output_parts(
+            order, meta, 2, attended, other_attended, out_weight, (jnp.bfloat16, jnp.float32)
+        )
+        if waiting is not None:
+            out = final_rows(order, out, slab, bounds[i - 1], waiting)
+        if more:
+            far_middle, far_end = order.arrive(far_middle, far_end)
+            farthest = hop(far_middle, OUTER_OUT)
+        (middle,) = order.add([(second, inward)], [jnp.bfloat16])
+        waiting = (first, third, fourth, hop(middle, MIDDLE), inward_next)
+    fourth, outer, middle = last_sums(order, meta, *waiting)
+    outer, middle = hop(outer, OUTER_IN + OUTER_OUT), hop(middle, MIDDLE)
+    return final_rows(order, out, slab, bounds[-1], (fourth, outer, middle))
+
+
 def solution(mesh):
     placed = (
         P("seq", ("row", "col")),
@@ -103,6 +701,11 @@
         P(),
         P(),
     )
+    on_line = mesh.shape["col"] == LINE == KVH and mesh.shape["row"] == 2
     return jax.shard_map(
-        shards, mesh=mesh, in_specs=placed, out_specs=P("seq", ("row", "col")), check_vma=False
-    )
+        line_shards if on_line else gathered_shards,
+        mesh=mesh,
+        in_specs=placed,
+        out_specs=P("seq", ("row", "col")),
+        check_vma=False,
+    )

time: 595 us -> 312 us (0.52)
  waiting for transfers between devices: 429 us -> 90 us
  Pallas kernels: 0 us -> 135 us
  matrix products: 86.6 us -> 0 us
  starting transfers between devices: 0.17 us -> 62.5 us
  blocking collectives: 35.2 us -> 0 us
  other arithmetic: 14.1 us -> 1.21 us
    reduce_scatter x2 -> x0, waiting for transfers between devices: 278 us -> none  [the longest x1 278 us: shards(): lax.psum_scatter(partial_out, 'col', scatter_dimension=1, tiled=True)]
    all_gather x2 -> x1, waiting for transfers between devices: 151 us -> 0.01 us  [line_shards(): pairs = lax.all_gather(pairs, ('seq', 'row'), axis=0, tiled=True)]
    pallas_call x0 -> x36, Pallas kernels: none -> 135 us  [call(): pl.pallas_call(kernel, out_shape=list(outs) + [jax.ShapeDtypeStruct((8, H...]
    ppermute x0 -> x40, waiting for transfers between devices: none -> 90 us  [hop(): return lax.ppermute(values, axis, list(pairs))]
    dot_general x5 -> x0, matrix products: 86.6 us -> none  [the longest x1 24.8 us: shards(): jnp.einsum('td,dhe->hte', panel_rows, columns, preferred_element_type=jnp...]
    ppermute x0 -> x40, starting transfers between devices: none -> 62.5 us  [hop(): return lax.ppermute(values, axis, list(pairs))]
    all_gather x2 -> x0, blocking collectives: 20.6 us -> none  [the longest x1 10.4 us: shards(): value_piece = lax.all_gather(value_rows, 'seq', axis=0, tiled=True)]
    psum x1 -> x0, blocking collectives: 14.6 us -> none  [shards(): squares = lax.psum(jnp.sum(wide_input * wide_input, axis=1), ('row', 'col'))]
  transfers between devices with their start and end apart: 5 -> 41, of which waited for: 3 -> 21; matrix products, arithmetic and copies ran while one was open for 6% -> 1% of each run, Pallas kernels for 0% -> 42%
where the time goes in v2:
time: 312 us; the launch traced here: 311 us
  Pallas kernels  135 us (43%)
  waiting for transfers between devices  90 us (29%)
  starting transfers between devices  62.5 us (20%)
  between operations  14.2 us (5%)
  local copies, waits for them, and re-layouts  8.34 us (3%)
    pallas_call x36, Pallas kernels, call(): pl.pallas_call(kernel, out_shape=list(outs) + [jax.ShapeDtypeStruct((8, H...  135 us
    ppermute x40, waiting for transfers between devices, hop(): return lax.ppermute(values, axis, list(pairs))  90 us
    ppermute x40, starting transfers between devices, hop(): return lax.ppermute(values, axis, list(pairs))  62.5 us
    unnamed x26, local copies, waits for them, and re-layouts  7.36 us
  transfers between devices with their start and end apart: 41, of which 21 were waited for; matrix products, arithmetic and copies ran while one was open for 1% of the time, Pallas kernels for 42%

profile of v2, /device:TPU:8, one launch (start us, length us, event | category | flops | bytes accessed | tf_op | source)
XLA Modules:
  0.0 310.9 jit_solution(17794425889857100508)
XLA Ops:
  6.5 1.6 copy-done.2
  10.0 5.0 %collective-permute-start.1 = (bf16[192,2048]{1,0:T(8,128)(2,1)}, bf16[192,2048]{1,0:T(8,128)(2,1)}, u32[]{:S(2)}, u32[]{:S(2)}) collective-permute-start(bf16[192,2048]{1,0:T(8,128)(2,1)} %get-tuple-element.108.refs_2_), channel_id=1, source_target_pairs={{1,2},{2,1},{5,6},{6,5},{9,10},{10,9},{13,14},{14,13},{17,18},{18,... | collective-permute-start | bytes 2359304 | tf_op jit(solution)/shard_map/ppermute | solution.py:113
  15.9 7.6 %key_value_terms.1 = (f32[272,1024]{1,0:T(8,128)S(1)}, f32[272,1024]{1,0:T(8,128)}, bf16[192,2048]{1,0:T(8,128)(2,1)S(1)}, bf16[128,2048]{1,0:T(8,128)(2,1)S(1)}, f32[8,128]{1,0:T(8,128)S(1)}) custom-call(s32[11]{0:T(128)S(1)} %concatenate.9.refs_0_, bf16[512,2048]{1,0:T(8,128)(2,1)S(1)} %copy-done.3, f32[1,2048]{1,0:T(1,128)S(1)} %bitcast.15, ...), custom_call_target="tpu_custom_call" | custom-call | bytes 15000000 | tf_op jit(solution)/shard_map/key_value_terms/pallas_call | solution.py:134
  26.6 3.0 collective-permute-done.refs_0_
  29.6 3.0 collective-permute-done.1.refs_1_
  32.8 3.6 %collective-permute-start.2 = (bf16[192,2048]{1,0:T(8,128)(2,1)}, bf16[192,2048]{1,0:T(8,128)(2,1)S(1)}, u32[]{:S(2)}, u32[]{:S(2)}) collective-permute-start(bf16[192,2048]{1,0:T(8,128)(2,1)} %get-tuple-element.111.refs_3_), channel_id=1, source_target_pairs={{1,2},{2,1},{5,6},{6,5},{9,10},{10,9},{13,14},{14,13},{17,18},{18,... | collective-permute-start | bytes 2359304 | tf_op jit(solution)/shard_map/ppermute | solution.py:113
  39.7 1.7 collective-permute-start.7
  41.4 21.2 %collective-permute-done.5.refs_2_ = bf16[272,256]{1,0:T(8,128)(2,1)S(1)} collective-permute-done((bf16[272,256]{1,0:T(8,128)(2,1)S(1)}, bf16[272,256]{1,0:T(8,128)(2,1)S(1)}, u32[]{:S(2)}, u32[]{:S(2)}) %collective-permute-start.5) | collective-permute-done | bytes 139296 | tf_op jit(solution)/shard_map/ppermute | solution.py:113
  67.5 11.7 %project.6 = (f32[192,2048]{1,0:T(8,128)S(1)}, f32[8,128]{1,0:T(8,128)S(1)}) custom-call(s32[11]{0:T(128)S(1)} %concatenate.9.refs_0_, bf16[8192,2048]{1,0:T(8,128)(2,1)} %refs_1_.13, bf16[192,2048]{1,0:T(8,128)(2,1)} %get-tuple-element.108.refs_2_, bf16[192,2048]{1,0:T(8,128)(2,1)} %get-tuple-element.111.refs_3_, ...), custom_call_target="tpu_custom_call" | custom-call | bytes 25165824 | tf_op jit(solution)/shard_map/project/pallas_call | solution.py:134
  79.2 5.3 %collective-permute-done.8.refs_0_ = bf16[192,2048]{1,0:T(8,128)(2,1)S(1)} collective-permute-done((bf16[192,2048]{1,0:T(8,128)(2,1)S(1)}, bf16[192,2048]{1,0:T(8,128)(2,1)S(1)}, u32[]{:S(2)}, u32[]{:S(2)}) %collective-permute-start.8) | collective-permute-done | bytes 786464 | tf_op jit(solution)/shard_map/ppermute | solution.py:113
  84.6 6.2 %project.7 = (f32[192,1024]{1,0:T(8,128)S(1)}, f32[192,1024]{1,0:T(8,128)}, f32[8,128]{1,0:T(8,128)S(1)}) custom-call(s32[11]{0:T(128)S(1)} %concatenate.9.refs_0_, bf16[8192,2048]{1,0:T(8,128)(2,1)} %refs_1_.13, f32[192,2048]{1,0:T(8,128)S(1)} %get-tuple-element.130.refs_2_, bf16[192,2048]{1,0:T(8,128)(2,1)S(1)} %get-tuple-element.124.refs_3_, ...), custom_call_target="tpu_custom_call" | custom-call | bytes 8388608 | tf_op jit(solution)/shard_map/project/pallas_call | solution.py:134
  91.7 3.2 %collective-permute-start.10 = (bf16[192,2048]{1,0:T(8,128)(2,1)S(1)}, bf16[192,2048]{1,0:T(8,128)(2,1)S(1)}, u32[]{:S(2)}, u32[]{:S(2)}) collective-permute-start(bf16[192,2048]{1,0:T(8,128)(2,1)S(1)} %get-tuple-element.129.refs_2_), channel_id=1, source_target_pairs={{1,2},{2,1},{5,6},{6,5},{9,10},{10,9},{13,14},{14,13},{17,18},{18,... | collective-permute-start | bytes 2359304 | tf_op jit(solution)/shard_map/ppermute | solution.py:113
  97.4 6.6 %attend.3 = (bf16[192,1024]{1,0:T(8,128)(2,1)S(1)}, f32[8,128]{1,0:T(8,128)S(1)}) custom-call(f32[192,1024]{1,0:T(8,128)S(1)} %copy-done.9, f32[192,1024]{1,0:T(8,128)} %collective-permute-done.11.refs_1_, f32[512,128]{1,0:T(8,128)S(1)} %get-tuple-element.135.refs_2_, f32[512,128]{1,0:T(8,128)S(1)} %get-tuple-element.136.refs_3_, ...), custom_call_target="tpu_custom_call" | custom-call | bytes 20000000 | tf_op jit(solution)/shard_map/attend/pallas_call | solution.py:134
  103.9 9.6 %collective-permute-done.10.refs_1_ = bf16[192,2048]{1,0:T(8,128)(2,1)S(1)} collective-permute-done((bf16[192,2048]{1,0:T(8,128)(2,1)S(1)}, bf16[192,2048]{1,0:T(8,128)(2,1)S(1)}, u32[]{:S(2)}, u32[]{:S(2)}) %collective-permute-start.10) | collective-permute-done | bytes 786464 | tf_op jit(solution)/shard_map/ppermute | solution.py:113
  114.6 2.7 collective-permute-start.12
  118.7 1.7 collective-permute-done.14.refs_2_
  120.4 9.0 %output_parts.6 = (bf16[192,2048]{1,0:T(8,128)(2,1)S(1)}, bf16[192,2048]{1,0:T(8,128)(2,1)S(1)}, f32[8,128]{1,0:T(8,128)S(1)}) custom-call(s32[11]{0:T(128)S(1)} %concatenate.9.refs_0_, bf16[192,1024]{1,0:T(8,128)(2,1)S(1)} %get-tuple-element.144.refs_1_, bf16[192,1024]{1,0:T(8,128)(2,1)S(1)} %collective-permute-done.14.refs_2_, ...), custom_call_target="tpu_custom_call" | custom-call | bytes 16777216 | tf_op jit(solution)/shard_map/output_parts/pallas_call | solution.py:134
  130.9 9.1 %output_parts.7 = (bf16[192,2048]{1,0:T(8,128)(2,1)S(1)}, f32[192,2048]{1,0:T(8,128)S(1)}, f32[8,128]{1,0:T(8,128)S(1)}) custom-call(s32[11]{0:T(128)S(1)} %concatenate.9.refs_0_, bf16[192,1024]{1,0:T(8,128)(2,1)S(1)} %get-tuple-element.144.refs_1_, bf16[192,1024]{1,0:T(8,128)(2,1)S(1)} %collective-permute-done.14.refs_2_, bf16[2048,8192]{1,0:T(8,128)(2,1)} %refs_3_.13, ...), custom_call_target="tpu_custom_call" | custom-call | bytes 16777216 | tf_op jit(solution)/shard_map/output_parts/pallas_call | solution.py:134
  140.0 4.6 %collective-permute-start.15 = (bf16[192,2048]{1,0:T(8,128)(2,1)S(1)}, bf16[192,2048]{1,0:T(8,128)(2,1)S(1)}, u32[]{:S(2)}, u32[]{:S(2)}) collective-permute-start(bf16[192,2048]{1,0:T(8,128)(2,1)S(1)} %get-tuple-element.148.refs_3_), channel_id=1, source_target_pairs={{2,3},{1,0},{6,7},{5,4},{10,11},{9,8},{14,15},{13,12},{18,19},{17,... | collective-permute-start | bytes 2359304 | tf_op jit(solution)/shard_map/ppermute | solution.py:113
  146.0 5.7 %collective-permute-done.16.refs_1_ = bf16[192,2048]{1,0:T(8,128)(2,1)S(1)} collective-permute-done((bf16[192,2048]{1,0:T(8,128)(2,1)S(1)}, bf16[192,2048]{1,0:T(8,128)(2,1)S(1)}, u32[]{:S(2)}, u32[]{:S(2)}) %collective-permute-start.16) | collective-permute-done | bytes 786464 | tf_op jit(solution)/shard_map/ppermute | solution.py:113
  151.9 3.2 %collective-permute-start.20 = (bf16[192,2048]{1,0:T(8,128)(2,1)S(1)}, bf16[192,2048]{1,0:T(8,128)(2,1)S(1)}, u32[]{:S(2)}, u32[]{:S(2)}) collective-permute-start(bf16[192,2048]{1,0:T(8,128)(2,1)S(1)} %get-tuple-element.163), channel_id=1, source_target_pairs={{1,2},{2,1},{5,6},{6,5},{9,10},{10,9},{13,14},{14,13},{17,18},{18,... | collective-permute-start | bytes 2359304 | tf_op jit(solution)/shard_map/ppermute | solution.py:113
  155.1 11.1 %project.8 = (f32[192,2048]{1,0:T(8,128)S(1)}, f32[8,128]{1,0:T(8,128)S(1)}) custom-call(s32[11]{0:T(128)S(1)} %concatenate.9.refs_0_, bf16[8192,2048]{1,0:T(8,128)(2,1)} %refs_1_.13, bf16[192,2048]{1,0:T(8,128)(2,1)S(1)} %get-tuple-element.129.refs_2_, bf16[192,2048]{1,0:T(8,128)(2,1)S(1)} %get-tuple-element.142.refs_3_, ...), custom_call_target="tpu_custom_call" | custom-call | bytes 25165824 | tf_op jit(solution)/shard_map/project/pallas_call | solution.py:134
  166.2 5.3 %project.9 = (f32[192,1024]{1,0:T(8,128)S(1)}, f32[192,1024]{1,0:T(8,128)S(1)}, f32[8,128]{1,0:T(8,128)S(1)}) custom-call(s32[11]{0:T(128)S(1)} %concatenate.9.refs_0_, bf16[8192,2048]{1,0:T(8,128)(2,1)} %refs_1_.13, f32[192,2048]{1,0:T(8,128)S(1)} %get-tuple-element.157.refs_2_, bf16[192,2048]{1,0:T(8,128)(2,1)S(1)} %get-tuple-element.148.refs_3_, ...), custom_call_target="tpu_custom_call" | custom-call | bytes 8388608 | tf_op jit(solution)/shard_map/project/pallas_call | solution.py:134
  171.7 2.8 collective-permute-start.18
  175.5 5.4 %attend.4 = (bf16[192,1024]{1,0:T(8,128)(2,1)S(1)}, f32[8,128]{1,0:T(8,128)S(1)}) custom-call(f32[192,1024]{1,0:T(8,128)S(1)} %get-tuple-element.160.refs_0_, f32[192,1024]{1,0:T(8,128)S(1)} %collective-permute-done.19.refs_1_, f32[512,128]{1,0:T(8,128)S(1)} %get-tuple-element.135.refs_2_, f32[512,128]{1,0:T(8,128)S(1)} %get-tuple-element.136.refs_3_, ...), custom_call_target="tpu_custom_call" | custom-call | bytes 20000000 | tf_op jit(solution)/shard_map/attend/pallas_call | solution.py:134
  181.1 3.2 %collective-permute-start.25 = (bf16[192,2048]{1,0:T(8,128)(2,1)S(1)}, bf16[192,2048]{1,0:T(8,128)(2,1)S(1)}, u32[]{:S(2)}, u32[]{:S(2)}) collective-permute-start(bf16[192,2048]{1,0:T(8,128)(2,1)S(1)} %get-tuple-element.171), channel_id=1, source_target_pairs={{1,2},{2,1},{5,6},{6,5},{9,10},{10,9},{13,14},{14,13},{17,18},{18,... | collective-permute-start | bytes 2359304 | tf_op jit(solution)/shard_map/ppermute | solution.py:113
  184.3 2.2 collective-permute-done.17.refs_0_
  186.4 2.1 collective-permute-done.18.refs_1_
  188.5 9.0 %output_parts.8 = (bf16[192,2048]{1,0:T(8,128)(2,1)S(1)}, bf16[192,2048]{1,0:T(8,128)(2,1)S(1)}, f32[8,128]{1,0:T(8,128)S(1)}) custom-call(s32[11]{0:T(128)S(1)} %concatenate.9.refs_0_, bf16[192,1024]{1,0:T(8,128)(2,1)S(1)} %get-tuple-element.172.refs_1_, bf16[192,1024]{1,0:T(8,128)(2,1)S(1)} %collective-permute-done.26.refs_2_, ...), custom_call_target="tpu_custom_call" | custom-call | bytes 16777216 | tf_op jit(solution)/shard_map/output_parts/pallas_call | solution.py:134
  198.8 2.7 collective-permute-start.22
  201.5 2.6 collective-permute-start.23
  204.1 9.1 %output_parts.9 = (bf16[192,2048]{1,0:T(8,128)(2,1)S(1)}, f32[192,2048]{1,0:T(8,128)S(1)}, f32[8,128]{1,0:T(8,128)S(1)}) custom-call(s32[11]{0:T(128)S(1)} %concatenate.9.refs_0_, bf16[192,1024]{1,0:T(8,128)(2,1)S(1)} %get-tuple-element.172.refs_1_, bf16[192,1024]{1,0:T(8,128)(2,1)S(1)} %collective-permute-done.26.refs_2_, bf16[2048,8192]{1,0:T(8,128)(2,1)} %refs_3_.13, ...), custom_call_target="tpu_custom_call" | custom-call | bytes 16777216 | tf_op jit(solution)/shard_map/output_parts/pallas_call | solution.py:134
  216.0 2.4 collective-permute-start.28
  219.9 2.7 collective-permute-start.30
  222.6 10.0 %project.10 = (f32[128,2048]{1,0:T(8,128)S(1)}, f32[8,128]{1,0:T(8,128)S(1)}) custom-call(s32[11]{0:T(128)S(1)} %concatenate.9.refs_0_, bf16[8192,2048]{1,0:T(8,128)(2,1)} %refs_1_.13, bf16[128,2048]{1,0:T(8,128)(2,1)S(1)} %get-tuple-element.156.refs_2_, bf16[128,2048]{1,0:T(8,128)(2,1)S(1)} %get-tuple-element.167.refs_3_, ...), custom_call_target="tpu_custom_call" | custom-call | bytes 25165824 | tf_op jit(solution)/shard_map/project/pallas_call | solution.py:134
  232.6 4.8 %project.11 = (f32[128,1024]{1,0:T(8,128)S(1)}, f32[128,1024]{1,0:T(8,128)S(1)}, f32[8,128]{1,0:T(8,128)S(1)}) custom-call(s32[11]{0:T(128)S(1)} %concatenate.9.refs_0_, bf16[8192,2048]{1,0:T(8,128)(2,1)} %refs_1_.13, f32[128,2048]{1,0:T(8,128)S(1)} %get-tuple-element.182.refs_2_, bf16[128,2048]{1,0:T(8,128)(2,1)S(1)} %get-tuple-element.183.refs_3_, ...), custom_call_target="tpu_custom_call" | custom-call | bytes 8388608 | tf_op jit(solution)/shard_map/project/pallas_call | solution.py:134
  238.1 2.8 collective-permute-done.30.refs_3_
  241.9 2.7 collective-permute-start.35
  244.6 4.1 %attend.5 = (bf16[128,1024]{1,0:T(8,128)(2,1)S(1)}, f32[8,128]{1,0:T(8,128)S(1)}) custom-call(f32[128,1024]{1,0:T(8,128)S(1)} %get-tuple-element.185.refs_0_, f32[128,1024]{1,0:T(8,128)S(1)} %collective-permute-done.29.refs_1_, f32[512,128]{1,0:T(8,128)S(1)} %get-tuple-element.135.refs_2_, f32[512,128]{1,0:T(8,128)S(1)} %get-tuple-element.136.refs_3_, ...), custom_call_target="tpu_custom_call" | custom-call | bytes 20000000 | tf_op jit(solution)/shard_map/attend/pallas_call | solution.py:134
  250.3 7.5 %output_parts.10 = (bf16[128,2048]{1,0:T(8,128)(2,1)S(1)}, bf16[128,2048]{1,0:T(8,128)(2,1)S(1)}, f32[8,128]{1,0:T(8,128)S(1)}) custom-call(s32[11]{0:T(128)S(1)} %concatenate.9.refs_0_, bf16[128,1024]{1,0:T(8,128)(2,1)S(1)} %get-tuple-element.191.refs_1_, bf16[128,1024]{1,0:T(8,128)(2,1)S(1)} %collective-permute-done.32.refs_2_, ...), custom_call_target="tpu_custom_call" | custom-call | bytes 16777216 | tf_op jit(solution)/shard_map/output_parts/pallas_call | solution.py:134
  260.5 7.6 %output_parts.11 = (bf16[128,2048]{1,0:T(8,128)(2,1)S(1)}, f32[128,2048]{1,0:T(8,128)S(1)}, f32[8,128]{1,0:T(8,128)S(1)}) custom-call(s32[11]{0:T(128)S(1)} %concatenate.9.refs_0_, bf16[128,1024]{1,0:T(8,128)(2,1)S(1)} %get-tuple-element.191.refs_1_, bf16[128,1024]{1,0:T(8,128)(2,1)S(1)} %collective-permute-done.32.refs_2_, bf16[2048,8192]{1,0:T(8,128)(2,1)} %refs_3_.13, ...), custom_call_target="tpu_custom_call" | custom-call | bytes 16777216 | tf_op jit(solution)/shard_map/output_parts/pallas_call | solution.py:134
  269.2 5.3 %collective-permute-done.33.refs_1_ = bf16[128,2048]{1,0:T(8,128)(2,1)S(1)} collective-permute-done((bf16[128,2048]{1,0:T(8,128)(2,1)S(1)}, bf16[128,2048]{1,0:T(8,128)(2,1)S(1)}, u32[]{:S(2)}, u32[]{:S(2)}) %collective-permute-start.33) | collective-permute-done | bytes 524320 | tf_op jit(solution)/shard_map/ppermute | solution.py:113
  274.6 3.2 %collective-permute-start.36 = (bf16[128,2048]{1,0:T(8,128)(2,1)S(1)}, bf16[128,2048]{1,0:T(8,128)(2,1)S(1)}, u32[]{:S(2)}, u32[]{:S(2)}) collective-permute-start(bf16[128,2048]{1,0:T(8,128)(2,1)S(1)} %get-tuple-element.204), channel_id=1, source_target_pairs={{1,2},{2,1},{5,6},{6,5},{9,10},{10,9},{13,14},{14,13},{17,18},{18,... | collective-permute-start | bytes 1572872 | tf_op jit(solution)/shard_map/ppermute | solution.py:113
  277.8 7.1 %collective-permute-done.37.refs_4_ = bf16[128,2048]{1,0:T(8,128)(2,1)S(1)} collective-permute-done((bf16[128,2048]{1,0:T(8,128)(2,1)S(1)}, bf16[128,2048]{1,0:T(8,128)(2,1)S(1)}, u32[]{:S(2)}, u32[]{:S(2)}) %collective-permute-start.37) | collective-permute-done | bytes 524320 | tf_op jit(solution)/shard_map/ppermute | solution.py:113
  285.0 3.9 %collective-permute-done.36.refs_3_ = bf16[128,2048]{1,0:T(8,128)(2,1)S(1)} collective-permute-done((bf16[128,2048]{1,0:T(8,128)(2,1)S(1)}, bf16[128,2048]{1,0:T(8,128)(2,1)S(1)}, u32[]{:S(2)}, u32[]{:S(2)}) %collective-permute-start.36) | collective-permute-done | bytes 524320 | tf_op jit(solution)/shard_map/ppermute | solution.py:113
  289.8 3.1 %collective-permute-start.39 = (bf16[128,2048]{1,0:T(8,128)(2,1)S(1)}, bf16[128,2048]{1,0:T(8,128)(2,1)S(1)}, u32[]{:S(2)}, u32[]{:S(2)}) collective-permute-start(bf16[128,2048]{1,0:T(8,128)(2,1)S(1)} %get-tuple-element.207), channel_id=1, source_target_pairs={{1,2},{2,1},{5,6},{6,5},{9,10},{10,9},{13,14},{14,13},{17,18},{18,... | collective-permute-start | bytes 1572872 | tf_op jit(solution)/shard_map/ppermute | solution.py:113
  292.9 8.3 %collective-permute-done.38.refs_1_ = bf16[128,2048]{1,0:T(8,128)(2,1)S(1)} collective-permute-done((bf16[128,2048]{1,0:T(8,128)(2,1)S(1)}, bf16[128,2048]{1,0:T(8,128)(2,1)S(1)}, u32[]{:S(2)}, u32[]{:S(2)}) %collective-permute-start.38) | collective-permute-done | bytes 524320 | tf_op jit(solution)/shard_map/ppermute | solution.py:113
  301.2 1.9 collective-permute-done.39.refs_2_
  (106 shorter events, 38.4 us)
Async XLA Ops:
  6.5 88.5 %all-gather.2.cloned.1.call-start = ((), (), s32[]{:S(2)}) async-start(), calls=%async_computation | async-start | bytes 1179648 | tf_op jit(solution)/shard_map/all_gather | solution.py:646
  6.5 1.6 copy-start.2
  8.8 7.0 %copy-start.3 = (bf16[512,2048]{1,0:T(8,128)(2,1)S(1)}, bf16[512,2048]{1,0:T(8,128)(2,1)}, u32[]{:S(2)}) copy-start(bf16[512,2048]{1,0:T(8,128)(2,1)} %refs_1_.7) | copy-start | bytes 6291460
  9.9 19.7 %collective-permute-start = (bf16[192,2048]{1,0:T(8,128)(2,1)}, bf16[192,2048]{1,0:T(8,128)(2,1)}, u32[]{:S(2)}, u32[]{:S(2)}) collective-permute-start(bf16[192,2048]{1,0:T(8,128)(2,1)} %get-tuple-element.108.refs_2_), channel_id=1, source_target_pairs={{0,1},{3,2},{2,3},{1,0},{4,5},{7,6},{6,7},{5,4},{8,9},{11,10},{10,... | collective-permute-start | bytes 2359304 | tf_op jit(solution)/shard_map/ppermute | solution.py:113
  10.0 22.6 %collective-permute-start.1 = (bf16[192,2048]{1,0:T(8,128)(2,1)}, bf16[192,2048]{1,0:T(8,128)(2,1)}, u32[]{:S(2)}, u32[]{:S(2)}) collective-permute-start(bf16[192,2048]{1,0:T(8,128)(2,1)} %get-tuple-element.108.refs_2_), channel_id=1, source_target_pairs={{1,2},{2,1},{5,6},{6,5},{9,10},{10,9},{13,14},{14,13},{17,18},{18,... | collective-permute-start | bytes 2359304 | tf_op jit(solution)/shard_map/ppermute | solution.py:113
  15.9 9.4 %copy-start.10 = (s32[2048]{0:T(1024)S(1)}, s32[2048]{0:T(1024)}, u32[]{:S(2)}) copy-start(s32[2048]{0:T(1024)} %param.14) | copy-start | bytes 24580
  25.3 1.3 copy-start.12
  25.3 12.5 %collective-permute-start.4 = (f32[272,1024]{1,0:T(8,128)}, f32[272,1024]{1,0:T(8,128)}, u32[]{:S(2)}, u32[]{:S(2)}) collective-permute-start(f32[272,1024]{1,0:T(8,128)} %get-tuple-element.114), channel_id=1, source_target_pairs={{0,4},{4,0},{1,5},{5,1},{2,6},{6,2},{3,7},{7,3},{8,12},{12,8},{9,1... | collective-permute-start | bytes 3342344 | tf_op jit(solution)/shard_map/ppermute | solution.py:113
  26.4 11.4 %copy-start.7 = (f32[272,1024]{1,0:T(8,128)S(1)}, f32[272,1024]{1,0:T(8,128)}, u32[]{:S(2)}) copy-start(f32[272,1024]{1,0:T(8,128)} %copy-done.6) | copy-start | bytes 3342340
  32.8 33.4 %collective-permute-start.2 = (bf16[192,2048]{1,0:T(8,128)(2,1)}, bf16[192,2048]{1,0:T(8,128)(2,1)S(1)}, u32[]{:S(2)}, u32[]{:S(2)}) collective-permute-start(bf16[192,2048]{1,0:T(8,128)(2,1)} %get-tuple-element.111.refs_3_), channel_id=1, source_target_pairs={{1,2},{2,1},{5,6},{6,5},{9,10},{10,9},{13,14},{14,13},{17,18},{18,... | collective-permute-start | bytes 2359304 | tf_op jit(solution)/shard_map/ppermute | solution.py:113
  36.4 29.8 %collective-permute-start.3 = (bf16[192,2048]{1,0:T(8,128)(2,1)}, bf16[192,2048]{1,0:T(8,128)(2,1)S(1)}, u32[]{:S(2)}, u32[]{:S(2)}) collective-permute-start(bf16[192,2048]{1,0:T(8,128)(2,1)} %get-tuple-element.112.refs_4_), channel_id=1, source_target_pairs={{2,3},{1,0},{6,7},{5,4},{10,11},{9,8},{14,15},{13,12},{18,19},{17,... | collective-permute-start | bytes 2359304 | tf_op jit(solution)/shard_map/ppermute | solution.py:113
  39.3 23.3 %collective-permute-start.5 = (bf16[272,256]{1,0:T(8,128)(2,1)S(1)}, bf16[272,256]{1,0:T(8,128)(2,1)S(1)}, u32[]{:S(2)}, u32[]{:S(2)}) collective-permute-start(bf16[272,256]{1,0:T(8,128)(2,1)S(1)} %get-tuple-element.117), channel_id=1, source_target_pairs={{0,1},{1,2},{2,3},{3,0},{4,5},{5,6},{6,7},{7,4},{8,9},{9,10},{10,1... | collective-permute-start | bytes 417800 | tf_op jit(solution)/shard_map/ppermute | solution.py:113
  39.7 24.5 %collective-permute-start.6 = (bf16[272,256]{1,0:T(8,128)(2,1)S(1)}, bf16[272,256]{1,0:T(8,128)(2,1)S(1)}, u32[]{:S(2)}, u32[]{:S(2)}) collective-permute-start(bf16[272,256]{1,0:T(8,128)(2,1)S(1)} %get-tuple-element.118), channel_id=1, source_target_pairs={{0,2},{1,3},{2,0},{3,1},{4,6},{5,7},{6,4},{7,5},{8,10},{9,11},{10,... | collective-permute-start | bytes 417800 | tf_op jit(solution)/shard_map/ppermute | solution.py:113
  39.7 25.0 %collective-permute-start.7 = (bf16[272,256]{1,0:T(8,128)(2,1)S(1)}, bf16[272,256]{1,0:T(8,128)(2,1)S(1)}, u32[]{:S(2)}, u32[]{:S(2)}) collective-permute-start(bf16[272,256]{1,0:T(8,128)(2,1)S(1)} %get-tuple-element.119), channel_id=1, source_target_pairs={{0,3},{1,0},{2,1},{3,2},{4,7},{5,4},{6,5},{7,6},{8,11},{9,8},{10,9... | collective-permute-start | bytes 417800 | tf_op jit(solution)/shard_map/ppermute | solution.py:113
  66.2 18.4 %collective-permute-start.8 = (bf16[192,2048]{1,0:T(8,128)(2,1)S(1)}, bf16[192,2048]{1,0:T(8,128)(2,1)S(1)}, u32[]{:S(2)}, u32[]{:S(2)}) collective-permute-start(bf16[192,2048]{1,0:T(8,128)(2,1)S(1)} %get-tuple-element.124.refs_3_), channel_id=1, source_target_pairs={{2,3},{1,0},{6,7},{5,4},{10,11},{9,8},{14,15},{13,12},{18,19},{17,... | collective-permute-start | bytes 2359304 | tf_op jit(solution)/shard_map/ppermute | solution.py:113
  91.7 3.3 %collective-permute-start.11 = (f32[192,1024]{1,0:T(8,128)}, f32[192,1024]{1,0:T(8,128)}, u32[]{:S(2)}, u32[]{:S(2)}) collective-permute-start(f32[192,1024]{1,0:T(8,128)} %get-tuple-element.134), channel_id=1, source_target_pairs={{0,4},{4,0},{1,5},{5,1},{2,6},{6,2},{3,7},{7,3},{8,12},{12,8},{9,1... | collective-permute-start | bytes 2359304 | tf_op jit(solution)/shard_map/ppermute | solution.py:113
  91.7 21.8 %collective-permute-start.10 = (bf16[192,2048]{1,0:T(8,128)(2,1)S(1)}, bf16[192,2048]{1,0:T(8,128)(2,1)S(1)}, u32[]{:S(2)}, u32[]{:S(2)}) collective-permute-start(bf16[192,2048]{1,0:T(8,128)(2,1)S(1)} %get-tuple-element.129.refs_2_), channel_id=1, source_target_pairs={{1,2},{2,1},{5,6},{6,5},{9,10},{10,9},{13,14},{14,13},{17,18},{18,... | collective-permute-start | bytes 2359304 | tf_op jit(solution)/shard_map/ppermute | solution.py:113
  94.9 19.7 %collective-permute-start.9 = (bf16[192,2048]{1,0:T(8,128)(2,1)S(1)}, bf16[192,2048]{1,0:T(8,128)(2,1)S(1)}, u32[]{:S(2)}, u32[]{:S(2)}) collective-permute-start(bf16[192,2048]{1,0:T(8,128)(2,1)S(1)} %get-tuple-element.129.refs_2_), channel_id=1, source_target_pairs={{0,1},{3,2},{2,3},{1,0},{4,5},{7,6},{6,7},{5,4},{8,9},{11,10},{10,... | collective-permute-start | bytes 2359304 | tf_op jit(solution)/shard_map/ppermute | solution.py:113
  114.6 25.4 %collective-permute-start.12 = (bf16[192,2048]{1,0:T(8,128)(2,1)S(1)}, bf16[192,2048]{1,0:T(8,128)(2,1)S(1)}, u32[]{:S(2)}, u32[]{:S(2)}) collective-permute-start(bf16[192,2048]{1,0:T(8,128)(2,1)S(1)} %get-tuple-element.142.refs_3_), channel_id=1, source_target_pairs={{1,2},{2,1},{5,6},{6,5},{9,10},{10,9},{13,14},{14,13},{17,18},{18,... | collective-permute-start | bytes 2359304 | tf_op jit(solution)/shard_map/ppermute | solution.py:113
  117.3 22.7 %collective-permute-start.13 = (bf16[192,2048]{1,0:T(8,128)(2,1)S(1)}, bf16[192,2048]{1,0:T(8,128)(2,1)S(1)}, u32[]{:S(2)}, u32[]{:S(2)}) collective-permute-start(bf16[192,2048]{1,0:T(8,128)(2,1)S(1)} %get-tuple-element.143.refs_4_), channel_id=1, source_target_pairs={{2,3},{1,0},{6,7},{5,4},{10,11},{9,8},{14,15},{13,12},{18,19},{17,... | collective-permute-start | bytes 2359304 | tf_op jit(solution)/shard_map/ppermute | solution.py:113
  118.6 1.8 collective-permute-start.14
  129.4 22.3 %collective-permute-start.16 = (bf16[192,2048]{1,0:T(8,128)(2,1)S(1)}, bf16[192,2048]{1,0:T(8,128)(2,1)S(1)}, u32[]{:S(2)}, u32[]{:S(2)}) collective-permute-start(bf16[192,2048]{1,0:T(8,128)(2,1)S(1)} %get-tuple-element.152.refs_1_), channel_id=1, source_target_pairs={{0,1},{3,2},{4,5},{7,6},{8,9},{11,10},{12,13},{15,14},{16,17},{19,... | collective-permute-start | bytes 2359304 | tf_op jit(solution)/shard_map/ppermute | solution.py:113
  140.0 26.2 %collective-permute-start.15 = (bf16[192,2048]{1,0:T(8,128)(2,1)S(1)}, bf16[192,2048]{1,0:T(8,128)(2,1)S(1)}, u32[]{:S(2)}, u32[]{:S(2)}) collective-permute-start(bf16[192,2048]{1,0:T(8,128)(2,1)S(1)} %get-tuple-element.148.refs_3_), channel_id=1, source_target_pairs={{2,3},{1,0},{6,7},{5,4},{10,11},{9,8},{14,15},{13,12},{18,19},{17,... | collective-permute-start | bytes 2359304 | tf_op jit(solution)/shard_map/ppermute | solution.py:113
  144.7 29.9 %collective-permute-start.21 = (bf16[192,2048]{1,0:T(8,128)(2,1)S(1)}, bf16[192,2048]{1,0:T(8,128)(2,1)S(1)}, u32[]{:S(2)}, u32[]{:S(2)}) collective-permute-start(bf16[192,2048]{1,0:T(8,128)(2,1)S(1)} %get-tuple-element.151.refs_0_), channel_id=1, source_target_pairs={{0,1},{3,2},{4,5},{7,6},{8,9},{11,10},{12,13},{15,14},{16,17},{19,... | collective-permute-start | bytes 2359304 | tf_op jit(solution)/shard_map/ppermute | solution.py:113
  151.9 22.6 %collective-permute-start.20 = (bf16[192,2048]{1,0:T(8,128)(2,1)S(1)}, bf16[192,2048]{1,0:T(8,128)(2,1)S(1)}, u32[]{:S(2)}, u32[]{:S(2)}) collective-permute-start(bf16[192,2048]{1,0:T(8,128)(2,1)S(1)} %get-tuple-element.163), channel_id=1, source_target_pairs={{1,2},{2,1},{5,6},{6,5},{9,10},{10,9},{13,14},{14,13},{17,18},{18,... | collective-permute-start | bytes 2359304 | tf_op jit(solution)/shard_map/ppermute | solution.py:113
  155.1 11.1 %copy-start.5 = (bf16[128,2048]{1,0:T(8,128)(2,1)S(1)}, bf16[128,2048]{1,0:T(8,128)(2,1)}, u32[]{:S(2)}) copy-start(bf16[128,2048]{1,0:T(8,128)(2,1)} %copy-done.4) | copy-start | bytes 1572868
  171.6 3.9 %copy-start.1 = (bf16[2048,256]{1,0:T(8,128)(2,1)S(1)}, bf16[2048,256]{1,0:T(8,128)(2,1)}, u32[]{:S(2)}) copy-start(bf16[2048,256]{1,0:T(8,128)(2,1)} %all-gather.2.cloned.1.call-done.refs_4_) | copy-start | bytes 3145732
  171.6 3.9 %collective-permute-start.19 = (f32[192,1024]{1,0:T(8,128)S(1)}, f32[192,1024]{1,0:T(8,128)S(1)}, u32[]{:S(2)}, u32[]{:S(2)}) collective-permute-start(f32[192,1024]{1,0:T(8,128)S(1)} %get-tuple-element.161), channel_id=1, source_target_pairs={{0,4},{4,0},{1,5},{5,1},{2,6},{6,2},{3,7},{7,3},{8,12},{12,8},{9,1... | collective-permute-start | bytes 2359304 | tf_op jit(solution)/shard_map/ppermute | solution.py:113
  171.7 14.8 %collective-permute-start.17 = (bf16[128,2048]{1,0:T(8,128)(2,1)S(1)}, bf16[128,2048]{1,0:T(8,128)(2,1)S(1)}, u32[]{:S(2)}, u32[]{:S(2)}) collective-permute-start(bf16[128,2048]{1,0:T(8,128)(2,1)S(1)} %get-tuple-element.156.refs_2_), channel_id=1, source_target_pairs={{0,1},{3,2},{2,3},{1,0},{4,5},{7,6},{6,7},{5,4},{8,9},{11,10},{10,... | collective-permute-start | bytes 1572872 | tf_op jit(solution)/shard_map/ppermute | solution.py:113
  171.7 16.8 %collective-permute-start.18 = (bf16[128,2048]{1,0:T(8,128)(2,1)S(1)}, bf16[128,2048]{1,0:T(8,128)(2,1)S(1)}, u32[]{:S(2)}, u32[]{:S(2)}) collective-permute-start(bf16[128,2048]{1,0:T(8,128)(2,1)S(1)} %get-tuple-element.156.refs_2_), channel_id=1, source_target_pairs={{1,2},{2,1},{5,6},{6,5},{9,10},{10,9},{13,14},{14,13},{17,18},{18,... | collective-permute-start | bytes 1572872 | tf_op jit(solution)/shard_map/ppermute | solution.py:113
  180.9 7.6 %collective-permute-start.26 = (bf16[192,1024]{1,0:T(8,128)(2,1)S(1)}, bf16[192,1024]{1,0:T(8,128)(2,1)S(1)}, u32[]{:S(2)}, u32[]{:S(2)}) collective-permute-start(bf16[192,1024]{1,0:T(8,128)(2,1)S(1)} %get-tuple-element.172.refs_1_), channel_id=1, source_target_pairs={{0,4},{4,0},{1,5},{5,1},{2,6},{6,2},{3,7},{7,3},{8,12},{12,8},{9,1... | collective-permute-start | bytes 1179656 | tf_op jit(solution)/shard_map/ppermute | solution.py:113
  181.0 32.2 %collective-permute-start.24 = (bf16[192,2048]{1,0:T(8,128)(2,1)S(1)}, bf16[192,2048]{1,0:T(8,128)(2,1)S(1)}, u32[]{:S(2)}, u32[]{:S(2)}) collective-permute-start(bf16[192,2048]{1,0:T(8,128)(2,1)S(1)} %get-tuple-element.170), channel_id=1, source_target_pairs={{0,1},{3,2},{2,3},{1,0},{4,5},{7,6},{6,7},{5,4},{8,9},{11,10},{10,... | collective-permute-start | bytes 2359304 | tf_op jit(solution)/shard_map/ppermute | solution.py:113
  181.1 32.1 %collective-permute-start.25 = (bf16[192,2048]{1,0:T(8,128)(2,1)S(1)}, bf16[192,2048]{1,0:T(8,128)(2,1)S(1)}, u32[]{:S(2)}, u32[]{:S(2)}) collective-permute-start(bf16[192,2048]{1,0:T(8,128)(2,1)S(1)} %get-tuple-element.171), channel_id=1, source_target_pairs={{1,2},{2,1},{5,6},{6,5},{9,10},{10,9},{13,14},{14,13},{17,18},{18,... | collective-permute-start | bytes 2359304 | tf_op jit(solution)/shard_map/ppermute | solution.py:113
  197.5 22.2 %collective-permute-start.27 = (bf16[192,2048]{1,0:T(8,128)(2,1)S(1)}, bf16[192,2048]{1,0:T(8,128)(2,1)S(1)}, u32[]{:S(2)}, u32[]{:S(2)}) collective-permute-start(bf16[192,2048]{1,0:T(8,128)(2,1)S(1)} %get-tuple-element.179.refs_1_), channel_id=1, source_target_pairs={{0,1},{3,2},{4,5},{7,6},{8,9},{11,10},{12,13},{15,14},{16,17},{19,... | collective-permute-start | bytes 2359304 | tf_op jit(solution)/shard_map/ppermute | solution.py:113
  198.8 17.1 %collective-permute-start.22 = (bf16[128,2048]{1,0:T(8,128)(2,1)S(1)}, bf16[128,2048]{1,0:T(8,128)(2,1)S(1)}, u32[]{:S(2)}, u32[]{:S(2)}) collective-permute-start(bf16[128,2048]{1,0:T(8,128)(2,1)S(1)} %get-tuple-element.167.refs_3_), channel_id=1, source_target_pairs={{1,2},{2,1},{5,6},{6,5},{9,10},{10,9},{13,14},{14,13},{17,18},{18,... | collective-permute-start | bytes 1572872 | tf_op jit(solution)/shard_map/ppermute | solution.py:113
  201.5 14.5 %collective-permute-start.23 = (bf16[128,2048]{1,0:T(8,128)(2,1)S(1)}, bf16[128,2048]{1,0:T(8,128)(2,1)S(1)}, u32[]{:S(2)}, u32[]{:S(2)}) collective-permute-start(bf16[128,2048]{1,0:T(8,128)(2,1)S(1)} %get-tuple-element.168.refs_4_), channel_id=1, source_target_pairs={{2,3},{1,0},{6,7},{5,4},{10,11},{9,8},{14,15},{13,12},{18,19},{17,... | collective-permute-start | bytes 1572872 | tf_op jit(solution)/shard_map/ppermute | solution.py:113
  216.0 16.6 %collective-permute-start.28 = (bf16[128,2048]{1,0:T(8,128)(2,1)S(1)}, bf16[128,2048]{1,0:T(8,128)(2,1)S(1)}, u32[]{:S(2)}, u32[]{:S(2)}) collective-permute-start(bf16[128,2048]{1,0:T(8,128)(2,1)S(1)} %get-tuple-element.183.refs_3_), channel_id=1, source_target_pairs={{2,3},{1,0},{6,7},{5,4},{10,11},{9,8},{14,15},{13,12},{18,19},{17,... | collective-permute-start | bytes 1572872 | tf_op jit(solution)/shard_map/ppermute | solution.py:113
  218.4 19.7 %collective-permute-start.31 = (bf16[192,2048]{1,0:T(8,128)(2,1)S(1)}, bf16[192,2048]{1,0:T(8,128)(2,1)S(1)}, u32[]{:S(2)}, u32[]{:S(2)}) collective-permute-start(bf16[192,2048]{1,0:T(8,128)(2,1)S(1)} %get-tuple-element.178.refs_0_), channel_id=1, source_target_pairs={{0,1},{3,2},{4,5},{7,6},{8,9},{11,10},{12,13},{15,14},{16,17},{19,... | collective-permute-start | bytes 2359304 | tf_op jit(solution)/shard_map/ppermute | solution.py:113
  219.9 21.0 %collective-permute-start.30 = (bf16[192,2048]{1,0:T(8,128)(2,1)S(1)}, bf16[192,2048]{1,0:T(8,128)(2,1)S(1)}, u32[]{:S(2)}, u32[]{:S(2)}) collective-permute-start(bf16[192,2048]{1,0:T(8,128)(2,1)S(1)} %get-tuple-element.188), channel_id=1, source_target_pairs={{1,2},{2,1},{5,6},{6,5},{9,10},{10,9},{13,14},{14,13},{17,18},{18,... | collective-permute-start | bytes 2359304 | tf_op jit(solution)/shard_map/ppermute | solution.py:113
  237.4 7.1 %collective-permute-start.29 = (f32[128,1024]{1,0:T(8,128)S(1)}, f32[128,1024]{1,0:T(8,128)S(1)}, u32[]{:S(2)}, u32[]{:S(2)}) collective-permute-start(f32[128,1024]{1,0:T(8,128)S(1)} %get-tuple-element.186), channel_id=1, source_target_pairs={{0,4},{4,0},{1,5},{5,1},{2,6},{6,2},{3,7},{7,3},{8,12},{12,8},{9,1... | collective-permute-start | bytes 1572872 | tf_op jit(solution)/shard_map/ppermute | solution.py:113
  241.8 26.2 %collective-permute-start.34 = (bf16[192,2048]{1,0:T(8,128)(2,1)S(1)}, bf16[192,2048]{1,0:T(8,128)(2,1)S(1)}, u32[]{:S(2)}, u32[]{:S(2)}) collective-permute-start(bf16[192,2048]{1,0:T(8,128)(2,1)S(1)} %get-tuple-element.199), channel_id=1, source_target_pairs={{0,1},{3,2},{2,3},{1,0},{4,5},{7,6},{6,7},{5,4},{8,9},{11,10},{10,... | collective-permute-start | bytes 2359304 | tf_op jit(solution)/shard_map/ppermute | solution.py:113
  241.9 26.2 %collective-permute-start.35 = (bf16[192,2048]{1,0:T(8,128)(2,1)S(1)}, bf16[192,2048]{1,0:T(8,128)(2,1)S(1)}, u32[]{:S(2)}, u32[]{:S(2)}) collective-permute-start(bf16[192,2048]{1,0:T(8,128)(2,1)S(1)} %get-tuple-element.200), channel_id=1, source_target_pairs={{1,2},{2,1},{5,6},{6,5},{9,10},{10,9},{13,14},{14,13},{17,18},{18,... | collective-permute-start | bytes 2359304 | tf_op jit(solution)/shard_map/ppermute | solution.py:113
  248.7 1.6 collective-permute-start.32
  257.9 16.7 %collective-permute-start.33 = (bf16[128,2048]{1,0:T(8,128)(2,1)S(1)}, bf16[128,2048]{1,0:T(8,128)(2,1)S(1)}, u32[]{:S(2)}, u32[]{:S(2)}) collective-permute-start(bf16[128,2048]{1,0:T(8,128)(2,1)S(1)} %get-tuple-element.195.refs_1_), channel_id=1, source_target_pairs={{0,1},{3,2},{4,5},{7,6},{8,9},{11,10},{12,13},{15,14},{16,17},{19,... | collective-permute-start | bytes 1572872 | tf_op jit(solution)/shard_map/ppermute | solution.py:113
  259.2 25.8 %collective-permute-start.37 = (bf16[128,2048]{1,0:T(8,128)(2,1)S(1)}, bf16[128,2048]{1,0:T(8,128)(2,1)S(1)}, u32[]{:S(2)}, u32[]{:S(2)}) collective-permute-start(bf16[128,2048]{1,0:T(8,128)(2,1)S(1)} %get-tuple-element.197.refs_0_), channel_id=1, source_target_pairs={{0,1},{3,2},{4,5},{7,6},{8,9},{11,10},{12,13},{15,14},{16,17},{19,... | collective-permute-start | bytes 1572872 | tf_op jit(solution)/shard_map/ppermute | solution.py:113
  274.6 14.2 %collective-permute-start.36 = (bf16[128,2048]{1,0:T(8,128)(2,1)S(1)}, bf16[128,2048]{1,0:T(8,128)(2,1)S(1)}, u32[]{:S(2)}, u32[]{:S(2)}) collective-permute-start(bf16[128,2048]{1,0:T(8,128)(2,1)S(1)} %get-tuple-element.204), channel_id=1, source_target_pairs={{1,2},{2,1},{5,6},{6,5},{9,10},{10,9},{13,14},{14,13},{17,18},{18,... | collective-permute-start | bytes 1572872 | tf_op jit(solution)/shard_map/ppermute | solution.py:113
  289.7 11.5 %collective-permute-start.38 = (bf16[128,2048]{1,0:T(8,128)(2,1)S(1)}, bf16[128,2048]{1,0:T(8,128)(2,1)S(1)}, u32[]{:S(2)}, u32[]{:S(2)}) collective-permute-start(bf16[128,2048]{1,0:T(8,128)(2,1)S(1)} %get-tuple-element.206), channel_id=1, source_target_pairs={{0,1},{3,2},{2,3},{1,0},{4,5},{7,6},{6,7},{5,4},{8,9},{11,10},{10,... | collective-permute-start | bytes 1572872 | tf_op jit(solution)/shard_map/ppermute | solution.py:113
  289.8 13.3 %collective-permute-start.39 = (bf16[128,2048]{1,0:T(8,128)(2,1)S(1)}, bf16[128,2048]{1,0:T(8,128)(2,1)S(1)}, u32[]{:S(2)}, u32[]{:S(2)}) collective-permute-start(bf16[128,2048]{1,0:T(8,128)(2,1)S(1)} %get-tuple-element.207), channel_id=1, source_target_pairs={{1,2},{2,1},{5,6},{6,5},{9,10},{10,9},{13,14},{14,13},{17,18},{18,... | collective-permute-start | bytes 1572872 | tf_op jit(solution)/shard_map/ppermute | solution.py:113
  (6 other events, 5.8 us)
Sparse Core Ops, SparseCore 0:
  66.3 24.8 all-gather.1

commit v3 on v2

--- a/solution.py
+++ b/solution.py
@@ -392,10 +392,10 @@
 
 
 def project(order, meta, slots, features, so_far, weight, split):
-    rows, width = features[0].shape[-2:]
+    rows, width = features[0].shape
     columns = weight.shape[1]
-    steps = width // DEPTH
-    first, turns = slots[0][0] if slots else 0, len(slots) or LINE
+    steps = columns // DEPTH
+    first, turns = slots[0][0], len(slots)
 
     def body(meta_ref, weight_ref, *refs):
         if so_far is not None:
@@ -408,9 +408,6 @@
         if so_far is not None:
             brought = pltpu.make_async_copy(so_far_ref, total, here.at[turns])
             brought.start()
-        if not slots:
-            for turn in range(turns):
-                pltpu.make_async_copy(feature_refs[0].at[turn], held.at[turn], here.at[turn]).start()
         for turn, (_, choices) in enumerate(slots):
             def start(which):
                 pltpu.make_async_copy(feature_refs[which], held.at[turn], here.at[turn]).start()
@@ -421,26 +418,34 @@
                 pl.when(meta_ref[4] == 0)(functools.partial(start, choices[0]))
                 pl.when(meta_ref[4] == 1)(functools.partial(start, choices[1]))
         def place(step):
-            block = meta_ref[first + step // steps] * steps + lax.rem(step, steps) if slots else step
-            return (pl.ds(pl.multiple_of(block * DEPTH, DEPTH), DEPTH), slice(None))
+            rows_of = meta_ref[first + step // steps]
+            return (
+                pl.ds(pl.multiple_of(rows_of * width, width), width),
+                pl.ds(pl.multiple_of(lax.rem(step, steps) * DEPTH, DEPTH), DEPTH),
+            )
 
         def multiply(step, block):
             turn, inner = step // steps, lax.rem(step, steps)
-
-            @pl.when(step == 0)
-            def _():
-                if so_far is None:
-                    total[...] = jnp.zeros_like(total)
-                else:
-                    brought.wait()
+            spot = pl.ds(pl.multiple_of(inner * DEPTH, DEPTH), DEPTH)
+
+            if so_far is not None:
+                pl.when(step == 0)(brought.wait)
 
             @pl.when(inner == 0)
             def _():
-                source = feature_refs[0] if slots else feature_refs[0].at[0]
-                pltpu.make_async_copy(source, held.at[turn], here.at[turn]).wait()
-
-            left = held[turn, :, pl.ds(pl.multiple_of(inner * DEPTH, DEPTH), DEPTH)]
-            total[...] += jnp.dot(left, block, preferred_element_type=jnp.float32)
+                pltpu.make_async_copy(feature_refs[0], held.at[turn], here.at[turn]).wait()
+
+            part = jnp.dot(held[turn], block, preferred_element_type=jnp.float32)
+            if so_far is not None:
+                total[:, spot] += part
+            else:
+                @pl.when(turn == 0)
+                def _():
+                    total[:, spot] = part
+
+                @pl.when(turn > 0)
+                def _():
+                    total[:, spot] += part
 
         streamed(weight_ref, place, turns * steps, buffer, arrived, multiply)
         if split:
@@ -459,7 +464,7 @@
         ([pltpu.VMEM((rows, columns), jnp.float32)] if split else [])
         + [
             pltpu.VMEM((turns, rows, width), jnp.bfloat16),
-            pltpu.VMEM((BUFFERS, DEPTH, columns), jnp.bfloat16),
+            pltpu.VMEM((BUFFERS, width, DEPTH), jnp.bfloat16),
             pltpu.SemaphoreType.DMA((turns + 1,)),
             pltpu.SemaphoreType.DMA((BUFFERS,)),
         ],
@@ -519,16 +524,17 @@
 
 def output_parts(order, meta, first_slot, mine, other, weight, kinds):
     rows, width = mine.shape
-    steps = weight.shape[0] // DEPTH
-    near = steps // 2
+    depth = weight.shape[0]
     columns = weight.shape[1] // LINE
+    steps = columns // DEPTH
     turns = len(kinds)
 
     def body(meta_ref, mine_ref, other_ref, weight_ref, *refs):
-        outs, (total, *rounded, near_held, far_held, buffer, arrived, gone, here) = refs[:turns], refs[turns:]
+        outs, (*rounded, held, buffer, arrived, gone, here) = refs[:turns], refs[turns:]
+        core = meta_ref[5]
         brought = [
-            pltpu.make_async_copy(mine_ref, near_held, here.at[0]),
-            pltpu.make_async_copy(other_ref, far_held, here.at[1]),
+            pltpu.make_async_copy(source, held.at[:, pl.ds(pl.multiple_of(which * width, width), width)], here.at[i])
+            for i, (source, which) in enumerate(((mine_ref, core), (other_ref, 1 - core)))
         ]
         for copy in brought:
             copy.start()
@@ -536,41 +542,26 @@
         def leave(turn):
             return pltpu.make_async_copy(rounded[turn], outs[turn], gone.at[turn])
 
-
         def place(step):
-            block = lax.rem(lax.rem(step, steps) + meta_ref[5] * near, steps)
             dest = meta_ref[6 + first_slot + step // steps]
-            return (
-                pl.ds(pl.multiple_of(block * DEPTH, DEPTH), DEPTH),
-                pl.ds(pl.multiple_of(dest * columns, columns), columns),
-            )
+            spot = dest * columns + lax.rem(step, steps) * DEPTH
+            return (slice(None), pl.ds(pl.multiple_of(spot, DEPTH), DEPTH))
 
         def multiply(step, block):
             inner = lax.rem(step, steps)
-            spot = pl.ds(pl.multiple_of(lax.rem(inner, near) * DEPTH, DEPTH), DEPTH)
 
             @pl.when(step == 0)
             def _():
                 for copy in brought:
                     copy.wait()
 
-            @pl.when(inner == 0)
-            def _():
-                total[...] = jnp.dot(near_held[:, spot], block, preferred_element_type=jnp.float32)
-
-            @pl.when((inner > 0) & (inner < near))
-            def _():
-                total[...] += jnp.dot(near_held[:, spot], block, preferred_element_type=jnp.float32)
-
-            @pl.when(inner >= near)
-            def _():
-                total[...] += jnp.dot(far_held[:, spot], block, preferred_element_type=jnp.float32)
-
+            part = jnp.dot(held[...], block, preferred_element_type=jnp.float32)
             for turn in range(turns):
-                @pl.when(step == turn * steps + steps - 1)
+                @pl.when(step // steps == turn)
                 def _():
-                    rounded[turn][...] = total[...].astype(rounded[turn].dtype)
-                    leave(turn).start()
+                    spot = pl.ds(pl.multiple_of(inner * DEPTH, DEPTH), DEPTH)
+                    rounded[turn][:, spot] = part.astype(rounded[turn].dtype)
+                    pl.when(inner == steps - 1)(leave(turn).start)
 
         streamed(weight_ref, place, turns * steps, buffer, arrived, multiply)
         for turn in range(turns):
@@ -580,11 +571,9 @@
         body,
         [jax.ShapeDtypeStruct((rows, columns), kind) for kind in kinds],
         [
-            pltpu.VMEM((rows, columns), jnp.float32),
             *[pltpu.VMEM((rows, columns), kind) for kind in kinds],
-            pltpu.VMEM((rows, width), jnp.bfloat16),
-            pltpu.VMEM((rows, width), jnp.bfloat16),
-            pltpu.VMEM((BUFFERS, DEPTH, columns), jnp.bfloat16),
+            pltpu.VMEM((rows, depth), jnp.bfloat16),
+            pltpu.VMEM((BUFFERS, depth, DEPTH), jnp.bfloat16),
             pltpu.SemaphoreType.DMA((BUFFERS,)),
             pltpu.SemaphoreType.DMA((turns,)),
             pltpu.SemaphoreType.DMA((2,)),
@@ -593,7 +582,7 @@
         [pltpu.SMEM, pl.ANY, pl.ANY, pl.ANY],
         "output_parts",
         [pl.ANY] * turns,
-        cost=2 * turns * weight.shape[0] * columns,
+        cost=2 * turns * depth * columns,
     )
 
 
@@ -669,16 +658,20 @@
             waiting = (fourth, hop(outer, OUTER_IN + OUTER_OUT), hop(middle, MIDDLE))
         attended = attend(order, mine, other, bounds[i], cosine, sine, pairs, my_ids, ids, cut)
         other_attended = hop(attended, swap, "row")
+        spread_out = lambda slot, *kinds: output_parts(
+            order, meta, slot, attended, other_attended, out_weight, kinds
+        )
         if more:
+            first, second = spread_out(0, jnp.bfloat16, jnp.bfloat16)
+            inward, inward_next = hop(first, OUTER_IN), hop(second, OUTER_IN)
             beside, across = order.arrive(beside, across)
             far_middle, far_end = send_far(beside, across)
-        first, second = output_parts(
-            order, meta, 0, attended, other_attended, out_weight, (jnp.bfloat16, jnp.bfloat16)
-        )
-        inward, inward_next = hop(first, OUTER_IN), hop(second, OUTER_IN)
-        third, fourth = output_parts(
-            order, meta, 2, attended, other_attended, out_weight, (jnp.bfloat16, jnp.float32)
-        )
+            third, fourth = spread_out(2, jnp.bfloat16, jnp.float32)
+        else:
+            (first,) = spread_out(0, jnp.bfloat16)
+            inward = hop(first, OUTER_IN)
+            second, third, fourth = spread_out(1, jnp.bfloat16, jnp.bfloat16, jnp.float32)
+            inward_next = hop(second, OUTER_IN)
         if waiting is not None:
             out = final_rows(order, out, slab, bounds[i - 1], waiting)
         if more:

time: 312 us -> 302 us (0.968)
  waiting for transfers between devices: 90 us -> 80 us
    ppermute x40, waiting for transfers between devices: 90 us -> 80 us  [hop(): return lax.ppermute(values, axis, list(pairs))]
    unnamed x26 -> x30, local copies, waits for them, and re-layouts: 7.36 us -> 8.06 us
  transfers between devices with their start and end apart: 41 -> 41, of which waited for: 21 -> 20; matrix products, arithmetic and copies ran while one was open for 1% -> 1% of each run, Pallas kernels for 42% -> 43%
where the time goes in v3:
time: 302 us; the launch traced here: 301 us
  Pallas kernels  133 us (44%)
  waiting for transfers between devices  80 us (26%)
  starting transfers between devices  63.6 us (21%)
  between operations  14.2 us (5%)
  local copies, waits for them, and re-layouts  9.05 us (3%)
    pallas_call x36, Pallas kernels, call(): pl.pallas_call(kernel, out_shape=list(outs) + [jax.ShapeDtypeStruct((8, H...  133 us
    ppermute x40, waiting for transfers between devices, hop(): return lax.ppermute(values, axis, list(pairs))  80 us
    ppermute x40, starting transfers between devices, hop(): return lax.ppermute(values, axis, list(pairs))  63.6 us
    unnamed x30, local copies, waits for them, and re-layouts  8.06 us
  transfers between devices with their start and end apart: 41, of which 20 were waited for; matrix products, arithmetic and copies ran while one was open for 1% of the time, Pallas kernels for 43%

profile of v3, /device:TPU:8, one launch (start us, length us, event | category | flops | bytes accessed | tf_op | source)
XLA Modules:
  0.0 300.7 jit_solution(14703280392120992423)
XLA Ops:
  6.5 1.6 copy-done.2
  10.0 5.0 %collective-permute-start.1 = (bf16[192,2048]{1,0:T(8,128)(2,1)}, bf16[192,2048]{1,0:T(8,128)(2,1)}, u32[]{:S(2)}, u32[]{:S(2)}) collective-permute-start(bf16[192,2048]{1,0:T(8,128)(2,1)} %get-tuple-element.108.refs_2_), channel_id=1, source_target_pairs={{1,2},{2,1},{5,6},{6,5},{9,10},{10,9},{13,14},{14,13},{17,18},{18,... | collective-permute-start | bytes 2359304 | tf_op jit(solution)/shard_map/ppermute | solution.py:113
  15.9 7.6 %key_value_terms.1 = (f32[272,1024]{1,0:T(8,128)S(1)}, f32[272,1024]{1,0:T(8,128)}, bf16[192,2048]{1,0:T(8,128)(2,1)S(1)}, bf16[128,2048]{1,0:T(8,128)(2,1)S(1)}, f32[8,128]{1,0:T(8,128)S(1)}) custom-call(s32[11]{0:T(128)S(1)} %concatenate.9.refs_0_, bf16[512,2048]{1,0:T(8,128)(2,1)S(1)} %copy-done.3, f32[1,2048]{1,0:T(1,128)S(1)} %bitcast.15, ...), custom_call_target="tpu_custom_call" | custom-call | bytes 15000000 | tf_op jit(solution)/shard_map/key_value_terms/pallas_call | solution.py:134
  26.7 3.0 collective-permute-done.refs_0_
  29.6 3.0 %collective-permute-done.1.refs_1_ = bf16[192,2048]{1,0:T(8,128)(2,1)} collective-permute-done((bf16[192,2048]{1,0:T(8,128)(2,1)}, bf16[192,2048]{1,0:T(8,128)(2,1)}, u32[]{:S(2)}, u32[]{:S(2)}) %collective-permute-start.1) | collective-permute-done | bytes 786464 | tf_op jit(solution)/shard_map/ppermute | solution.py:113
  32.8 3.6 %collective-permute-start.2 = (bf16[192,2048]{1,0:T(8,128)(2,1)}, bf16[192,2048]{1,0:T(8,128)(2,1)S(1)}, u32[]{:S(2)}, u32[]{:S(2)}) collective-permute-start(bf16[192,2048]{1,0:T(8,128)(2,1)} %get-tuple-element.111.refs_3_), channel_id=1, source_target_pairs={{1,2},{2,1},{5,6},{6,5},{9,10},{10,9},{13,14},{14,13},{17,18},{18,... | collective-permute-start | bytes 2359304 | tf_op jit(solution)/shard_map/ppermute | solution.py:113
  37.8 1.5 key_value_shares.1
  39.7 1.7 collective-permute-start.7
  41.4 21.2 %collective-permute-done.5.refs_2_ = bf16[272,256]{1,0:T(8,128)(2,1)S(1)} collective-permute-done((bf16[272,256]{1,0:T(8,128)(2,1)S(1)}, bf16[272,256]{1,0:T(8,128)(2,1)S(1)}, u32[]{:S(2)}, u32[]{:S(2)}) %collective-permute-start.5) | collective-permute-done | bytes 139296 | tf_op jit(solution)/shard_map/ppermute | solution.py:113
  67.6 12.0 %project.6 = (f32[192,2048]{1,0:T(8,128)S(1)}, f32[8,128]{1,0:T(8,128)S(1)}) custom-call(s32[11]{0:T(128)S(1)} %concatenate.9.refs_0_, bf16[8192,2048]{1,0:T(8,128)(2,1)} %refs_1_.13, bf16[192,2048]{1,0:T(8,128)(2,1)} %get-tuple-element.108.refs_2_, bf16[192,2048]{1,0:T(8,128)(2,1)} %get-tuple-element.111.refs_3_, ...), custom_call_target="tpu_custom_call" | custom-call | bytes 25165824 | tf_op jit(solution)/shard_map/project/pallas_call | solution.py:134
  79.6 5.0 %collective-permute-done.8.refs_0_ = bf16[192,2048]{1,0:T(8,128)(2,1)S(1)} collective-permute-done((bf16[192,2048]{1,0:T(8,128)(2,1)S(1)}, bf16[192,2048]{1,0:T(8,128)(2,1)S(1)}, u32[]{:S(2)}, u32[]{:S(2)}) %collective-permute-start.8) | collective-permute-done | bytes 786464 | tf_op jit(solution)/shard_map/ppermute | solution.py:113
  84.6 6.2 %project.7 = (f32[192,1024]{1,0:T(8,128)S(1)}, f32[192,1024]{1,0:T(8,128)}, f32[8,128]{1,0:T(8,128)S(1)}) custom-call(s32[11]{0:T(128)S(1)} %concatenate.9.refs_0_, bf16[8192,2048]{1,0:T(8,128)(2,1)} %refs_1_.13, f32[192,2048]{1,0:T(8,128)S(1)} %get-tuple-element.130.refs_2_, bf16[192,2048]{1,0:T(8,128)(2,1)S(1)} %get-tuple-element.124.refs_3_, ...), custom_call_target="tpu_custom_call" | custom-call | bytes 8388608 | tf_op jit(solution)/shard_map/project/pallas_call | solution.py:134
  91.8 3.2 %collective-permute-start.10 = (bf16[192,2048]{1,0:T(8,128)(2,1)S(1)}, bf16[192,2048]{1,0:T(8,128)(2,1)S(1)}, u32[]{:S(2)}, u32[]{:S(2)}) collective-permute-start(bf16[192,2048]{1,0:T(8,128)(2,1)S(1)} %get-tuple-element.129.refs_2_), channel_id=1, source_target_pairs={{1,2},{2,1},{5,6},{6,5},{9,10},{10,9},{13,14},{14,13},{17,18},{18,... | collective-permute-start | bytes 2359304 | tf_op jit(solution)/shard_map/ppermute | solution.py:113
  97.4 6.6 %attend.3 = (bf16[192,1024]{1,0:T(8,128)(2,1)S(1)}, f32[8,128]{1,0:T(8,128)S(1)}) custom-call(f32[192,1024]{1,0:T(8,128)S(1)} %copy-done.9, f32[192,1024]{1,0:T(8,128)} %collective-permute-done.11.refs_1_, f32[512,128]{1,0:T(8,128)S(1)} %get-tuple-element.135.refs_2_, f32[512,128]{1,0:T(8,128)S(1)} %get-tuple-element.136.refs_3_, ...), custom_call_target="tpu_custom_call" | custom-call | bytes 20000000 | tf_op jit(solution)/shard_map/attend/pallas_call | solution.py:134
  104.3 1.5 collective-permute-done.12.refs_2_
  105.8 8.4 %output_parts.6 = (bf16[192,2048]{1,0:T(8,128)(2,1)S(1)}, bf16[192,2048]{1,0:T(8,128)(2,1)S(1)}, f32[8,128]{1,0:T(8,128)S(1)}) custom-call(s32[11]{0:T(128)S(1)} %concatenate.9.refs_0_, bf16[192,1024]{1,0:T(8,128)(2,1)S(1)} %get-tuple-element.141.refs_1_, bf16[192,1024]{1,0:T(8,128)(2,1)S(1)} %collective-permute-done.12.refs_2_, ...), custom_call_target="tpu_custom_call" | custom-call | bytes 16777216 | tf_op jit(solution)/shard_map/output_parts/pallas_call | solution.py:134
  114.7 2.7 collective-permute-start.13
  120.2 8.5 %output_parts.7 = (bf16[192,2048]{1,0:T(8,128)(2,1)S(1)}, f32[192,2048]{1,0:T(8,128)S(1)}, f32[8,128]{1,0:T(8,128)S(1)}) custom-call(s32[11]{0:T(128)S(1)} %concatenate.9.refs_0_, bf16[192,1024]{1,0:T(8,128)(2,1)S(1)} %get-tuple-element.141.refs_1_, bf16[192,1024]{1,0:T(8,128)(2,1)S(1)} %collective-permute-done.12.refs_2_, bf16[2048,8192]{1,0:T(8,128)(2,1)} %refs_3_.13, ...), custom_call_target="tpu_custom_call" | custom-call | bytes 16777216 | tf_op jit(solution)/shard_map/output_parts/pallas_call | solution.py:134
  128.7 7.1 %collective-permute-done.13.refs_0_ = bf16[192,2048]{1,0:T(8,128)(2,1)S(1)} collective-permute-done((bf16[192,2048]{1,0:T(8,128)(2,1)S(1)}, bf16[192,2048]{1,0:T(8,128)(2,1)S(1)}, u32[]{:S(2)}, u32[]{:S(2)}) %collective-permute-start.13) | collective-permute-done | bytes 786464 | tf_op jit(solution)/shard_map/ppermute | solution.py:113
  136.0 4.4 %collective-permute-start.15 = (bf16[192,2048]{1,0:T(8,128)(2,1)S(1)}, bf16[192,2048]{1,0:T(8,128)(2,1)S(1)}, u32[]{:S(2)}, u32[]{:S(2)}) collective-permute-start(bf16[192,2048]{1,0:T(8,128)(2,1)S(1)} %get-tuple-element.148.refs_3_), channel_id=1, source_target_pairs={{2,3},{1,0},{6,7},{5,4},{10,11},{9,8},{14,15},{13,12},{18,19},{17,... | collective-permute-start | bytes 2359304 | tf_op jit(solution)/shard_map/ppermute | solution.py:113
  141.9 3.0 collective-permute-start.20
  144.9 11.5 %project.8 = (f32[192,2048]{1,0:T(8,128)S(1)}, f32[8,128]{1,0:T(8,128)S(1)}) custom-call(s32[11]{0:T(128)S(1)} %concatenate.9.refs_0_, bf16[8192,2048]{1,0:T(8,128)(2,1)} %refs_1_.13, bf16[192,2048]{1,0:T(8,128)(2,1)S(1)} %get-tuple-element.129.refs_2_, bf16[192,2048]{1,0:T(8,128)(2,1)S(1)} %get-tuple-element.144.refs_3_, ...), custom_call_target="tpu_custom_call" | custom-call | bytes 25165824 | tf_op jit(solution)/shard_map/project/pallas_call | solution.py:134
  156.6 5.5 %project.9 = (f32[192,1024]{1,0:T(8,128)S(1)}, f32[192,1024]{1,0:T(8,128)S(1)}, f32[8,128]{1,0:T(8,128)S(1)}) custom-call(s32[11]{0:T(128)S(1)} %concatenate.9.refs_0_, bf16[8192,2048]{1,0:T(8,128)(2,1)} %refs_1_.13, f32[192,2048]{1,0:T(8,128)S(1)} %get-tuple-element.157.refs_2_, bf16[192,2048]{1,0:T(8,128)(2,1)S(1)} %get-tuple-element.148.refs_3_, ...), custom_call_target="tpu_custom_call" | custom-call | bytes 8388608 | tf_op jit(solution)/shard_map/project/pallas_call | solution.py:134
  162.3 2.5 collective-permute-start.17
  164.8 2.9 collective-permute-start.18
  168.7 5.5 %attend.4 = (bf16[192,1024]{1,0:T(8,128)(2,1)S(1)}, f32[8,128]{1,0:T(8,128)S(1)}) custom-call(f32[192,1024]{1,0:T(8,128)S(1)} %get-tuple-element.160.refs_0_, f32[192,1024]{1,0:T(8,128)S(1)} %collective-permute-done.19.refs_1_, f32[512,128]{1,0:T(8,128)S(1)} %get-tuple-element.135.refs_2_, f32[512,128]{1,0:T(8,128)S(1)} %get-tuple-element.136.refs_3_, ...), custom_call_target="tpu_custom_call" | custom-call | bytes 20000000 | tf_op jit(solution)/shard_map/attend/pallas_call | solution.py:134
  174.3 2.9 collective-permute-start.26
  177.3 8.4 %output_parts.8 = (bf16[192,2048]{1,0:T(8,128)(2,1)S(1)}, bf16[192,2048]{1,0:T(8,128)(2,1)S(1)}, f32[8,128]{1,0:T(8,128)S(1)}) custom-call(s32[11]{0:T(128)S(1)} %concatenate.9.refs_0_, bf16[192,1024]{1,0:T(8,128)(2,1)S(1)} %get-tuple-element.166.refs_1_, bf16[192,1024]{1,0:T(8,128)(2,1)S(1)} %collective-permute-done.22.refs_2_, ...), custom_call_target="tpu_custom_call" | custom-call | bytes 16777216 | tf_op jit(solution)/shard_map/output_parts/pallas_call | solution.py:134
  187.0 2.9 collective-permute-start.23
  189.9 2.4 collective-permute-start.24
  192.3 8.5 %output_parts.9 = (bf16[192,2048]{1,0:T(8,128)(2,1)S(1)}, f32[192,2048]{1,0:T(8,128)S(1)}, f32[8,128]{1,0:T(8,128)S(1)}) custom-call(s32[11]{0:T(128)S(1)} %concatenate.9.refs_0_, bf16[192,1024]{1,0:T(8,128)(2,1)S(1)} %get-tuple-element.166.refs_1_, bf16[192,1024]{1,0:T(8,128)(2,1)S(1)} %collective-permute-done.22.refs_2_, bf16[2048,8192]{1,0:T(8,128)(2,1)} %refs_3_.13, ...), custom_call_target="tpu_custom_call" | custom-call | bytes 16777216 | tf_op jit(solution)/shard_map/output_parts/pallas_call | solution.py:134
  202.1 6.7 %collective-permute-done.23.refs_0_ = bf16[128,2048]{1,0:T(8,128)(2,1)S(1)} collective-permute-done((bf16[128,2048]{1,0:T(8,128)(2,1)S(1)}, bf16[128,2048]{1,0:T(8,128)(2,1)S(1)}, u32[]{:S(2)}, u32[]{:S(2)}) %collective-permute-start.23) | collective-permute-done | bytes 524320 | tf_op jit(solution)/shard_map/ppermute | solution.py:113
  211.6 2.9 collective-permute-start.30
  214.6 10.0 %project.10 = (f32[128,2048]{1,0:T(8,128)S(1)}, f32[8,128]{1,0:T(8,128)S(1)}) custom-call(s32[11]{0:T(128)S(1)} %concatenate.9.refs_0_, bf16[8192,2048]{1,0:T(8,128)(2,1)} %refs_1_.13, bf16[128,2048]{1,0:T(8,128)(2,1)S(1)} %get-tuple-element.156.refs_2_, bf16[128,2048]{1,0:T(8,128)(2,1)S(1)} %get-tuple-element.169.refs_3_, ...), custom_call_target="tpu_custom_call" | custom-call | bytes 25165824 | tf_op jit(solution)/shard_map/project/pallas_call | solution.py:134
  224.6 4.9 %project.11 = (f32[128,1024]{1,0:T(8,128)S(1)}, f32[128,1024]{1,0:T(8,128)S(1)}, f32[8,128]{1,0:T(8,128)S(1)}) custom-call(s32[11]{0:T(128)S(1)} %concatenate.9.refs_0_, bf16[8192,2048]{1,0:T(8,128)(2,1)} %refs_1_.13, f32[128,2048]{1,0:T(8,128)S(1)} %get-tuple-element.182.refs_2_, bf16[128,2048]{1,0:T(8,128)(2,1)S(1)} %get-tuple-element.183.refs_3_, ...), custom_call_target="tpu_custom_call" | custom-call | bytes 8388608 | tf_op jit(solution)/shard_map/project/pallas_call | solution.py:134
  230.8 1.5 collective-permute-done.30.refs_3_
  233.3 2.9 collective-permute-start.35
  236.2 4.2 %attend.5 = (bf16[128,1024]{1,0:T(8,128)(2,1)S(1)}, f32[8,128]{1,0:T(8,128)S(1)}) custom-call(f32[128,1024]{1,0:T(8,128)S(1)} %get-tuple-element.185.refs_0_, f32[128,1024]{1,0:T(8,128)S(1)} %collective-permute-done.29.refs_1_, f32[512,128]{1,0:T(8,128)S(1)} %get-tuple-element.135.refs_2_, f32[512,128]{1,0:T(8,128)S(1)} %get-tuple-element.136.refs_3_, ...), custom_call_target="tpu_custom_call" | custom-call | bytes 20000000 | tf_op jit(solution)/shard_map/attend/pallas_call | solution.py:134
  240.5 1.5 collective-permute-done.32.refs_2_
  242.1 4.8 %output_parts.10 = (bf16[128,2048]{1,0:T(8,128)(2,1)S(1)}, f32[8,128]{1,0:T(8,128)S(1)}) custom-call(s32[11]{0:T(128)S(1)} %concatenate.9.refs_0_, bf16[128,1024]{1,0:T(8,128)(2,1)S(1)} %get-tuple-element.191.refs_1_, bf16[128,1024]{1,0:T(8,128)(2,1)S(1)} %collective-permute-done.32.refs_2_, bf16[2048,8192]{1,0:T(8,128)(2,1)} %refs_3_.13, ...), custom_call_target="tpu_custom_call" | custom-call | bytes 8388608 | tf_op jit(solution)/shard_map/output_parts/pallas_call | solution.py:134
  248.2 10.1 %output_parts.11 = (bf16[128,2048]{1,0:T(8,128)(2,1)S(1)}, bf16[128,2048]{1,0:T(8,128)(2,1)S(1)}, f32[128,2048]{1,0:T(8,128)S(1)}, f32[8,128]{1,0:T(8,128)S(1)}) custom-call(s32[11]{0:T(128)S(1)} %concatenate.9.refs_0_, bf16[128,1024]{1,0:T(8,128)(2,1)S(1)} %get-tuple-element.191.refs_1_, bf16[128,1024]{1,0:T(8,128)(2,1)S(1)} %collective-permute-done.32.refs_2_, ...), custom_call_target="tpu_custom_call" | custom-call | bytes 25165824 | tf_op jit(solution)/shard_map/output_parts/pallas_call | solution.py:134
  260.7 2.0 collective-permute-done.33.refs_1_
  262.9 2.9 collective-permute-start.36
  265.8 8.4 %collective-permute-done.37.refs_4_ = bf16[128,2048]{1,0:T(8,128)(2,1)S(1)} collective-permute-done((bf16[128,2048]{1,0:T(8,128)(2,1)S(1)}, bf16[128,2048]{1,0:T(8,128)(2,1)S(1)}, u32[]{:S(2)}, u32[]{:S(2)}) %collective-permute-start.37) | collective-permute-done | bytes 524320 | tf_op jit(solution)/shard_map/ppermute | solution.py:113
  274.1 3.7 %collective-permute-done.36.refs_3_ = bf16[128,2048]{1,0:T(8,128)(2,1)S(1)} collective-permute-done((bf16[128,2048]{1,0:T(8,128)(2,1)S(1)}, bf16[128,2048]{1,0:T(8,128)(2,1)S(1)}, u32[]{:S(2)}, u32[]{:S(2)}) %collective-permute-start.36) | collective-permute-done | bytes 524320 | tf_op jit(solution)/shard_map/ppermute | solution.py:113
  278.8 2.9 collective-permute-start.39
  281.7 9.3 %collective-permute-done.38.refs_1_ = bf16[128,2048]{1,0:T(8,128)(2,1)S(1)} collective-permute-done((bf16[128,2048]{1,0:T(8,128)(2,1)S(1)}, bf16[128,2048]{1,0:T(8,128)(2,1)S(1)}, u32[]{:S(2)}, u32[]{:S(2)}) %collective-permute-start.38) | collective-permute-done | bytes 524320 | tf_op jit(solution)/shard_map/ppermute | solution.py:113
  291.0 1.9 collective-permute-done.39.refs_2_
  (110 shorter events, 35.6 us)
Async XLA Ops:
  6.5 88.5 %all-gather.2.cloned.1.call-start = ((), (), s32[]{:S(2)}) async-start(), calls=%async_computation | async-start | bytes 1179648 | tf_op jit(solution)/shard_map/all_gather | solution.py:635
  6.5 1.6 copy-start.2
  8.8 7.1 %copy-start.3 = (bf16[512,2048]{1,0:T(8,128)(2,1)S(1)}, bf16[512,2048]{1,0:T(8,128)(2,1)}, u32[]{:S(2)}) copy-start(bf16[512,2048]{1,0:T(8,128)(2,1)} %refs_1_.7) | copy-start | bytes 6291460
  8.8 7.1 %copy-start.13 = (f32[2048]{0:T(1024)S(1)}, f32[2048]{0:T(1024)}, u32[]{:S(2)}) copy-start(f32[2048]{0:T(1024)} %param.10) | copy-start | bytes 24580
  10.0 19.7 %collective-permute-start = (bf16[192,2048]{1,0:T(8,128)(2,1)}, bf16[192,2048]{1,0:T(8,128)(2,1)}, u32[]{:S(2)}, u32[]{:S(2)}) collective-permute-start(bf16[192,2048]{1,0:T(8,128)(2,1)} %get-tuple-element.108.refs_2_), channel_id=1, source_target_pairs={{0,1},{3,2},{2,3},{1,0},{4,5},{7,6},{6,7},{5,4},{8,9},{11,10},{10,... | collective-permute-start | bytes 2359304 | tf_op jit(solution)/shard_map/ppermute | solution.py:113
  10.0 22.6 %collective-permute-start.1 = (bf16[192,2048]{1,0:T(8,128)(2,1)}, bf16[192,2048]{1,0:T(8,128)(2,1)}, u32[]{:S(2)}, u32[]{:S(2)}) collective-permute-start(bf16[192,2048]{1,0:T(8,128)(2,1)} %get-tuple-element.108.refs_2_), channel_id=1, source_target_pairs={{1,2},{2,1},{5,6},{6,5},{9,10},{10,9},{13,14},{14,13},{17,18},{18,... | collective-permute-start | bytes 2359304 | tf_op jit(solution)/shard_map/ppermute | solution.py:113
  15.9 9.4 %copy-start.10 = (s32[2048]{0:T(1024)S(1)}, s32[2048]{0:T(1024)}, u32[]{:S(2)}) copy-start(s32[2048]{0:T(1024)} %param.14) | copy-start | bytes 24580
  25.3 12.5 %collective-permute-start.4 = (f32[272,1024]{1,0:T(8,128)}, f32[272,1024]{1,0:T(8,128)}, u32[]{:S(2)}, u32[]{:S(2)}) collective-permute-start(f32[272,1024]{1,0:T(8,128)} %get-tuple-element.114), channel_id=1, source_target_pairs={{0,4},{4,0},{1,5},{5,1},{2,6},{6,2},{3,7},{7,3},{8,12},{12,8},{9,1... | collective-permute-start | bytes 3342344 | tf_op jit(solution)/shard_map/ppermute | solution.py:113
  26.4 11.4 %copy-start.7 = (f32[272,1024]{1,0:T(8,128)S(1)}, f32[272,1024]{1,0:T(8,128)}, u32[]{:S(2)}) copy-start(f32[272,1024]{1,0:T(8,128)} %copy-done.6) | copy-start | bytes 3342340
  32.8 33.4 %collective-permute-start.2 = (bf16[192,2048]{1,0:T(8,128)(2,1)}, bf16[192,2048]{1,0:T(8,128)(2,1)S(1)}, u32[]{:S(2)}, u32[]{:S(2)}) collective-permute-start(bf16[192,2048]{1,0:T(8,128)(2,1)} %get-tuple-element.111.refs_3_), channel_id=1, source_target_pairs={{1,2},{2,1},{5,6},{6,5},{9,10},{10,9},{13,14},{14,13},{17,18},{18,... | collective-permute-start | bytes 2359304 | tf_op jit(solution)/shard_map/ppermute | solution.py:113
  36.4 29.8 %collective-permute-start.3 = (bf16[192,2048]{1,0:T(8,128)(2,1)}, bf16[192,2048]{1,0:T(8,128)(2,1)S(1)}, u32[]{:S(2)}, u32[]{:S(2)}) collective-permute-start(bf16[192,2048]{1,0:T(8,128)(2,1)} %get-tuple-element.112.refs_4_), channel_id=1, source_target_pairs={{2,3},{1,0},{6,7},{5,4},{10,11},{9,8},{14,15},{13,12},{18,19},{17,... | collective-permute-start | bytes 2359304 | tf_op jit(solution)/shard_map/ppermute | solution.py:113
  39.3 23.3 %collective-permute-start.5 = (bf16[272,256]{1,0:T(8,128)(2,1)S(1)}, bf16[272,256]{1,0:T(8,128)(2,1)S(1)}, u32[]{:S(2)}, u32[]{:S(2)}) collective-permute-start(bf16[272,256]{1,0:T(8,128)(2,1)S(1)} %get-tuple-element.117), channel_id=1, source_target_pairs={{0,1},{1,2},{2,3},{3,0},{4,5},{5,6},{6,7},{7,4},{8,9},{9,10},{10,1... | collective-permute-start | bytes 417800 | tf_op jit(solution)/shard_map/ppermute | solution.py:113
  39.7 24.5 %collective-permute-start.6 = (bf16[272,256]{1,0:T(8,128)(2,1)S(1)}, bf16[272,256]{1,0:T(8,128)(2,1)S(1)}, u32[]{:S(2)}, u32[]{:S(2)}) collective-permute-start(bf16[272,256]{1,0:T(8,128)(2,1)S(1)} %get-tuple-element.118), channel_id=1, source_target_pairs={{0,2},{1,3},{2,0},{3,1},{4,6},{5,7},{6,4},{7,5},{8,10},{9,11},{10,... | collective-permute-start | bytes 417800 | tf_op jit(solution)/shard_map/ppermute | solution.py:113
  39.7 25.0 %collective-permute-start.7 = (bf16[272,256]{1,0:T(8,128)(2,1)S(1)}, bf16[272,256]{1,0:T(8,128)(2,1)S(1)}, u32[]{:S(2)}, u32[]{:S(2)}) collective-permute-start(bf16[272,256]{1,0:T(8,128)(2,1)S(1)} %get-tuple-element.119), channel_id=1, source_target_pairs={{0,3},{1,0},{2,1},{3,2},{4,7},{5,4},{6,5},{7,6},{8,11},{9,8},{10,9... | collective-permute-start | bytes 417800 | tf_op jit(solution)/shard_map/ppermute | solution.py:113
  66.2 18.4 %collective-permute-start.8 = (bf16[192,2048]{1,0:T(8,128)(2,1)S(1)}, bf16[192,2048]{1,0:T(8,128)(2,1)S(1)}, u32[]{:S(2)}, u32[]{:S(2)}) collective-permute-start(bf16[192,2048]{1,0:T(8,128)(2,1)S(1)} %get-tuple-element.124.refs_3_), channel_id=1, source_target_pairs={{2,3},{1,0},{6,7},{5,4},{10,11},{9,8},{14,15},{13,12},{18,19},{17,... | collective-permute-start | bytes 2359304 | tf_op jit(solution)/shard_map/ppermute | solution.py:113
  91.8 3.3 %collective-permute-start.11 = (f32[192,1024]{1,0:T(8,128)}, f32[192,1024]{1,0:T(8,128)}, u32[]{:S(2)}, u32[]{:S(2)}) collective-permute-start(f32[192,1024]{1,0:T(8,128)} %get-tuple-element.134), channel_id=1, source_target_pairs={{0,4},{4,0},{1,5},{5,1},{2,6},{6,2},{3,7},{7,3},{8,12},{12,8},{9,1... | collective-permute-start | bytes 2359304 | tf_op jit(solution)/shard_map/ppermute | solution.py:113
  91.8 22.5 %collective-permute-start.10 = (bf16[192,2048]{1,0:T(8,128)(2,1)S(1)}, bf16[192,2048]{1,0:T(8,128)(2,1)S(1)}, u32[]{:S(2)}, u32[]{:S(2)}) collective-permute-start(bf16[192,2048]{1,0:T(8,128)(2,1)S(1)} %get-tuple-element.129.refs_2_), channel_id=1, source_target_pairs={{1,2},{2,1},{5,6},{6,5},{9,10},{10,9},{13,14},{14,13},{17,18},{18,... | collective-permute-start | bytes 2359304 | tf_op jit(solution)/shard_map/ppermute | solution.py:113
  95.0 19.7 %collective-permute-start.9 = (bf16[192,2048]{1,0:T(8,128)(2,1)S(1)}, bf16[192,2048]{1,0:T(8,128)(2,1)S(1)}, u32[]{:S(2)}, u32[]{:S(2)}) collective-permute-start(bf16[192,2048]{1,0:T(8,128)(2,1)S(1)} %get-tuple-element.129.refs_2_), channel_id=1, source_target_pairs={{0,1},{3,2},{2,3},{1,0},{4,5},{7,6},{6,7},{5,4},{8,9},{11,10},{10,... | collective-permute-start | bytes 2359304 | tf_op jit(solution)/shard_map/ppermute | solution.py:113
  104.1 1.8 collective-permute-start.12
  114.7 21.2 %collective-permute-start.13 = (bf16[192,2048]{1,0:T(8,128)(2,1)S(1)}, bf16[192,2048]{1,0:T(8,128)(2,1)S(1)}, u32[]{:S(2)}, u32[]{:S(2)}) collective-permute-start(bf16[192,2048]{1,0:T(8,128)(2,1)S(1)} %get-tuple-element.144.refs_3_), channel_id=1, source_target_pairs={{1,2},{2,1},{5,6},{6,5},{9,10},{10,9},{13,14},{14,13},{17,18},{18,... | collective-permute-start | bytes 2359304 | tf_op jit(solution)/shard_map/ppermute | solution.py:113
  117.5 18.5 %collective-permute-start.14 = (bf16[192,2048]{1,0:T(8,128)(2,1)S(1)}, bf16[192,2048]{1,0:T(8,128)(2,1)S(1)}, u32[]{:S(2)}, u32[]{:S(2)}) collective-permute-start(bf16[192,2048]{1,0:T(8,128)(2,1)S(1)} %get-tuple-element.145.refs_4_), channel_id=1, source_target_pairs={{2,3},{1,0},{6,7},{5,4},{10,11},{9,8},{14,15},{13,12},{18,19},{17,... | collective-permute-start | bytes 2359304 | tf_op jit(solution)/shard_map/ppermute | solution.py:113
  118.9 22.8 %collective-permute-start.16 = (bf16[192,2048]{1,0:T(8,128)(2,1)S(1)}, bf16[192,2048]{1,0:T(8,128)(2,1)S(1)}, u32[]{:S(2)}, u32[]{:S(2)}) collective-permute-start(bf16[192,2048]{1,0:T(8,128)(2,1)S(1)} %get-tuple-element.152.refs_1_), channel_id=1, source_target_pairs={{0,1},{3,2},{4,5},{7,6},{8,9},{11,10},{12,13},{15,14},{16,17},{19,... | collective-permute-start | bytes 2359304 | tf_op jit(solution)/shard_map/ppermute | solution.py:113
  136.0 20.7 %collective-permute-start.15 = (bf16[192,2048]{1,0:T(8,128)(2,1)S(1)}, bf16[192,2048]{1,0:T(8,128)(2,1)S(1)}, u32[]{:S(2)}, u32[]{:S(2)}) collective-permute-start(bf16[192,2048]{1,0:T(8,128)(2,1)S(1)} %get-tuple-element.148.refs_3_), channel_id=1, source_target_pairs={{2,3},{1,0},{6,7},{5,4},{10,11},{9,8},{14,15},{13,12},{18,19},{17,... | collective-permute-start | bytes 2359304 | tf_op jit(solution)/shard_map/ppermute | solution.py:113
  140.4 27.3 %collective-permute-start.21 = (bf16[192,2048]{1,0:T(8,128)(2,1)S(1)}, bf16[192,2048]{1,0:T(8,128)(2,1)S(1)}, u32[]{:S(2)}, u32[]{:S(2)}) collective-permute-start(bf16[192,2048]{1,0:T(8,128)(2,1)S(1)} %get-tuple-element.151.refs_0_), channel_id=1, source_target_pairs={{0,1},{3,2},{4,5},{7,6},{8,9},{11,10},{12,13},{15,14},{16,17},{19,... | collective-permute-start | bytes 2359304 | tf_op jit(solution)/shard_map/ppermute | solution.py:113
  141.9 25.8 %collective-permute-start.20 = (bf16[192,2048]{1,0:T(8,128)(2,1)S(1)}, bf16[192,2048]{1,0:T(8,128)(2,1)S(1)}, u32[]{:S(2)}, u32[]{:S(2)}) collective-permute-start(bf16[192,2048]{1,0:T(8,128)(2,1)S(1)} %get-tuple-element.163), channel_id=1, source_target_pairs={{1,2},{2,1},{5,6},{6,5},{9,10},{10,9},{13,14},{14,13},{17,18},{18,... | collective-permute-start | bytes 2359304 | tf_op jit(solution)/shard_map/ppermute | solution.py:113
  144.9 11.7 %copy-start.5 = (bf16[128,2048]{1,0:T(8,128)(2,1)S(1)}, bf16[128,2048]{1,0:T(8,128)(2,1)}, u32[]{:S(2)}) copy-start(bf16[128,2048]{1,0:T(8,128)(2,1)} %copy-done.4) | copy-start | bytes 1572868
  162.2 6.5 %copy-start.1 = (bf16[2048,256]{1,0:T(8,128)(2,1)S(1)}, bf16[2048,256]{1,0:T(8,128)(2,1)}, u32[]{:S(2)}) copy-start(bf16[2048,256]{1,0:T(8,128)(2,1)} %all-gather.2.cloned.1.call-done.refs_4_) | copy-start | bytes 3145732
  162.2 6.5 %collective-permute-start.19 = (f32[192,1024]{1,0:T(8,128)S(1)}, f32[192,1024]{1,0:T(8,128)S(1)}, u32[]{:S(2)}, u32[]{:S(2)}) collective-permute-start(f32[192,1024]{1,0:T(8,128)S(1)} %get-tuple-element.161), channel_id=1, source_target_pairs={{0,4},{4,0},{1,5},{5,1},{2,6},{6,2},{3,7},{7,3},{8,12},{12,8},{9,1... | collective-permute-start | bytes 2359304 | tf_op jit(solution)/shard_map/ppermute | solution.py:113
  162.3 24.7 %collective-permute-start.17 = (bf16[128,2048]{1,0:T(8,128)(2,1)S(1)}, bf16[128,2048]{1,0:T(8,128)(2,1)S(1)}, u32[]{:S(2)}, u32[]{:S(2)}) collective-permute-start(bf16[128,2048]{1,0:T(8,128)(2,1)S(1)} %get-tuple-element.156.refs_2_), channel_id=1, source_target_pairs={{0,1},{3,2},{2,3},{1,0},{4,5},{7,6},{6,7},{5,4},{8,9},{11,10},{10,... | collective-permute-start | bytes 1572872 | tf_op jit(solution)/shard_map/ppermute | solution.py:113
  164.8 22.2 %collective-permute-start.18 = (bf16[128,2048]{1,0:T(8,128)(2,1)S(1)}, bf16[128,2048]{1,0:T(8,128)(2,1)S(1)}, u32[]{:S(2)}, u32[]{:S(2)}) collective-permute-start(bf16[128,2048]{1,0:T(8,128)(2,1)S(1)} %get-tuple-element.156.refs_2_), channel_id=1, source_target_pairs={{1,2},{2,1},{5,6},{6,5},{9,10},{10,9},{13,14},{14,13},{17,18},{18,... | collective-permute-start | bytes 1572872 | tf_op jit(solution)/shard_map/ppermute | solution.py:113
  174.2 3.1 %collective-permute-start.22 = (bf16[192,1024]{1,0:T(8,128)(2,1)S(1)}, bf16[192,1024]{1,0:T(8,128)(2,1)S(1)}, u32[]{:S(2)}, u32[]{:S(2)}) collective-permute-start(bf16[192,1024]{1,0:T(8,128)(2,1)S(1)} %get-tuple-element.166.refs_1_), channel_id=1, source_target_pairs={{0,4},{4,0},{1,5},{5,1},{2,6},{6,2},{3,7},{7,3},{8,12},{12,8},{9,1... | collective-permute-start | bytes 1179656 | tf_op jit(solution)/shard_map/ppermute | solution.py:113
  174.3 26.6 %collective-permute-start.25 = (bf16[192,2048]{1,0:T(8,128)(2,1)S(1)}, bf16[192,2048]{1,0:T(8,128)(2,1)S(1)}, u32[]{:S(2)}, u32[]{:S(2)}) collective-permute-start(bf16[192,2048]{1,0:T(8,128)(2,1)S(1)} %get-tuple-element.172), channel_id=1, source_target_pairs={{0,1},{3,2},{2,3},{1,0},{4,5},{7,6},{6,7},{5,4},{8,9},{11,10},{10,... | collective-permute-start | bytes 2359304 | tf_op jit(solution)/shard_map/ppermute | solution.py:113
  174.3 26.6 %collective-permute-start.26 = (bf16[192,2048]{1,0:T(8,128)(2,1)S(1)}, bf16[192,2048]{1,0:T(8,128)(2,1)S(1)}, u32[]{:S(2)}, u32[]{:S(2)}) collective-permute-start(bf16[192,2048]{1,0:T(8,128)(2,1)S(1)} %get-tuple-element.173), channel_id=1, source_target_pairs={{1,2},{2,1},{5,6},{6,5},{9,10},{10,9},{13,14},{14,13},{17,18},{18,... | collective-permute-start | bytes 2359304 | tf_op jit(solution)/shard_map/ppermute | solution.py:113
  185.7 25.7 %collective-permute-start.27 = (bf16[192,2048]{1,0:T(8,128)(2,1)S(1)}, bf16[192,2048]{1,0:T(8,128)(2,1)S(1)}, u32[]{:S(2)}, u32[]{:S(2)}) collective-permute-start(bf16[192,2048]{1,0:T(8,128)(2,1)S(1)} %get-tuple-element.179.refs_1_), channel_id=1, source_target_pairs={{0,1},{3,2},{4,5},{7,6},{8,9},{11,10},{12,13},{15,14},{16,17},{19,... | collective-permute-start | bytes 2359304 | tf_op jit(solution)/shard_map/ppermute | solution.py:113
  187.0 21.8 %collective-permute-start.23 = (bf16[128,2048]{1,0:T(8,128)(2,1)S(1)}, bf16[128,2048]{1,0:T(8,128)(2,1)S(1)}, u32[]{:S(2)}, u32[]{:S(2)}) collective-permute-start(bf16[128,2048]{1,0:T(8,128)(2,1)S(1)} %get-tuple-element.169.refs_3_), channel_id=1, source_target_pairs={{1,2},{2,1},{5,6},{6,5},{9,10},{10,9},{13,14},{14,13},{17,18},{18,... | collective-permute-start | bytes 1572872 | tf_op jit(solution)/shard_map/ppermute | solution.py:113
  189.9 18.8 %collective-permute-start.24 = (bf16[128,2048]{1,0:T(8,128)(2,1)S(1)}, bf16[128,2048]{1,0:T(8,128)(2,1)S(1)}, u32[]{:S(2)}, u32[]{:S(2)}) collective-permute-start(bf16[128,2048]{1,0:T(8,128)(2,1)S(1)} %get-tuple-element.170.refs_4_), channel_id=1, source_target_pairs={{2,3},{1,0},{6,7},{5,4},{10,11},{9,8},{14,15},{13,12},{18,19},{17,... | collective-permute-start | bytes 1572872 | tf_op jit(solution)/shard_map/ppermute | solution.py:113
  208.8 15.8 %collective-permute-start.28 = (bf16[128,2048]{1,0:T(8,128)(2,1)S(1)}, bf16[128,2048]{1,0:T(8,128)(2,1)S(1)}, u32[]{:S(2)}, u32[]{:S(2)}) collective-permute-start(bf16[128,2048]{1,0:T(8,128)(2,1)S(1)} %get-tuple-element.183.refs_3_), channel_id=1, source_target_pairs={{2,3},{1,0},{6,7},{5,4},{10,11},{9,8},{14,15},{13,12},{18,19},{17,... | collective-permute-start | bytes 1572872 | tf_op jit(solution)/shard_map/ppermute | solution.py:113
  210.1 20.7 %collective-permute-start.31 = (bf16[192,2048]{1,0:T(8,128)(2,1)S(1)}, bf16[192,2048]{1,0:T(8,128)(2,1)S(1)}, u32[]{:S(2)}, u32[]{:S(2)}) collective-permute-start(bf16[192,2048]{1,0:T(8,128)(2,1)S(1)} %get-tuple-element.178.refs_0_), channel_id=1, source_target_pairs={{0,1},{3,2},{4,5},{7,6},{8,9},{11,10},{12,13},{15,14},{16,17},{19,... | collective-permute-start | bytes 2359304 | tf_op jit(solution)/shard_map/ppermute | solution.py:113
  211.6 20.7 %collective-permute-start.30 = (bf16[192,2048]{1,0:T(8,128)(2,1)S(1)}, bf16[192,2048]{1,0:T(8,128)(2,1)S(1)}, u32[]{:S(2)}, u32[]{:S(2)}) collective-permute-start(bf16[192,2048]{1,0:T(8,128)(2,1)S(1)} %get-tuple-element.188), channel_id=1, source_target_pairs={{1,2},{2,1},{5,6},{6,5},{9,10},{10,9},{13,14},{14,13},{17,18},{18,... | collective-permute-start | bytes 2359304 | tf_op jit(solution)/shard_map/ppermute | solution.py:113
  229.5 6.7 %collective-permute-start.29 = (f32[128,1024]{1,0:T(8,128)S(1)}, f32[128,1024]{1,0:T(8,128)S(1)}, u32[]{:S(2)}, u32[]{:S(2)}) collective-permute-start(f32[128,1024]{1,0:T(8,128)S(1)} %get-tuple-element.186), channel_id=1, source_target_pairs={{0,4},{4,0},{1,5},{5,1},{2,6},{6,2},{3,7},{7,3},{8,12},{12,8},{9,1... | collective-permute-start | bytes 1572872 | tf_op jit(solution)/shard_map/ppermute | solution.py:113
  233.2 26.3 %collective-permute-start.34 = (bf16[192,2048]{1,0:T(8,128)(2,1)S(1)}, bf16[192,2048]{1,0:T(8,128)(2,1)S(1)}, u32[]{:S(2)}, u32[]{:S(2)}) collective-permute-start(bf16[192,2048]{1,0:T(8,128)(2,1)S(1)} %get-tuple-element.199), channel_id=1, source_target_pairs={{0,1},{3,2},{2,3},{1,0},{4,5},{7,6},{6,7},{5,4},{8,9},{11,10},{10,... | collective-permute-start | bytes 2359304 | tf_op jit(solution)/shard_map/ppermute | solution.py:113
  233.3 26.3 %collective-permute-start.35 = (bf16[192,2048]{1,0:T(8,128)(2,1)S(1)}, bf16[192,2048]{1,0:T(8,128)(2,1)S(1)}, u32[]{:S(2)}, u32[]{:S(2)}) collective-permute-start(bf16[192,2048]{1,0:T(8,128)(2,1)S(1)} %get-tuple-element.200), channel_id=1, source_target_pairs={{1,2},{2,1},{5,6},{6,5},{9,10},{10,9},{13,14},{14,13},{17,18},{18,... | collective-permute-start | bytes 2359304 | tf_op jit(solution)/shard_map/ppermute | solution.py:113
  240.5 1.6 collective-permute-start.32
  246.9 15.9 %collective-permute-start.33 = (bf16[128,2048]{1,0:T(8,128)(2,1)S(1)}, bf16[128,2048]{1,0:T(8,128)(2,1)S(1)}, u32[]{:S(2)}, u32[]{:S(2)}) collective-permute-start(bf16[128,2048]{1,0:T(8,128)(2,1)S(1)} %get-tuple-element.195.refs_1_), channel_id=1, source_target_pairs={{0,1},{3,2},{4,5},{7,6},{8,9},{11,10},{12,13},{15,14},{16,17},{19,... | collective-permute-start | bytes 1572872 | tf_op jit(solution)/shard_map/ppermute | solution.py:113
  258.2 15.9 %collective-permute-start.37 = (bf16[128,2048]{1,0:T(8,128)(2,1)S(1)}, bf16[128,2048]{1,0:T(8,128)(2,1)S(1)}, u32[]{:S(2)}, u32[]{:S(2)}) collective-permute-start(bf16[128,2048]{1,0:T(8,128)(2,1)S(1)} %get-tuple-element.197.refs_0_), channel_id=1, source_target_pairs={{0,1},{3,2},{4,5},{7,6},{8,9},{11,10},{12,13},{15,14},{16,17},{19,... | collective-permute-start | bytes 1572872 | tf_op jit(solution)/shard_map/ppermute | solution.py:113
  262.9 15.0 %collective-permute-start.36 = (bf16[128,2048]{1,0:T(8,128)(2,1)S(1)}, bf16[128,2048]{1,0:T(8,128)(2,1)S(1)}, u32[]{:S(2)}, u32[]{:S(2)}) collective-permute-start(bf16[128,2048]{1,0:T(8,128)(2,1)S(1)} %get-tuple-element.204), channel_id=1, source_target_pairs={{1,2},{2,1},{5,6},{6,5},{9,10},{10,9},{13,14},{14,13},{17,18},{18,... | collective-permute-start | bytes 1572872 | tf_op jit(solution)/shard_map/ppermute | solution.py:113
  278.7 12.3 %collective-permute-start.38 = (bf16[128,2048]{1,0:T(8,128)(2,1)S(1)}, bf16[128,2048]{1,0:T(8,128)(2,1)S(1)}, u32[]{:S(2)}, u32[]{:S(2)}) collective-permute-start(bf16[128,2048]{1,0:T(8,128)(2,1)S(1)} %get-tuple-element.206), channel_id=1, source_target_pairs={{0,1},{3,2},{2,3},{1,0},{4,5},{7,6},{6,7},{5,4},{8,9},{11,10},{10,... | collective-permute-start | bytes 1572872 | tf_op jit(solution)/shard_map/ppermute | solution.py:113
  278.8 14.1 %collective-permute-start.39 = (bf16[128,2048]{1,0:T(8,128)(2,1)S(1)}, bf16[128,2048]{1,0:T(8,128)(2,1)S(1)}, u32[]{:S(2)}, u32[]{:S(2)}) collective-permute-start(bf16[128,2048]{1,0:T(8,128)(2,1)S(1)} %get-tuple-element.207), channel_id=1, source_target_pairs={{1,2},{2,1},{5,6},{6,5},{9,10},{10,9},{13,14},{14,13},{17,18},{18,... | collective-permute-start | bytes 1572872 | tf_op jit(solution)/shard_map/ppermute | solution.py:113
  (8 other events, 7.8 us)
Sparse Core Ops, SparseCore 0:
  66.3 24.8 all-gather.1

commit v4 on v3

--- a/solution.py
+++ b/solution.py
@@ -196,18 +196,27 @@
 def gain_rows(order, activations, gain, rows):
     width = activations.shape[1]
 
-    def body(source, gain_ref, out, held, here):
-        copy = pltpu.make_async_copy(source.at[:rows, :], held, here)
-        copy.start()
-        copy.wait()
+    def body(source, gain_hbm, out, held, gain_ref, here):
+        copies = [
+            pltpu.make_async_copy(source.at[:rows, :], held, here.at[0]),
+            pltpu.make_async_copy(gain_hbm, gain_ref, here.at[1]),
+        ]
+        for copy in copies:
+            copy.start()
+        for copy in copies:
+            copy.wait()
         out[...] = (held[...].astype(jnp.float32) * gain_ref[...]).astype(out.dtype)
 
     return order.call(
         body,
         [jax.ShapeDtypeStruct((rows, width), jnp.bfloat16)],
-        [pltpu.VMEM((rows, width), jnp.bfloat16), pltpu.SemaphoreType.DMA(())],
+        [
+            pltpu.VMEM((rows, width), jnp.bfloat16),
+            pltpu.VMEM(gain.shape, jnp.float32),
+            pltpu.SemaphoreType.DMA((2,)),
+        ],
         [activations, gain],
-        [pl.ANY, pltpu.VMEM],
+        [pl.ANY, pl.ANY],
         "gain_rows",
     )[0]
 
@@ -391,7 +400,7 @@
     lax.fori_loop(0, steps, one, 0)
 
 
-def project(order, meta, slots, features, so_far, weight, split):
+def project(order, meta, slots, features, so_far, weight, split, kind=jnp.float32):
     rows, width = features[0].shape
     columns = weight.shape[1]
     steps = columns // DEPTH
@@ -452,7 +461,7 @@
             half = columns // 2
             mine = meta_ref[5]
             outs[0][...] = total[:, pl.ds(pl.multiple_of(mine * half, half), half)]
-            outs[1][...] = total[:, pl.ds(pl.multiple_of((1 - mine) * half, half), half)]
+            outs[1][...] = total[:, pl.ds(pl.multiple_of((1 - mine) * half, half), half)].astype(outs[1].dtype)
 
     whole = jax.ShapeDtypeStruct((rows, columns), jnp.float32)
     halves = jax.ShapeDtypeStruct((rows, columns // 2), jnp.float32)
@@ -460,7 +469,7 @@
     spaces = [pltpu.SMEM, pl.ANY] + ([] if so_far is None else [pl.ANY]) + [pl.ANY] * len(features)
     return order.call(
         body,
-        [halves, halves] if split else [whole],
+        [halves, jax.ShapeDtypeStruct(halves.shape, kind)] if split else [whole],
         ([pltpu.VMEM((rows, columns), jnp.float32)] if split else [])
         + [
             pltpu.VMEM((turns, rows, width), jnp.bfloat16),
@@ -495,7 +504,7 @@
 
         def one_head(head, carry):
             place = pl.ds(pl.multiple_of(head * HD, HD), HD)
-            raw = mine_ref[:, place] + arrived_ref[:, place]
+            raw = mine_ref[:, place] + arrived_ref[:, place].astype(jnp.float32)
             turned = pltpu.roll(raw, HD // 2, 1)
             query = (raw * cosine_ref[spot_rows, :] + turned * sine_ref[spot_rows, :]).astype(jnp.bfloat16)
             summed = jnp.zeros((rows, values.shape[1]), jnp.float32)
@@ -651,21 +660,24 @@
         if more:
             farthest, gained[i + 1] = order.arrive(farthest, gained[i + 1])
             beside, across = hop(gained[i + 1], OUTER_IN + OUTER_OUT), hop(gained[i + 1], MIDDLE)
-        mine, other = project(order, meta, ((3, (0, 1)),), (far_middle, farthest), so_far, query_weight, True)
+        mine, other = project(
+            order, meta, ((3, (0, 1)),), (far_middle, farthest), so_far, query_weight, True, jnp.bfloat16 if i == 0 else jnp.float32
+        )
         other = hop(other, swap, "row")
         if waiting is not None:
             fourth, outer, middle = last_sums(order, meta, *waiting)
             waiting = (fourth, hop(outer, OUTER_IN + OUTER_OUT), hop(middle, MIDDLE))
         attended = attend(order, mine, other, bounds[i], cosine, sine, pairs, my_ids, ids, cut)
         other_attended = hop(attended, swap, "row")
+        if more:
+            beside, across = order.arrive(beside, across)
+            far_middle, far_end = send_far(beside, across)
         spread_out = lambda slot, *kinds: output_parts(
             order, meta, slot, attended, other_attended, out_weight, kinds
         )
         if more:
             first, second = spread_out(0, jnp.bfloat16, jnp.bfloat16)
             inward, inward_next = hop(first, OUTER_IN), hop(second, OUTER_IN)
-            beside, across = order.arrive(beside, across)
-            far_middle, far_end = send_far(beside, across)
             third, fourth = spread_out(2, jnp.bfloat16, jnp.float32)
         else:
             (first,) = spread_out(0, jnp.bfloat16)
@@ -679,9 +691,10 @@
             farthest = hop(far_middle, OUTER_OUT)
         (middle,) = order.add([(second, inward)], [jnp.bfloat16])
         waiting = (first, third, fourth, hop(middle, MIDDLE), inward_next)
+    inward_last = hop(waiting[1], OUTER_IN)
     fourth, outer, middle = last_sums(order, meta, *waiting)
-    outer, middle = hop(outer, OUTER_IN + OUTER_OUT), hop(middle, MIDDLE)
-    return final_rows(order, out, slab, bounds[-1], (fourth, outer, middle))
+    outer, middle = hop(outer, OUTER_OUT), hop(middle, MIDDLE)
+    return final_rows(order, out, slab, bounds[-1], (fourth, inward_last, outer, middle))
 
 
 def solution(mesh):

time: 302 us -> 303 us (level)
    ppermute x40 -> x41, starting transfers between devices: 63.6 us -> 66.4 us  [hop(): return lax.ppermute(values, axis, list(pairs))]
    unnamed x30 -> x34, local copies, waits for them, and re-layouts: 8.06 us -> 9.73 us
    ppermute x40 -> x41, waiting for transfers between devices: 80 us -> 78.9 us  [hop(): return lax.ppermute(values, axis, list(pairs))]
  transfers between devices with their start and end apart: 41 -> 42, of which waited for: 20 -> 21; matrix products, arithmetic and copies ran while one was open for 1% -> 1% of each run, Pallas kernels for 43% -> 43%
where the time goes in v4:
time: 303 us; the launch traced here: 302 us
  Pallas kernels  131 us (43%)
  waiting for transfers between devices  79 us (26%)
  starting transfers between devices  66.4 us (22%)
  between operations  14.2 us (5%)
  local copies, waits for them, and re-layouts  10.7 us (4%)
    pallas_call x36, Pallas kernels, call(): pl.pallas_call(kernel, out_shape=list(outs) + [jax.ShapeDtypeStruct((8, H...  131 us
    ppermute x41, waiting for transfers between devices, hop(): return lax.ppermute(values, axis, list(pairs))  78.9 us
    ppermute x41, starting transfers between devices, hop(): return lax.ppermute(values, axis, list(pairs))  66.4 us
    unnamed x34, local copies, waits for them, and re-layouts  9.73 us
  transfers between devices with their start and end apart: 42, of which 21 were waited for; matrix products, arithmetic and copies ran while one was open for 1% of the time, Pallas kernels for 43%

profile of v4, /device:TPU:8, one launch (start us, length us, event | category | flops | bytes accessed | tf_op | source)
XLA Modules:
  0.0 302.3 jit_solution(17694399325437847395)
XLA Ops:
  10.0 5.0 %collective-permute-start.1 = (bf16[192,2048]{1,0:T(8,128)(2,1)}, bf16[192,2048]{1,0:T(8,128)(2,1)}, u32[]{:S(2)}, u32[]{:S(2)}) collective-permute-start(bf16[192,2048]{1,0:T(8,128)(2,1)} %get-tuple-element.108.refs_2_), channel_id=1, source_target_pairs={{1,2},{2,1},{5,6},{6,5},{9,10},{10,9},{13,14},{14,13},{17,18},{18,... | collective-permute-start | bytes 2359304 | tf_op jit(solution)/shard_map/ppermute | solution.py:113
  15.9 7.6 %key_value_terms.1 = (f32[272,1024]{1,0:T(8,128)S(1)}, f32[272,1024]{1,0:T(8,128)}, bf16[192,2048]{1,0:T(8,128)(2,1)S(1)}, bf16[128,2048]{1,0:T(8,128)(2,1)S(1)}, f32[8,128]{1,0:T(8,128)S(1)}) custom-call(s32[11]{0:T(128)S(1)} %concatenate.9.refs_0_, bf16[512,2048]{1,0:T(8,128)(2,1)S(1)} %copy-done.3, f32[1,2048]{1,0:T(1,128)S(1)} %bitcast.15, ...), custom_call_target="tpu_custom_call" | custom-call | bytes 15000000 | tf_op jit(solution)/shard_map/key_value_terms/pallas_call | solution.py:134
  26.6 3.0 collective-permute-done.refs_0_
  29.6 3.0 collective-permute-done.1.refs_1_
  32.8 3.6 %collective-permute-start.2 = (bf16[192,2048]{1,0:T(8,128)(2,1)}, bf16[192,2048]{1,0:T(8,128)(2,1)S(1)}, u32[]{:S(2)}, u32[]{:S(2)}) collective-permute-start(bf16[192,2048]{1,0:T(8,128)(2,1)} %get-tuple-element.111.refs_3_), channel_id=1, source_target_pairs={{1,2},{2,1},{5,6},{6,5},{9,10},{10,9},{13,14},{14,13},{17,18},{18,... | collective-permute-start | bytes 2359304 | tf_op jit(solution)/shard_map/ppermute | solution.py:113
  39.7 1.7 collective-permute-start.7
  41.4 21.2 %collective-permute-done.5.refs_2_ = bf16[272,256]{1,0:T(8,128)(2,1)S(1)} collective-permute-done((bf16[272,256]{1,0:T(8,128)(2,1)S(1)}, bf16[272,256]{1,0:T(8,128)(2,1)S(1)}, u32[]{:S(2)}, u32[]{:S(2)}) %collective-permute-start.5) | collective-permute-done | bytes 139296 | tf_op jit(solution)/shard_map/ppermute | solution.py:113
  67.5 12.1 %project.6 = (f32[192,2048]{1,0:T(8,128)S(1)}, f32[8,128]{1,0:T(8,128)S(1)}) custom-call(s32[11]{0:T(128)S(1)} %concatenate.9.refs_0_, bf16[8192,2048]{1,0:T(8,128)(2,1)} %refs_1_.13, bf16[192,2048]{1,0:T(8,128)(2,1)} %get-tuple-element.108.refs_2_, bf16[192,2048]{1,0:T(8,128)(2,1)} %get-tuple-element.111.refs_3_, ...), custom_call_target="tpu_custom_call" | custom-call | bytes 25165824 | tf_op jit(solution)/shard_map/project/pallas_call | solution.py:134
  79.6 5.0 %collective-permute-done.8.refs_0_ = bf16[192,2048]{1,0:T(8,128)(2,1)S(1)} collective-permute-done((bf16[192,2048]{1,0:T(8,128)(2,1)S(1)}, bf16[192,2048]{1,0:T(8,128)(2,1)S(1)}, u32[]{:S(2)}, u32[]{:S(2)}) %collective-permute-start.8) | collective-permute-done | bytes 786464 | tf_op jit(solution)/shard_map/ppermute | solution.py:113
  84.6 3.2 %collective-permute-start.10 = (bf16[192,2048]{1,0:T(8,128)(2,1)S(1)}, bf16[192,2048]{1,0:T(8,128)(2,1)S(1)}, u32[]{:S(2)}, u32[]{:S(2)}) collective-permute-start(bf16[192,2048]{1,0:T(8,128)(2,1)S(1)} %get-tuple-element.129.refs_2_), channel_id=1, source_target_pairs={{1,2},{2,1},{5,6},{6,5},{9,10},{10,9},{13,14},{14,13},{17,18},{18,... | collective-permute-start | bytes 2359304 | tf_op jit(solution)/shard_map/ppermute | solution.py:113
  87.8 5.3 %project.7 = (f32[192,1024]{1,0:T(8,128)S(1)}, bf16[192,1024]{1,0:T(8,128)(2,1)S(1)}, f32[8,128]{1,0:T(8,128)S(1)}) custom-call(s32[11]{0:T(128)S(1)} %concatenate.9.refs_0_, bf16[8192,2048]{1,0:T(8,128)(2,1)} %refs_1_.13, f32[192,2048]{1,0:T(8,128)S(1)} %get-tuple-element.130.refs_2_, bf16[192,2048]{1,0:T(8,128)(2,1)S(1)} %get-tuple-element.124.refs_3_, ...), custom_call_target="tpu_custom_call" | custom-call | bytes 8388608 | tf_op jit(solution)/shard_map/project/pallas_call | solution.py:134
  94.1 1.7 collective-permute-done.11.refs_1_
  99.9 5.5 %attend.3 = (bf16[192,1024]{1,0:T(8,128)(2,1)S(1)}, f32[8,128]{1,0:T(8,128)S(1)}) custom-call(f32[192,1024]{1,0:T(8,128)S(1)} %copy-done.9, bf16[192,1024]{1,0:T(8,128)(2,1)S(1)} %copy-done.11, f32[512,128]{1,0:T(8,128)S(1)} %get-tuple-element.135.refs_2_, f32[512,128]{1,0:T(8,128)S(1)} %get-tuple-element.136.refs_3_, bf16[2048,256]{1,0:T(8,128)(2,1)S(1)} %copy-done, ...), custom_call_target="tpu_custom_call" | custom-call | bytes 20000000 | tf_op jit(solution)/shard_map/attend/pallas_call | solution.py:134
  105.4 3.6 %collective-permute-start.12 = (bf16[192,2048]{1,0:T(8,128)(2,1)}, bf16[192,2048]{1,0:T(8,128)(2,1)S(1)}, u32[]{:S(2)}, u32[]{:S(2)}) collective-permute-start(bf16[192,2048]{1,0:T(8,128)(2,1)} %get-tuple-element.142.refs_3_), channel_id=1, source_target_pairs={{1,2},{2,1},{5,6},{6,5},{9,10},{10,9},{13,14},{14,13},{17,18},{18,... | collective-permute-start | bytes 2359304 | tf_op jit(solution)/shard_map/ppermute | solution.py:113
  112.2 8.4 %output_parts.6 = (bf16[192,2048]{1,0:T(8,128)(2,1)S(1)}, bf16[192,2048]{1,0:T(8,128)(2,1)S(1)}, f32[8,128]{1,0:T(8,128)S(1)}) custom-call(s32[11]{0:T(128)S(1)} %concatenate.9.refs_0_, bf16[192,1024]{1,0:T(8,128)(2,1)S(1)} %get-tuple-element.144.refs_1_, bf16[192,1024]{1,0:T(8,128)(2,1)S(1)} %collective-permute-done.14.refs_2_, ...), custom_call_target="tpu_custom_call" | custom-call | bytes 16777216 | tf_op jit(solution)/shard_map/output_parts/pallas_call | solution.py:134
  121.9 8.5 %output_parts.7 = (bf16[192,2048]{1,0:T(8,128)(2,1)S(1)}, f32[192,2048]{1,0:T(8,128)S(1)}, f32[8,128]{1,0:T(8,128)S(1)}) custom-call(s32[11]{0:T(128)S(1)} %concatenate.9.refs_0_, bf16[192,1024]{1,0:T(8,128)(2,1)S(1)} %get-tuple-element.144.refs_1_, bf16[192,1024]{1,0:T(8,128)(2,1)S(1)} %collective-permute-done.14.refs_2_, bf16[2048,8192]{1,0:T(8,128)(2,1)} %refs_3_.13, ...), custom_call_target="tpu_custom_call" | custom-call | bytes 16777216 | tf_op jit(solution)/shard_map/output_parts/pallas_call | solution.py:134
  130.5 4.6 %collective-permute-start.15 = (bf16[192,2048]{1,0:T(8,128)(2,1)S(1)}, bf16[192,2048]{1,0:T(8,128)(2,1)S(1)}, u32[]{:S(2)}, u32[]{:S(2)}) collective-permute-start(bf16[192,2048]{1,0:T(8,128)(2,1)S(1)} %get-tuple-element.148.refs_3_), channel_id=1, source_target_pairs={{2,3},{1,0},{6,7},{5,4},{10,11},{9,8},{14,15},{13,12},{18,19},{17,... | collective-permute-start | bytes 2359304 | tf_op jit(solution)/shard_map/ppermute | solution.py:113
  136.5 6.5 %collective-permute-done.16.refs_1_ = bf16[192,2048]{1,0:T(8,128)(2,1)S(1)} collective-permute-done((bf16[192,2048]{1,0:T(8,128)(2,1)S(1)}, bf16[192,2048]{1,0:T(8,128)(2,1)S(1)}, u32[]{:S(2)}, u32[]{:S(2)}) %collective-permute-start.16) | collective-permute-done | bytes 786464 | tf_op jit(solution)/shard_map/ppermute | solution.py:113
  143.1 2.4 collective-permute-start.20
  145.5 11.6 %project.8 = (f32[192,2048]{1,0:T(8,128)S(1)}, f32[8,128]{1,0:T(8,128)S(1)}) custom-call(s32[11]{0:T(128)S(1)} %concatenate.9.refs_0_, bf16[8192,2048]{1,0:T(8,128)(2,1)} %refs_1_.13, bf16[192,2048]{1,0:T(8,128)(2,1)S(1)} %get-tuple-element.129.refs_2_, bf16[192,2048]{1,0:T(8,128)(2,1)} %get-tuple-element.142.refs_3_, ...), custom_call_target="tpu_custom_call" | custom-call | bytes 25165824 | tf_op jit(solution)/shard_map/project/pallas_call | solution.py:134
  157.2 5.5 %project.9 = (f32[192,1024]{1,0:T(8,128)S(1)}, f32[192,1024]{1,0:T(8,128)S(1)}, f32[8,128]{1,0:T(8,128)S(1)}) custom-call(s32[11]{0:T(128)S(1)} %concatenate.9.refs_0_, bf16[8192,2048]{1,0:T(8,128)(2,1)} %refs_1_.13, f32[192,2048]{1,0:T(8,128)S(1)} %get-tuple-element.157.refs_2_, bf16[192,2048]{1,0:T(8,128)(2,1)S(1)} %get-tuple-element.148.refs_3_, ...), custom_call_target="tpu_custom_call" | custom-call | bytes 8388608 | tf_op jit(solution)/shard_map/project/pallas_call | solution.py:134
  162.8 3.6 %collective-permute-start.18 = (bf16[128,2048]{1,0:T(8,128)(2,1)S(1)}, bf16[128,2048]{1,0:T(8,128)(2,1)S(1)}, u32[]{:S(2)}, u32[]{:S(2)}) collective-permute-start(bf16[128,2048]{1,0:T(8,128)(2,1)S(1)} %get-tuple-element.156.refs_2_), channel_id=1, source_target_pairs={{1,2},{2,1},{5,6},{6,5},{9,10},{10,9},{13,14},{14,13},{17,18},{18,... | collective-permute-start | bytes 1572872 | tf_op jit(solution)/shard_map/ppermute | solution.py:113
  167.4 5.5 %attend.4 = (bf16[192,1024]{1,0:T(8,128)(2,1)S(1)}, f32[8,128]{1,0:T(8,128)S(1)}) custom-call(f32[192,1024]{1,0:T(8,128)S(1)} %get-tuple-element.160.refs_0_, f32[192,1024]{1,0:T(8,128)S(1)} %collective-permute-done.19.refs_1_, f32[512,128]{1,0:T(8,128)S(1)} %get-tuple-element.135.refs_2_, f32[512,128]{1,0:T(8,128)S(1)} %get-tuple-element.136.refs_3_, ...), custom_call_target="tpu_custom_call" | custom-call | bytes 20000000 | tf_op jit(solution)/shard_map/attend/pallas_call | solution.py:134
  173.1 2.5 collective-permute-start.25
  175.6 2.0 collective-permute-done.17.refs_0_
  177.6 2.1 collective-permute-done.18.refs_1_
  179.6 8.4 %output_parts.8 = (bf16[192,2048]{1,0:T(8,128)(2,1)S(1)}, bf16[192,2048]{1,0:T(8,128)(2,1)S(1)}, f32[8,128]{1,0:T(8,128)S(1)}) custom-call(s32[11]{0:T(128)S(1)} %concatenate.9.refs_0_, bf16[192,1024]{1,0:T(8,128)(2,1)S(1)} %get-tuple-element.172.refs_1_, bf16[192,1024]{1,0:T(8,128)(2,1)S(1)} %collective-permute-done.26.refs_2_, ...), custom_call_target="tpu_custom_call" | custom-call | bytes 16777216 | tf_op jit(solution)/shard_map/output_parts/pallas_call | solution.py:134
  189.3 3.5 %collective-permute-start.22 = (bf16[128,2048]{1,0:T(8,128)(2,1)S(1)}, bf16[128,2048]{1,0:T(8,128)(2,1)S(1)}, u32[]{:S(2)}, u32[]{:S(2)}) collective-permute-start(bf16[128,2048]{1,0:T(8,128)(2,1)S(1)} %get-tuple-element.167.refs_3_), channel_id=1, source_target_pairs={{1,2},{2,1},{5,6},{6,5},{9,10},{10,9},{13,14},{14,13},{17,18},{18,... | collective-permute-start | bytes 1572872 | tf_op jit(solution)/shard_map/ppermute | solution.py:113
  192.8 1.8 collective-permute-start.23
  194.7 8.5 %output_parts.9 = (bf16[192,2048]{1,0:T(8,128)(2,1)S(1)}, f32[192,2048]{1,0:T(8,128)S(1)}, f32[8,128]{1,0:T(8,128)S(1)}) custom-call(s32[11]{0:T(128)S(1)} %concatenate.9.refs_0_, bf16[192,1024]{1,0:T(8,128)(2,1)S(1)} %get-tuple-element.172.refs_1_, bf16[192,1024]{1,0:T(8,128)(2,1)S(1)} %collective-permute-done.26.refs_2_, bf16[2048,8192]{1,0:T(8,128)(2,1)} %refs_3_.13, ...), custom_call_target="tpu_custom_call" | custom-call | bytes 16777216 | tf_op jit(solution)/shard_map/output_parts/pallas_call | solution.py:134
  204.4 2.7 collective-permute-done.22.refs_0_
  207.1 1.9 collective-permute-start.28
  211.0 3.5 %collective-permute-start.30 = (bf16[192,2048]{1,0:T(8,128)(2,1)S(1)}, bf16[192,2048]{1,0:T(8,128)(2,1)S(1)}, u32[]{:S(2)}, u32[]{:S(2)}) collective-permute-start(bf16[192,2048]{1,0:T(8,128)(2,1)S(1)} %get-tuple-element.188), channel_id=1, source_target_pairs={{1,2},{2,1},{5,6},{6,5},{9,10},{10,9},{13,14},{14,13},{17,18},{18,... | collective-permute-start | bytes 2359304 | tf_op jit(solution)/shard_map/ppermute | solution.py:113
  214.5 10.0 %project.10 = (f32[128,2048]{1,0:T(8,128)S(1)}, f32[8,128]{1,0:T(8,128)S(1)}) custom-call(s32[11]{0:T(128)S(1)} %concatenate.9.refs_0_, bf16[8192,2048]{1,0:T(8,128)(2,1)} %refs_1_.13, bf16[128,2048]{1,0:T(8,128)(2,1)S(1)} %get-tuple-element.156.refs_2_, bf16[128,2048]{1,0:T(8,128)(2,1)S(1)} %get-tuple-element.167.refs_3_, ...), custom_call_target="tpu_custom_call" | custom-call | bytes 25165824 | tf_op jit(solution)/shard_map/project/pallas_call | solution.py:134
  224.5 4.9 %project.11 = (f32[128,1024]{1,0:T(8,128)S(1)}, f32[128,1024]{1,0:T(8,128)S(1)}, f32[8,128]{1,0:T(8,128)S(1)}) custom-call(s32[11]{0:T(128)S(1)} %concatenate.9.refs_0_, bf16[8192,2048]{1,0:T(8,128)(2,1)} %refs_1_.13, f32[128,2048]{1,0:T(8,128)S(1)} %get-tuple-element.182.refs_2_, bf16[128,2048]{1,0:T(8,128)(2,1)S(1)} %get-tuple-element.183.refs_3_, ...), custom_call_target="tpu_custom_call" | custom-call | bytes 8388608 | tf_op jit(solution)/shard_map/project/pallas_call | solution.py:134
  229.5 2.5 collective-permute-done.30.refs_3_
  233.0 3.5 %collective-permute-start.36 = (bf16[192,2048]{1,0:T(8,128)(2,1)S(1)}, bf16[192,2048]{1,0:T(8,128)(2,1)S(1)}, u32[]{:S(2)}, u32[]{:S(2)}) collective-permute-start(bf16[192,2048]{1,0:T(8,128)(2,1)S(1)} %get-tuple-element.200), channel_id=1, source_target_pairs={{1,2},{2,1},{5,6},{6,5},{9,10},{10,9},{13,14},{14,13},{17,18},{18,... | collective-permute-start | bytes 2359304 | tf_op jit(solution)/shard_map/ppermute | solution.py:113
  236.5 4.2 %attend.5 = (bf16[128,1024]{1,0:T(8,128)(2,1)S(1)}, f32[8,128]{1,0:T(8,128)S(1)}) custom-call(f32[128,1024]{1,0:T(8,128)S(1)} %get-tuple-element.185.refs_0_, f32[128,1024]{1,0:T(8,128)S(1)} %collective-permute-done.29.refs_1_, f32[512,128]{1,0:T(8,128)S(1)} %get-tuple-element.135.refs_2_, f32[512,128]{1,0:T(8,128)S(1)} %get-tuple-element.136.refs_3_, ...), custom_call_target="tpu_custom_call" | custom-call | bytes 20000000 | tf_op jit(solution)/shard_map/attend/pallas_call | solution.py:134
  242.3 4.8 %output_parts.10 = (bf16[128,2048]{1,0:T(8,128)(2,1)S(1)}, f32[8,128]{1,0:T(8,128)S(1)}) custom-call(s32[11]{0:T(128)S(1)} %concatenate.9.refs_0_, bf16[128,1024]{1,0:T(8,128)(2,1)S(1)} %get-tuple-element.191.refs_1_, bf16[128,1024]{1,0:T(8,128)(2,1)S(1)} %collective-permute-done.32.refs_2_, bf16[2048,8192]{1,0:T(8,128)(2,1)} %refs_3_.13, ...), custom_call_target="tpu_custom_call" | custom-call | bytes 8388608 | tf_op jit(solution)/shard_map/output_parts/pallas_call | solution.py:134
  248.4 10.1 %output_parts.11 = (bf16[128,2048]{1,0:T(8,128)(2,1)S(1)}, bf16[128,2048]{1,0:T(8,128)(2,1)S(1)}, f32[128,2048]{1,0:T(8,128)S(1)}, f32[8,128]{1,0:T(8,128)S(1)}) custom-call(s32[11]{0:T(128)S(1)} %concatenate.9.refs_0_, bf16[128,1024]{1,0:T(8,128)(2,1)S(1)} %get-tuple-element.191.refs_1_, bf16[128,1024]{1,0:T(8,128)(2,1)S(1)} %collective-permute-done.32.refs_2_, ...), custom_call_target="tpu_custom_call" | custom-call | bytes 25165824 | tf_op jit(solution)/shard_map/output_parts/pallas_call | solution.py:134
  261.0 2.0 collective-permute-done.34.refs_1_
  263.1 3.3 %collective-permute-start.37 = (bf16[128,2048]{1,0:T(8,128)(2,1)S(1)}, bf16[128,2048]{1,0:T(8,128)(2,1)S(1)}, u32[]{:S(2)}, u32[]{:S(2)}) collective-permute-start(bf16[128,2048]{1,0:T(8,128)(2,1)S(1)} %get-tuple-element.204), channel_id=1, source_target_pairs={{1,2},{2,1},{5,6},{6,5},{9,10},{10,9},{13,14},{14,13},{17,18},{18,... | collective-permute-start | bytes 1572872 | tf_op jit(solution)/shard_map/ppermute | solution.py:113
  267.7 7.5 %collective-permute-done.38.refs_4_ = bf16[128,2048]{1,0:T(8,128)(2,1)S(1)} collective-permute-done((bf16[128,2048]{1,0:T(8,128)(2,1)S(1)}, bf16[128,2048]{1,0:T(8,128)(2,1)S(1)}, u32[]{:S(2)}, u32[]{:S(2)}) %collective-permute-start.38) | collective-permute-done | bytes 524320 | tf_op jit(solution)/shard_map/ppermute | solution.py:113
  275.2 3.0 collective-permute-done.37.refs_3_
  280.3 3.2 %collective-permute-start.40 = (bf16[128,2048]{1,0:T(8,128)(2,1)S(1)}, bf16[128,2048]{1,0:T(8,128)(2,1)S(1)}, u32[]{:S(2)}, u32[]{:S(2)}) collective-permute-start(bf16[128,2048]{1,0:T(8,128)(2,1)S(1)} %get-tuple-element.207), channel_id=1, source_target_pairs={{1,2},{2,1},{5,6},{6,5},{9,10},{10,9},{13,14},{14,13},{17,18},{18,... | collective-permute-start | bytes 1572872 | tf_op jit(solution)/shard_map/ppermute | solution.py:113
  283.5 2.1 collective-permute-done.33.refs_1_
  285.6 4.6 %collective-permute-done.39.refs_2_ = bf16[128,2048]{1,0:T(8,128)(2,1)S(1)} collective-permute-done((bf16[128,2048]{1,0:T(8,128)(2,1)S(1)}, bf16[128,2048]{1,0:T(8,128)(2,1)S(1)}, u32[]{:S(2)}, u32[]{:S(2)}) %collective-permute-start.39) | collective-permute-done | bytes 524320 | tf_op jit(solution)/shard_map/ppermute | solution.py:113
  290.2 4.1 %collective-permute-done.40.refs_3_ = bf16[128,2048]{1,0:T(8,128)(2,1)S(1)} collective-permute-done((bf16[128,2048]{1,0:T(8,128)(2,1)S(1)}, bf16[128,2048]{1,0:T(8,128)(2,1)S(1)}, u32[]{:S(2)}, u32[]{:S(2)}) %collective-permute-start.40) | collective-permute-done | bytes 524320 | tf_op jit(solution)/shard_map/ppermute | solution.py:113
  (116 shorter events, 43.2 us)
Async XLA Ops:
  6.5 90.0 %all-gather.2.cloned.1.call-start = ((), (), s32[]{:S(2)}) async-start(), calls=%async_computation | async-start | bytes 1179648 | tf_op jit(solution)/shard_map/all_gather | solution.py:644
  8.8 7.0 %copy-start.3 = (bf16[512,2048]{1,0:T(8,128)(2,1)S(1)}, bf16[512,2048]{1,0:T(8,128)(2,1)}, u32[]{:S(2)}) copy-start(bf16[512,2048]{1,0:T(8,128)(2,1)} %refs_1_.7) | copy-start | bytes 6291460
  8.8 7.0 %copy-start.15 = (f32[2048]{0:T(1024)S(1)}, f32[2048]{0:T(1024)}, u32[]{:S(2)}) copy-start(f32[2048]{0:T(1024)} %param.10) | copy-start | bytes 24580
  9.9 19.7 %collective-permute-start = (bf16[192,2048]{1,0:T(8,128)(2,1)}, bf16[192,2048]{1,0:T(8,128)(2,1)}, u32[]{:S(2)}, u32[]{:S(2)}) collective-permute-start(bf16[192,2048]{1,0:T(8,128)(2,1)} %get-tuple-element.108.refs_2_), channel_id=1, source_target_pairs={{0,1},{3,2},{2,3},{1,0},{4,5},{7,6},{6,7},{5,4},{8,9},{11,10},{10,... | collective-permute-start | bytes 2359304 | tf_op jit(solution)/shard_map/ppermute | solution.py:113
  10.0 22.6 %collective-permute-start.1 = (bf16[192,2048]{1,0:T(8,128)(2,1)}, bf16[192,2048]{1,0:T(8,128)(2,1)}, u32[]{:S(2)}, u32[]{:S(2)}) collective-permute-start(bf16[192,2048]{1,0:T(8,128)(2,1)} %get-tuple-element.108.refs_2_), channel_id=1, source_target_pairs={{1,2},{2,1},{5,6},{6,5},{9,10},{10,9},{13,14},{14,13},{17,18},{18,... | collective-permute-start | bytes 2359304 | tf_op jit(solution)/shard_map/ppermute | solution.py:113
  15.9 9.4 %copy-start.12 = (s32[2048]{0:T(1024)S(1)}, s32[2048]{0:T(1024)}, u32[]{:S(2)}) copy-start(s32[2048]{0:T(1024)} %param.14) | copy-start | bytes 24580
  25.3 12.5 %collective-permute-start.4 = (f32[272,1024]{1,0:T(8,128)}, f32[272,1024]{1,0:T(8,128)}, u32[]{:S(2)}, u32[]{:S(2)}) collective-permute-start(f32[272,1024]{1,0:T(8,128)} %get-tuple-element.114), channel_id=1, source_target_pairs={{0,4},{4,0},{1,5},{5,1},{2,6},{6,2},{3,7},{7,3},{8,12},{12,8},{9,1... | collective-permute-start | bytes 3342344 | tf_op jit(solution)/shard_map/ppermute | solution.py:113
  26.4 11.4 %copy-start.7 = (f32[272,1024]{1,0:T(8,128)S(1)}, f32[272,1024]{1,0:T(8,128)}, u32[]{:S(2)}) copy-start(f32[272,1024]{1,0:T(8,128)} %copy-done.6) | copy-start | bytes 3342340
  32.8 33.4 %collective-permute-start.2 = (bf16[192,2048]{1,0:T(8,128)(2,1)}, bf16[192,2048]{1,0:T(8,128)(2,1)S(1)}, u32[]{:S(2)}, u32[]{:S(2)}) collective-permute-start(bf16[192,2048]{1,0:T(8,128)(2,1)} %get-tuple-element.111.refs_3_), channel_id=1, source_target_pairs={{1,2},{2,1},{5,6},{6,5},{9,10},{10,9},{13,14},{14,13},{17,18},{18,... | collective-permute-start | bytes 2359304 | tf_op jit(solution)/shard_map/ppermute | solution.py:113
  36.4 29.8 %collective-permute-start.3 = (bf16[192,2048]{1,0:T(8,128)(2,1)}, bf16[192,2048]{1,0:T(8,128)(2,1)S(1)}, u32[]{:S(2)}, u32[]{:S(2)}) collective-permute-start(bf16[192,2048]{1,0:T(8,128)(2,1)} %get-tuple-element.112.refs_4_), channel_id=1, source_target_pairs={{2,3},{1,0},{6,7},{5,4},{10,11},{9,8},{14,15},{13,12},{18,19},{17,... | collective-permute-start | bytes 2359304 | tf_op jit(solution)/shard_map/ppermute | solution.py:113
  39.3 23.3 %collective-permute-start.5 = (bf16[272,256]{1,0:T(8,128)(2,1)S(1)}, bf16[272,256]{1,0:T(8,128)(2,1)S(1)}, u32[]{:S(2)}, u32[]{:S(2)}) collective-permute-start(bf16[272,256]{1,0:T(8,128)(2,1)S(1)} %get-tuple-element.117), channel_id=1, source_target_pairs={{0,1},{1,2},{2,3},{3,0},{4,5},{5,6},{6,7},{7,4},{8,9},{9,10},{10,1... | collective-permute-start | bytes 417800 | tf_op jit(solution)/shard_map/ppermute | solution.py:113
  39.7 24.5 %collective-permute-start.6 = (bf16[272,256]{1,0:T(8,128)(2,1)S(1)}, bf16[272,256]{1,0:T(8,128)(2,1)S(1)}, u32[]{:S(2)}, u32[]{:S(2)}) collective-permute-start(bf16[272,256]{1,0:T(8,128)(2,1)S(1)} %get-tuple-element.118), channel_id=1, source_target_pairs={{0,2},{1,3},{2,0},{3,1},{4,6},{5,7},{6,4},{7,5},{8,10},{9,11},{10,... | collective-permute-start | bytes 417800 | tf_op jit(solution)/shard_map/ppermute | solution.py:113
  39.7 25.0 %collective-permute-start.7 = (bf16[272,256]{1,0:T(8,128)(2,1)S(1)}, bf16[272,256]{1,0:T(8,128)(2,1)S(1)}, u32[]{:S(2)}, u32[]{:S(2)}) collective-permute-start(bf16[272,256]{1,0:T(8,128)(2,1)S(1)} %get-tuple-element.119), channel_id=1, source_target_pairs={{0,3},{1,0},{2,1},{3,2},{4,7},{5,4},{6,5},{7,6},{8,11},{9,8},{10,9... | collective-permute-start | bytes 417800 | tf_op jit(solution)/shard_map/ppermute | solution.py:113
  66.2 18.4 %collective-permute-start.8 = (bf16[192,2048]{1,0:T(8,128)(2,1)S(1)}, bf16[192,2048]{1,0:T(8,128)(2,1)S(1)}, u32[]{:S(2)}, u32[]{:S(2)}) collective-permute-start(bf16[192,2048]{1,0:T(8,128)(2,1)S(1)} %get-tuple-element.124.refs_3_), channel_id=1, source_target_pairs={{2,3},{1,0},{6,7},{5,4},{10,11},{9,8},{14,15},{13,12},{18,19},{17,... | collective-permute-start | bytes 2359304 | tf_op jit(solution)/shard_map/ppermute | solution.py:113
  84.6 20.8 %collective-permute-start.10 = (bf16[192,2048]{1,0:T(8,128)(2,1)S(1)}, bf16[192,2048]{1,0:T(8,128)(2,1)S(1)}, u32[]{:S(2)}, u32[]{:S(2)}) collective-permute-start(bf16[192,2048]{1,0:T(8,128)(2,1)S(1)} %get-tuple-element.129.refs_2_), channel_id=1, source_target_pairs={{1,2},{2,1},{5,6},{6,5},{9,10},{10,9},{13,14},{14,13},{17,18},{18,... | collective-permute-start | bytes 2359304 | tf_op jit(solution)/shard_map/ppermute | solution.py:113
  87.8 17.7 %collective-permute-start.9 = (bf16[192,2048]{1,0:T(8,128)(2,1)S(1)}, bf16[192,2048]{1,0:T(8,128)(2,1)}, u32[]{:S(2)}, u32[]{:S(2)}) collective-permute-start(bf16[192,2048]{1,0:T(8,128)(2,1)S(1)} %get-tuple-element.129.refs_2_), channel_id=1, source_target_pairs={{0,1},{3,2},{2,3},{1,0},{4,5},{7,6},{6,7},{5,4},{8,9},{11,10},{10,... | collective-permute-start | bytes 2359304 | tf_op jit(solution)/shard_map/ppermute | solution.py:113
  94.1 1.7 collective-permute-start.11
  105.4 25.0 %collective-permute-start.12 = (bf16[192,2048]{1,0:T(8,128)(2,1)}, bf16[192,2048]{1,0:T(8,128)(2,1)S(1)}, u32[]{:S(2)}, u32[]{:S(2)}) collective-permute-start(bf16[192,2048]{1,0:T(8,128)(2,1)} %get-tuple-element.142.refs_3_), channel_id=1, source_target_pairs={{1,2},{2,1},{5,6},{6,5},{9,10},{10,9},{13,14},{14,13},{17,18},{18,... | collective-permute-start | bytes 2359304 | tf_op jit(solution)/shard_map/ppermute | solution.py:113
  109.1 21.4 %collective-permute-start.13 = (bf16[192,2048]{1,0:T(8,128)(2,1)S(1)}, bf16[192,2048]{1,0:T(8,128)(2,1)S(1)}, u32[]{:S(2)}, u32[]{:S(2)}) collective-permute-start(bf16[192,2048]{1,0:T(8,128)(2,1)S(1)} %get-tuple-element.143.refs_4_), channel_id=1, source_target_pairs={{2,3},{1,0},{6,7},{5,4},{10,11},{9,8},{14,15},{13,12},{18,19},{17,... | collective-permute-start | bytes 2359304 | tf_op jit(solution)/shard_map/ppermute | solution.py:113
  110.4 1.8 collective-permute-start.14
  120.6 22.3 %collective-permute-start.16 = (bf16[192,2048]{1,0:T(8,128)(2,1)S(1)}, bf16[192,2048]{1,0:T(8,128)(2,1)S(1)}, u32[]{:S(2)}, u32[]{:S(2)}) collective-permute-start(bf16[192,2048]{1,0:T(8,128)(2,1)S(1)} %get-tuple-element.152.refs_1_), channel_id=1, source_target_pairs={{0,1},{3,2},{4,5},{7,6},{8,9},{11,10},{12,13},{15,14},{16,17},{19,... | collective-permute-start | bytes 2359304 | tf_op jit(solution)/shard_map/ppermute | solution.py:113
  130.5 26.6 %collective-permute-start.15 = (bf16[192,2048]{1,0:T(8,128)(2,1)S(1)}, bf16[192,2048]{1,0:T(8,128)(2,1)S(1)}, u32[]{:S(2)}, u32[]{:S(2)}) collective-permute-start(bf16[192,2048]{1,0:T(8,128)(2,1)S(1)} %get-tuple-element.148.refs_3_), channel_id=1, source_target_pairs={{2,3},{1,0},{6,7},{5,4},{10,11},{9,8},{14,15},{13,12},{18,19},{17,... | collective-permute-start | bytes 2359304 | tf_op jit(solution)/shard_map/ppermute | solution.py:113
  135.2 31.3 %collective-permute-start.21 = (bf16[192,2048]{1,0:T(8,128)(2,1)S(1)}, bf16[192,2048]{1,0:T(8,128)(2,1)S(1)}, u32[]{:S(2)}, u32[]{:S(2)}) collective-permute-start(bf16[192,2048]{1,0:T(8,128)(2,1)S(1)} %get-tuple-element.151.refs_0_), channel_id=1, source_target_pairs={{0,1},{3,2},{4,5},{7,6},{8,9},{11,10},{12,13},{15,14},{16,17},{19,... | collective-permute-start | bytes 2359304 | tf_op jit(solution)/shard_map/ppermute | solution.py:113
  143.1 23.4 %collective-permute-start.20 = (bf16[192,2048]{1,0:T(8,128)(2,1)S(1)}, bf16[192,2048]{1,0:T(8,128)(2,1)S(1)}, u32[]{:S(2)}, u32[]{:S(2)}) collective-permute-start(bf16[192,2048]{1,0:T(8,128)(2,1)S(1)} %get-tuple-element.163), channel_id=1, source_target_pairs={{1,2},{2,1},{5,6},{6,5},{9,10},{10,9},{13,14},{14,13},{17,18},{18,... | collective-permute-start | bytes 2359304 | tf_op jit(solution)/shard_map/ppermute | solution.py:113
  145.5 11.7 %copy-start.5 = (bf16[128,2048]{1,0:T(8,128)(2,1)S(1)}, bf16[128,2048]{1,0:T(8,128)(2,1)}, u32[]{:S(2)}) copy-start(bf16[128,2048]{1,0:T(8,128)(2,1)} %copy-done.4) | copy-start | bytes 1572868
  162.7 4.7 %copy-start.1 = (bf16[2048,256]{1,0:T(8,128)(2,1)S(1)}, bf16[2048,256]{1,0:T(8,128)(2,1)}, u32[]{:S(2)}) copy-start(bf16[2048,256]{1,0:T(8,128)(2,1)} %all-gather.2.cloned.1.call-done.refs_4_) | copy-start | bytes 3145732
  162.7 4.7 %collective-permute-start.19 = (f32[192,1024]{1,0:T(8,128)S(1)}, f32[192,1024]{1,0:T(8,128)S(1)}, u32[]{:S(2)}, u32[]{:S(2)}) collective-permute-start(f32[192,1024]{1,0:T(8,128)S(1)} %get-tuple-element.161), channel_id=1, source_target_pairs={{0,4},{4,0},{1,5},{5,1},{2,6},{6,2},{3,7},{7,3},{8,12},{12,8},{9,1... | collective-permute-start | bytes 2359304 | tf_op jit(solution)/shard_map/ppermute | solution.py:113
  162.8 14.8 %collective-permute-start.17 = (bf16[128,2048]{1,0:T(8,128)(2,1)S(1)}, bf16[128,2048]{1,0:T(8,128)(2,1)S(1)}, u32[]{:S(2)}, u32[]{:S(2)}) collective-permute-start(bf16[128,2048]{1,0:T(8,128)(2,1)S(1)} %get-tuple-element.156.refs_2_), channel_id=1, source_target_pairs={{0,1},{3,2},{2,3},{1,0},{4,5},{7,6},{6,7},{5,4},{8,9},{11,10},{10,... | collective-permute-start | bytes 1572872 | tf_op jit(solution)/shard_map/ppermute | solution.py:113
  162.8 16.8 %collective-permute-start.18 = (bf16[128,2048]{1,0:T(8,128)(2,1)S(1)}, bf16[128,2048]{1,0:T(8,128)(2,1)S(1)}, u32[]{:S(2)}, u32[]{:S(2)}) collective-permute-start(bf16[128,2048]{1,0:T(8,128)(2,1)S(1)} %get-tuple-element.156.refs_2_), channel_id=1, source_target_pairs={{1,2},{2,1},{5,6},{6,5},{9,10},{10,9},{13,14},{14,13},{17,18},{18,... | collective-permute-start | bytes 1572872 | tf_op jit(solution)/shard_map/ppermute | solution.py:113
  172.9 6.7 %collective-permute-start.26 = (bf16[192,1024]{1,0:T(8,128)(2,1)S(1)}, bf16[192,1024]{1,0:T(8,128)(2,1)S(1)}, u32[]{:S(2)}, u32[]{:S(2)}) collective-permute-start(bf16[192,1024]{1,0:T(8,128)(2,1)S(1)} %get-tuple-element.172.refs_1_), channel_id=1, source_target_pairs={{0,4},{4,0},{1,5},{5,1},{2,6},{6,2},{3,7},{7,3},{8,12},{12,8},{9,1... | collective-permute-start | bytes 1179656 | tf_op jit(solution)/shard_map/ppermute | solution.py:113
  173.0 30.2 %collective-permute-start.24 = (bf16[192,2048]{1,0:T(8,128)(2,1)S(1)}, bf16[192,2048]{1,0:T(8,128)(2,1)S(1)}, u32[]{:S(2)}, u32[]{:S(2)}) collective-permute-start(bf16[192,2048]{1,0:T(8,128)(2,1)S(1)} %get-tuple-element.170), channel_id=1, source_target_pairs={{0,1},{3,2},{2,3},{1,0},{4,5},{7,6},{6,7},{5,4},{8,9},{11,10},{10,... | collective-permute-start | bytes 2359304 | tf_op jit(solution)/shard_map/ppermute | solution.py:113
  173.1 30.1 %collective-permute-start.25 = (bf16[192,2048]{1,0:T(8,128)(2,1)S(1)}, bf16[192,2048]{1,0:T(8,128)(2,1)S(1)}, u32[]{:S(2)}, u32[]{:S(2)}) collective-permute-start(bf16[192,2048]{1,0:T(8,128)(2,1)S(1)} %get-tuple-element.171), channel_id=1, source_target_pairs={{1,2},{2,1},{5,6},{6,5},{9,10},{10,9},{13,14},{14,13},{17,18},{18,... | collective-permute-start | bytes 2359304 | tf_op jit(solution)/shard_map/ppermute | solution.py:113
  188.0 22.8 %collective-permute-start.27 = (bf16[192,2048]{1,0:T(8,128)(2,1)S(1)}, bf16[192,2048]{1,0:T(8,128)(2,1)S(1)}, u32[]{:S(2)}, u32[]{:S(2)}) collective-permute-start(bf16[192,2048]{1,0:T(8,128)(2,1)S(1)} %get-tuple-element.179.refs_1_), channel_id=1, source_target_pairs={{0,1},{3,2},{4,5},{7,6},{8,9},{11,10},{12,13},{15,14},{16,17},{19,... | collective-permute-start | bytes 2359304 | tf_op jit(solution)/shard_map/ppermute | solution.py:113
  189.3 17.7 %collective-permute-start.22 = (bf16[128,2048]{1,0:T(8,128)(2,1)S(1)}, bf16[128,2048]{1,0:T(8,128)(2,1)S(1)}, u32[]{:S(2)}, u32[]{:S(2)}) collective-permute-start(bf16[128,2048]{1,0:T(8,128)(2,1)S(1)} %get-tuple-element.167.refs_3_), channel_id=1, source_target_pairs={{1,2},{2,1},{5,6},{6,5},{9,10},{10,9},{13,14},{14,13},{17,18},{18,... | collective-permute-start | bytes 1572872 | tf_op jit(solution)/shard_map/ppermute | solution.py:113
  192.8 14.2 %collective-permute-start.23 = (bf16[128,2048]{1,0:T(8,128)(2,1)S(1)}, bf16[128,2048]{1,0:T(8,128)(2,1)S(1)}, u32[]{:S(2)}, u32[]{:S(2)}) collective-permute-start(bf16[128,2048]{1,0:T(8,128)(2,1)S(1)} %get-tuple-element.168.refs_4_), channel_id=1, source_target_pairs={{2,3},{1,0},{6,7},{5,4},{10,11},{9,8},{14,15},{13,12},{18,19},{17,... | collective-permute-start | bytes 1572872 | tf_op jit(solution)/shard_map/ppermute | solution.py:113
  207.1 17.5 %collective-permute-start.28 = (bf16[128,2048]{1,0:T(8,128)(2,1)S(1)}, bf16[128,2048]{1,0:T(8,128)(2,1)S(1)}, u32[]{:S(2)}, u32[]{:S(2)}) collective-permute-start(bf16[128,2048]{1,0:T(8,128)(2,1)S(1)} %get-tuple-element.183.refs_3_), channel_id=1, source_target_pairs={{2,3},{1,0},{6,7},{5,4},{10,11},{9,8},{14,15},{13,12},{18,19},{17,... | collective-permute-start | bytes 1572872 | tf_op jit(solution)/shard_map/ppermute | solution.py:113
  208.9 20.6 %collective-permute-start.31 = (bf16[192,2048]{1,0:T(8,128)(2,1)S(1)}, bf16[192,2048]{1,0:T(8,128)(2,1)S(1)}, u32[]{:S(2)}, u32[]{:S(2)}) collective-permute-start(bf16[192,2048]{1,0:T(8,128)(2,1)S(1)} %get-tuple-element.178.refs_0_), channel_id=1, source_target_pairs={{0,1},{3,2},{4,5},{7,6},{8,9},{11,10},{12,13},{15,14},{16,17},{19,... | collective-permute-start | bytes 2359304 | tf_op jit(solution)/shard_map/ppermute | solution.py:113
  211.0 21.0 %collective-permute-start.30 = (bf16[192,2048]{1,0:T(8,128)(2,1)S(1)}, bf16[192,2048]{1,0:T(8,128)(2,1)S(1)}, u32[]{:S(2)}, u32[]{:S(2)}) collective-permute-start(bf16[192,2048]{1,0:T(8,128)(2,1)S(1)} %get-tuple-element.188), channel_id=1, source_target_pairs={{1,2},{2,1},{5,6},{6,5},{9,10},{10,9},{13,14},{14,13},{17,18},{18,... | collective-permute-start | bytes 2359304 | tf_op jit(solution)/shard_map/ppermute | solution.py:113
  229.4 7.1 %collective-permute-start.29 = (f32[128,1024]{1,0:T(8,128)S(1)}, f32[128,1024]{1,0:T(8,128)S(1)}, u32[]{:S(2)}, u32[]{:S(2)}) collective-permute-start(f32[128,1024]{1,0:T(8,128)S(1)} %get-tuple-element.186), channel_id=1, source_target_pairs={{0,4},{4,0},{1,5},{5,1},{2,6},{6,2},{3,7},{7,3},{8,12},{12,8},{9,1... | collective-permute-start | bytes 1572872 | tf_op jit(solution)/shard_map/ppermute | solution.py:113
  232.9 26.9 %collective-permute-start.35 = (bf16[192,2048]{1,0:T(8,128)(2,1)S(1)}, bf16[192,2048]{1,0:T(8,128)(2,1)S(1)}, u32[]{:S(2)}, u32[]{:S(2)}) collective-permute-start(bf16[192,2048]{1,0:T(8,128)(2,1)S(1)} %get-tuple-element.199), channel_id=1, source_target_pairs={{0,1},{3,2},{2,3},{1,0},{4,5},{7,6},{6,7},{5,4},{8,9},{11,10},{10,... | collective-permute-start | bytes 2359304 | tf_op jit(solution)/shard_map/ppermute | solution.py:113
  233.0 26.8 %collective-permute-start.36 = (bf16[192,2048]{1,0:T(8,128)(2,1)S(1)}, bf16[192,2048]{1,0:T(8,128)(2,1)S(1)}, u32[]{:S(2)}, u32[]{:S(2)}) collective-permute-start(bf16[192,2048]{1,0:T(8,128)(2,1)S(1)} %get-tuple-element.200), channel_id=1, source_target_pairs={{1,2},{2,1},{5,6},{6,5},{9,10},{10,9},{13,14},{14,13},{17,18},{18,... | collective-permute-start | bytes 2359304 | tf_op jit(solution)/shard_map/ppermute | solution.py:113
  240.7 1.6 collective-permute-start.32
  247.1 15.9 %collective-permute-start.34 = (bf16[128,2048]{1,0:T(8,128)(2,1)S(1)}, bf16[128,2048]{1,0:T(8,128)(2,1)S(1)}, u32[]{:S(2)}, u32[]{:S(2)}) collective-permute-start(bf16[128,2048]{1,0:T(8,128)(2,1)S(1)} %get-tuple-element.196.refs_1_), channel_id=1, source_target_pairs={{0,1},{3,2},{4,5},{7,6},{8,9},{11,10},{12,13},{15,14},{16,17},{19,... | collective-permute-start | bytes 1572872 | tf_op jit(solution)/shard_map/ppermute | solution.py:113
  258.5 16.7 %collective-permute-start.38 = (bf16[128,2048]{1,0:T(8,128)(2,1)S(1)}, bf16[128,2048]{1,0:T(8,128)(2,1)S(1)}, u32[]{:S(2)}, u32[]{:S(2)}) collective-permute-start(bf16[128,2048]{1,0:T(8,128)(2,1)S(1)} %get-tuple-element.197.refs_0_), channel_id=1, source_target_pairs={{0,1},{3,2},{4,5},{7,6},{8,9},{11,10},{12,13},{15,14},{16,17},{19,... | collective-permute-start | bytes 1572872 | tf_op jit(solution)/shard_map/ppermute | solution.py:113
  263.1 15.0 %collective-permute-start.37 = (bf16[128,2048]{1,0:T(8,128)(2,1)S(1)}, bf16[128,2048]{1,0:T(8,128)(2,1)S(1)}, u32[]{:S(2)}, u32[]{:S(2)}) collective-permute-start(bf16[128,2048]{1,0:T(8,128)(2,1)S(1)} %get-tuple-element.204), channel_id=1, source_target_pairs={{1,2},{2,1},{5,6},{6,5},{9,10},{10,9},{13,14},{14,13},{17,18},{18,... | collective-permute-start | bytes 1572872 | tf_op jit(solution)/shard_map/ppermute | solution.py:113
  266.4 19.2 %collective-permute-start.33 = (bf16[128,2048]{1,0:T(8,128)(2,1)S(1)}, bf16[128,2048]{1,0:T(8,128)(2,1)S(1)}, u32[]{:S(2)}, u32[]{:S(2)}) collective-permute-start(bf16[128,2048]{1,0:T(8,128)(2,1)S(1)} %get-tuple-element.195.refs_2_), channel_id=1, source_target_pairs={{0,1},{3,2},{4,5},{7,6},{8,9},{11,10},{12,13},{15,14},{16,17},{19,... | collective-permute-start | bytes 1572872 | tf_op jit(solution)/shard_map/ppermute | solution.py:113
  278.9 11.3 %collective-permute-start.39 = (bf16[128,2048]{1,0:T(8,128)(2,1)S(1)}, bf16[128,2048]{1,0:T(8,128)(2,1)S(1)}, u32[]{:S(2)}, u32[]{:S(2)}) collective-permute-start(bf16[128,2048]{1,0:T(8,128)(2,1)S(1)} %get-tuple-element.206), channel_id=1, source_target_pairs={{2,3},{1,0},{6,7},{5,4},{10,11},{9,8},{14,15},{13,12},{18,19},{17,... | collective-permute-start | bytes 1572872 | tf_op jit(solution)/shard_map/ppermute | solution.py:113
  280.3 14.1 %collective-permute-start.40 = (bf16[128,2048]{1,0:T(8,128)(2,1)S(1)}, bf16[128,2048]{1,0:T(8,128)(2,1)S(1)}, u32[]{:S(2)}, u32[]{:S(2)}) collective-permute-start(bf16[128,2048]{1,0:T(8,128)(2,1)S(1)} %get-tuple-element.207), channel_id=1, source_target_pairs={{1,2},{2,1},{5,6},{6,5},{9,10},{10,9},{13,14},{14,13},{17,18},{18,... | collective-permute-start | bytes 1572872 | tf_op jit(solution)/shard_map/ppermute | solution.py:113
  (11 other events, 11.1 us)
Sparse Core Ops, SparseCore 0:
  66.3 24.9 all-gather.1
